TPU v7x, 32 devices: a whole 2x2x4 slice. The times are simulated.
32 devices in a mesh: rows: 8 (over y, x, core), cols: 4 (over z).
Axes of the slice: x: 2, y: 2, z: 4, core: 2. Of those that a mesh axis runs over, the one named last changes fastest.
Arguments:
- points: float32 [4096, 256], P('rows'), may hold values from -4 to 4, as said below
- centers: float32 [16384, 256], P('cols'), may hold values from -4 to 4, as said below
- inv_factor: float32 [16384, 16384], P('cols', 'rows'), may hold values from -2 to 2, as said below
- solution: float32 [16384, 128], P('rows'), may hold values from -6 to 6
- residual: float32 [16384, 128], P('rows'), may hold values from -40 to 40
- direction: float32 [16384, 128], P('rows'), may hold values from -40 to 40
Outputs:
- new_solution: float32 [16384, 128], P('rows')
- new_residual: float32 [16384, 128], P('rows')
- new_direction: float32 [16384, 128], P('rows')
Inputs may be any that keep to these rules, and one draw needn't show every extreme that they name: `points`: each point's coordinates have a fixed spread that differs from coordinate to coordinate. `centers`: drawn by the same law as points. `inv_factor`: upper triangular with a positive diagonal.
All inputs are finite; a program needn't handle non-finite values.
Results may differ from a plain program's by a relative error of at most 0.00027.
Values sent between devices are 32-bit elements; how exact they have to be, the bound alone decides.
No kernel may reach another device: no remote copies, remote signals or barrier semaphores. Data moves between devices by JAX's collectives and lax.ppermute only.
A program may use at most 128 MiB of HBM per device.

v0:
```python
import jax
import jax.numpy as jnp
from jax import lax
from jax.sharding import PartitionSpec as P

ridge_weight = 0.02


def body(points, centers, inv_factor, solution, residual, direction):
    highest = lax.Precision.HIGHEST
    mapped_part = jnp.dot(
        inv_factor, direction, precision=highest, preferred_element_type=jnp.float32
    )
    norm_part = jnp.sum(residual * residual, axis=0)
    square_part = jnp.sum(direction * direction, axis=0)
    mapped, norm_now, dir_norm = lax.psum((mapped_part, norm_part, square_part), "rows")
    point_sq = jnp.sum(points * points, axis=1)
    center_sq = jnp.sum(centers * centers, axis=1)
    inner_products = lax.dot_general(
        points,
        centers,
        (((1,), (1,)), ((), ())),
        precision=highest,
        preferred_element_type=jnp.float32,
    )
    kernel = jnp.exp(-0.5 * (point_sq[:, None] + center_sq[None, :] - 2.0 * inner_products))
    predicted_part = jnp.dot(kernel, mapped, precision=highest, preferred_element_type=jnp.float32)
    predicted = lax.psum(predicted_part, "cols")
    back_part = lax.dot_general(
        kernel,
        predicted,
        (((0,), (0,)), ((), ())),
        precision=highest,
        preferred_element_type=jnp.float32,
    )
    pred_norm = jnp.sum(predicted * predicted, axis=0)
    back, pred_total = lax.psum((back_part, pred_norm), "rows")
    image_part = lax.dot_general(
        inv_factor,
        back,
        (((0,), (0,)), ((), ())),
        precision=highest,
        preferred_element_type=jnp.float32,
    )
    image = lax.psum(image_part, "cols") + ridge_weight * direction
    curvature = pred_total + ridge_weight * dir_norm
    step_size = norm_now / curvature
    new_solution = solution + step_size[None, :] * direction
    new_residual = residual - step_size[None, :] * image
    norm_next = lax.psum(jnp.sum(new_residual * new_residual, axis=0), "rows")
    new_direction = new_residual + (norm_next / norm_now)[None, :] * direction
    return (new_solution, new_residual, new_direction)


def solution(mesh):
    return jax.shard_map(
        body,
        mesh=mesh,
        in_specs=(
            P("rows", None),
            P("cols", None),
            P("cols", "rows"),
            P("rows", None),
            P("rows", None),
            P("rows", None),
        ),
        out_specs=(P("rows", None), P("rows", None), P("rows", None)),
        check_vma=False,
    )
```

profile of v0, /device:TPU:0, one launch (start us, length us, event | category | flops | bytes accessed | tf_op | source)
XLA Modules:
  0.0 330.7 jit_solution(12084955347193782173)
XLA Ops:
  7.2 31.1 %fusion = f32[4096,128]{1,0:T(8,128)} fusion(f32[4096,2048]{1,0:T(8,128)} %param.8, f32[2048,128]{1,0:T(8,128)} %param.11), kind=kOutput, calls=%fused_computation.12 | convolution fusion | flops 12884901888 | bytes 36700160 | tf_op jit(solution)/shard_map/dot_general | solution.py:11
  38.3 0.2 all-reduce.8.cloned.1.call-start
  38.7 2.8 multiply_reduce_fusion
  41.5 12.0 %multiply_exponential_fusion = f32[512,4096]{1,0:T(8,128)} fusion(f32[512,256]{1,0:T(8,128)S(1)} %copy-done.2, f32[4096,256]{1,0:T(8,128)} %param.7, f32[4096]{0:T(1024)S(1)} %multiply_reduce_fusion, f32[512]{0:T(512)S(1)} %multiply_reduce_fusion.4), kind=kOutput, calls=%fused_computation | convolution fusion | flops 6450839552 | bytes 13125632 | tf_op jit(solution)/shard_map/dot_general | solution.py:19
  53.6 49.1 %all-reduce.6.cloned.1.call-done = f32[4096,128]{1,0:T(8,128)} async-done(((f32[4096,128]{1,0:T(8,128)}), f32[4096,128]{1,0:T(8,128)}) %all-reduce.6.cloned.1.call-update) | async-done | bytes 2097168 | tf_op jit(solution)/shard_map/psum | solution.py:16
  102.6 10.0 %fusion.1 = f32[512,128]{1,0:T(8,128)} fusion(f32[512,4096]{1,0:T(8,128)} %multiply_exponential_fusion, f32[4096,128]{1,0:T(8,128)} %all-reduce.6.cloned.1.call-done), kind=kOutput, calls=%fused_computation.13 | convolution fusion | flops 3221225472 | bytes 10747904 | tf_op jit(solution)/shard_map/dot_general | solution.py:27
  112.7 0.3 all-reduce.10.cloned.1.call-start
  113.0 34.4 %all-reduce.8.cloned.1.call-done = f32[512,128]{1,0:T(8,128)} async-done(((f32[512,128]{1,0:T(8,128)}), f32[512,128]{1,0:T(8,128)}) %all-reduce.8.cloned.1.call-update) | async-done | bytes 262160 | tf_op jit(solution)/shard_map/psum | solution.py:28
  147.3 16.6 %fusion.2 = f32[4096,128]{1,0:T(8,128)} fusion(f32[512,4096]{1,0:T(8,128)} %multiply_exponential_fusion, f32[512,128]{1,0:T(8,128)} %all-reduce.8.cloned.1.call-done), kind=kOutput, calls=%fused_computation.14 | convolution fusion | flops 3221225472 | bytes 10747904 | tf_op jit(solution)/shard_map/dot_general | solution.py:29
  164.0 0.3 all-reduce.12.cloned.1.call-start
  164.3 61.0 %all-reduce.10.cloned.1.call-done = f32[4096,128]{1,0:T(8,128)} async-done(((f32[4096,128]{1,0:T(8,128)}), f32[4096,128]{1,0:T(8,128)}) %all-reduce.10.cloned.1.call-update) | async-done | bytes 2097168 | tf_op jit(solution)/shard_map/psum | solution.py:37
  225.3 25.4 %convolution_bitcast_fusion = f32[2048,128]{0,1:T(8,128)} fusion(f32[4096,128]{1,0:T(8,128)} %all-reduce.10.cloned.1.call-done, f32[4096,2048]{1,0:T(8,128)} %param.8), kind=kOutput, calls=%fused_computation.2 | convolution fusion | flops 12884901888 | bytes 36700160 | tf_op jit(solution)/shard_map/dot_general | solution.py:38
  250.7 0.3 copy.9
  251.0 2.5 copy.10
  253.5 1.3 copy.12
  254.9 0.3 multiply_reduce_fusion.2
  255.1 0.3 multiply_reduce_fusion.3
  255.5 12.6 %all-reduce = (f32[128]{0:T(128)S(1)}, f32[128]{0:T(128)S(1)}, f32[128]{0:T(128)S(1)}) all-reduce(f32[128]{0:T(128)S(1)} %multiply_reduce_fusion.3, f32[128]{0:T(128)S(1)} %multiply_reduce_fusion.5, f32[128]{0:T(128)S(1)} %multiply_reduce_fusion.2), channel_id=1, replica_groups=mesh['rows'=8,'cols'=4] {'rows'}, use_global_device_ids=true, to_apply=%region_1.0 | all-reduce | flops 384 | bytes 3072 | tf_op jit(solution)/shard_map/psum | solution.py:16
  268.1 33.7 %all-reduce.12.cloned.1.call-done = f32[2048,128]{0,1:T(8,128)} async-done(((f32[2048,128]{0,1:T(8,128)}), f32[2048,128]{0,1:T(8,128)}) %all-reduce.12.cloned.1.call-update) | async-done | bytes 1048592 | tf_op jit(solution)/shard_map/psum | solution.py:45
  301.8 3.2 multiply_reduce_fusion.1
  305.1 13.8 %psum.63 = f32[128]{0:T(128)S(1)} all-reduce(f32[128]{0:T(128)S(1)} %get-tuple-element.9), channel_id=1, replica_groups=mesh['rows'=8,'cols'=4] {'rows'}, use_global_device_ids=true, to_apply=%region_13.0 | all-reduce | flops 128 | bytes 1024 | tf_op jit(solution)/shard_map/psum | solution.py:50
  318.9 1.3 copy.15
  320.3 1.3 copy.16
  321.7 2.5 copy.14
  (18 shorter events, 0.5 us)
Async XLA Ops:
  7.2 31.4 %copy-start.2 = (f32[512,256]{1,0:T(8,128)S(1)}, f32[512,256]{1,0:T(8,128)}, u32[]{:S(2)}) copy-start(f32[512,256]{1,0:T(8,128)} %param.6) | copy-start | bytes 1572868
  7.2 95.5 %all-reduce.6.cloned.1.call-start = ((), (), s32[]{:S(2)}) async-start(), calls=%async_computation | async-start | bytes 4194304 | tf_op jit(solution)/shard_map/psum | solution.py:16
  38.3 109.0 %all-reduce.8.cloned.1.call-start = ((), (), s32[]{:S(2)}) async-start(), calls=%async_computation.1 | async-start | bytes 524288 | tf_op jit(solution)/shard_map/psum | solution.py:28
  112.7 112.6 %all-reduce.10.cloned.1.call-start = ((), (), s32[]{:S(2)}) async-start(), calls=%async_computation.2 | async-start | bytes 4194304 | tf_op jit(solution)/shard_map/psum | solution.py:37
  163.9 86.7 %copy-start = (f32[2048,128]{1,0:T(8,128)S(1)}, f32[2048,128]{1,0:T(8,128)}, u32[]{:S(2)}) copy-start(f32[2048,128]{1,0:T(8,128)} %param.11) | copy-start | bytes 3145732
  164.0 89.6 %copy-start.1 = (f32[2048,128]{1,0:T(8,128)S(1)}, f32[2048,128]{1,0:T(8,128)}, u32[]{:S(2)}) copy-start(f32[2048,128]{1,0:T(8,128)} %param.10) | copy-start | bytes 3145732
  164.0 137.9 %all-reduce.12.cloned.1.call-start = ((), (), s32[]{:S(2)}) async-start(), calls=%async_computation.3 | async-start | bytes 2097152 | tf_op jit(solution)/shard_map/psum | solution.py:45
  250.6 4.8 %copy-start.3 = (f32[512,128]{1,0:T(8,128)S(1)}, f32[512,128]{1,0:T(8,128)}, u32[]{:S(2)}) copy-start(f32[512,128]{1,0:T(8,128)} %all-reduce.8.cloned.1.call-done) | copy-start | bytes 786436
Sparse Core Ops, SparseCore 0:
  38.5 64.1 all-reduce.5
  112.8 34.4 all-reduce.7
  164.1 61.1 all-reduce.9
  250.8 51.0 all-reduce.11
where the time goes:
time: 331 us
  waiting for transfers between devices  178 us (54%)
  matrix products  95.1 us (29%)
  blocking collectives  26.4 us (8%)
  between operations  13.8 us (4%)
  local copies, waits for them, and re-layouts  9.34 us (3%)
  other arithmetic  6.99 us (2%)
    psum x1, waiting for transfers between devices, body(): back, pred_total = lax.psum((back_part, pred_norm), 'rows')  61 us
    psum x1, waiting for transfers between devices, body(): lax.psum((mapped_part, norm_part, square_part), 'rows')  49.1 us
    psum x1, waiting for transfers between devices, body(): predicted = lax.psum(predicted_part, 'cols')  34.4 us
    psum x1, waiting for transfers between devices, body(): image = lax.psum(image_part, 'cols') + ridge_weight * direction  33.7 us
    dot_general x1, matrix products, body(): jnp.dot(inv_factor, direction, precision=highest, preferred_element_type=...  31.1 us
    dot_general x1, matrix products, body(): lax.dot_general(inv_factor, back, (((0,), (0,)), ((), ())), precision=hig...  25.4 us
    dot_general x1, matrix products, body(): lax.dot_general(kernel, predicted, (((0,), (0,)), ((), ())), precision=hi...  16.6 us
    psum x1, blocking collectives, body(): norm_next = lax.psum(jnp.sum(new_residual * new_residual, axis=0), 'rows')  13.8 us
  transfers between devices with their start and end apart: 4, of which 4 were waited for; matrix products, arithmetic and copies ran while one was open for 6% of the time, Pallas kernels for 0%

commit v1 on v0

v1 whole, which is shorter than its diff:
```python
import functools

import jax
import jax.numpy as jnp
from jax import lax
from jax.experimental import pallas as pl
from jax.experimental.pallas import tpu as pltpu
from jax.sharding import PartitionSpec as P

ridge_weight = 0.02
PAD = 8
f32, bf16 = jnp.float32, jnp.bfloat16
FIRST = (((0,), (0,)), ((), ()))
LAST = (((1,), (1,)), ((), ()))


def split(value):
    high = value.astype(bf16)
    return high, (value - high.astype(f32)).astype(bf16)


def pair(value):
    high, low = split(value)
    return jnp.concatenate([high, low], axis=1)


def wide(lhs, pairs, dims=None):
    high, low = split(lhs)
    n = pairs.shape[1] // 2
    both = jnp.dot(high, pairs, preferred_element_type=f32)
    both += jnp.dot(low, pairs, preferred_element_type=f32)
    return both[:, :n] + both[:, n:]


def turned(pairs, high, low):
    n = pairs.shape[1] // 2
    both = lax.dot_general(pairs, high, FIRST, preferred_element_type=f32)
    both += lax.dot_general(pairs, low, FIRST, preferred_element_type=f32)
    return both[:n] + both[n:]


def params(mib=56):
    return pltpu.CompilerParams(vmem_limit_bytes=mib << 20)


def cost(flops, nbytes, exps=0):
    return pl.CostEstimate(flops=flops, bytes_accessed=nbytes, transcendentals=exps)


def whole(shape):
    return pl.BlockSpec(shape, lambda *_: (0,) * len(shape))


def forward_kernel(place, l_ref, d_ref, r_ref, keep_ref, send_ref, pairs, norms):
    @pl.when(pl.program_id(0) == 0)
    def _():
        d, r = d_ref[...], r_ref[...]
        pairs[...] = pair(d)
        norms[...] = jnp.zeros_like(norms)
        norms[0:1, :] = jnp.sum(r * r, axis=0, keepdims=True)
        norms[1:2, :] = jnp.sum(d * d, axis=0, keepdims=True)

    m = l_ref.shape[0] // 2
    core = place[1]
    for out_ref, side in ((keep_ref, core), (send_ref, 1 - core)):
        rows = l_ref[pl.ds(pl.multiple_of(side * m, m), m), :]
        out_ref[0, :m, :] = wide(rows, pairs[...])
        out_ref[0, m:, :] = norms[...]


def forward(place, inv_factor, direction, residual, chips):
    n, depth = inv_factor.shape
    t = direction.shape[1]
    m = n // chips // 2
    out = jax.ShapeDtypeStruct((chips, m + PAD, t), f32)
    block = pl.BlockSpec((1, m + PAD, t), lambda i, s: (i, 0, 0))
    return pl.pallas_call(
        forward_kernel,
        grid_spec=pltpu.PrefetchScalarGridSpec(
            num_scalar_prefetch=1,
            grid=(chips,),
            in_specs=[
                pl.BlockSpec((2 * m, depth), lambda i, s: (s[0] ^ i, 0)),
                whole((depth, t)),
                whole((depth, t)),
            ],
            out_specs=(block, block),
            scratch_shapes=[pltpu.VMEM((depth, 2 * t), bf16), pltpu.VMEM((PAD, t), f32)],
        ),
        out_shape=(out, out),
        compiler_params=params(),
        cost_estimate=cost(8 * n * depth * t, 4 * n * depth),
    )(place, inv_factor, direction, residual)


def kernel_kernel(segments, place, own_ref, other_ref, c_ref, high_ref, low_ref, ph, plo, psq):
    @pl.when(pl.program_id(0) == 0)
    def _():
        n = own_ref.shape[0]
        seg = n // segments
        for side, ref in enumerate((own_ref, other_ref)):
            for u in range(segments):
                start = pl.multiple_of((place[2] ^ u) * seg, seg)
                p = ref[pl.ds(start, seg), :]
                at = slice(side * n + u * seg, side * n + (u + 1) * seg)
                ph[at, :], plo[at, :] = split(p)
                psq[at, :] = jnp.broadcast_to(0.5 * jnp.sum(p * p, axis=1, keepdims=True), (seg, 128))

    c = c_ref[...]
    ch, cl = split(c)
    x = lax.dot_general(ch, ph[...], LAST, preferred_element_type=f32)
    x += lax.dot_general(ch, plo[...], LAST, preferred_element_type=f32)
    x += lax.dot_general(cl, ph[...], LAST, preferred_element_type=f32)
    center_sq = 0.5 * jnp.sum(c * c, axis=1, keepdims=True)
    point_sq = psq[...].T[0:1, :]
    high_ref[0], low_ref[0] = split(jnp.exp(x - (center_sq + point_sq)))


def gaussian(place, own, other, centers, chips, segments):
    n, width = own.shape
    m = centers.shape[0] // chips // 2
    out = jax.ShapeDtypeStruct((chips, m, 2 * n), bf16)
    block = pl.BlockSpec((1, m, 2 * n), lambda i, s: (i, 0, 0))
    return pl.pallas_call(
        functools.partial(kernel_kernel, segments),
        grid_spec=pltpu.PrefetchScalarGridSpec(
            num_scalar_prefetch=1,
            grid=(chips,),
            in_specs=[
                whole((n, width)),
                whole((n, width)),
                pl.BlockSpec((m, width), lambda i, s: (2 * (s[0] ^ i) + s[1], 0)),
            ],
            out_specs=(block, block),
            scratch_shapes=[
                pltpu.VMEM((2 * n, width), bf16),
                pltpu.VMEM((2 * n, width), bf16),
                pltpu.VMEM((2 * n, 128), f32),
            ],
        ),
        out_shape=(out, out),
        compiler_params=params(),
        cost_estimate=cost(12 * chips * m * n * width, 8 * chips * m * n, 2 * chips * m * n),
    )(place, own, other, centers)


def predict_kernel(first, n_pieces, last, *refs):
    high_ref, low_ref = refs[:2]
    pieces = refs[2 : 2 + n_pieces]
    rest = refs[2 + n_pieces :]
    if first:
        acc = rest[0]
    else:
        start_ref, keep_ref, send_ref, acc = rest
    i = pl.program_id(0)
    m = high_ref.shape[1]
    for j, piece in enumerate(pieces):

        @pl.when(i == j)
        def _(j=j, piece=piece):
            value = turned(pair(piece[:m, :]), high_ref[0], low_ref[0])
            if first and j == 0:
                acc[...] = value
            elif j == 0:
                acc[...] = start_ref[...] + value
            else:
                acc[...] += value

    if last:

        @pl.when(i == n_pieces - 1)
        def _():
            half = keep_ref.shape[0]
            keep_ref[...] = acc[:, :half].T
            send_ref[...] = acc[:, half:].T


def predict(high, low, pieces, offset, start=None):
    _, m, n = high.shape
    t = pieces[0].shape[1]
    first = start is None
    k_block = pl.BlockSpec((1, m, n), lambda i: (i + offset, 0, 0))
    in_specs = [k_block, k_block] + [whole(p.shape) for p in pieces]
    args = [high, low, *pieces]
    if first:
        out_shape, out_specs = jax.ShapeDtypeStruct((t, n), f32), whole((t, n))
        scratch = []
    else:
        in_specs.append(whole((t, n)))
        args.append(start)
        out_shape = (jax.ShapeDtypeStruct((n // 2, t), f32),) * 2
        out_specs = (whole((n // 2, t)),) * 2
        scratch = [pltpu.VMEM((t, n), f32)]
    return pl.pallas_call(
        functools.partial(predict_kernel, first, len(pieces), not first),
        grid=(len(pieces),),
        in_specs=in_specs,
        out_specs=out_specs,
        out_shape=out_shape,
        scratch_shapes=scratch,
        compiler_params=params(),
        cost_estimate=cost(8 * len(pieces) * m * n * t, 4 * len(pieces) * m * n),
    )(*args)


def back_kernel(high_ref, low_ref, own_ref, other_ref, out_ref, pairs, norms):
    half = own_ref.shape[0]

    @pl.when(pl.program_id(0) == 0)
    def _():
        norms[...] = jnp.zeros_like(norms)
        a, b = own_ref[...], other_ref[...]
        pairs[:half, :] = pair(a)
        pairs[half:, :] = pair(b)
        norms[0:1, :] = jnp.sum(a * a, axis=0, keepdims=True) + jnp.sum(b * b, axis=0, keepdims=True)

    m = high_ref.shape[1]
    n = out_ref.shape[2]
    both = jnp.dot(high_ref[0], pairs[...], preferred_element_type=f32)
    both += jnp.dot(low_ref[0], pairs[...], preferred_element_type=f32)
    out_ref[0, :m, :] = both[:, :n] + both[:, n:]
    out_ref[0, m:, :] = norms[...]


def back_product(high, low, own, other):
    chips, m, n = high.shape
    t = own.shape[1]
    k_block = pl.BlockSpec((1, m, n), lambda i: (i, 0, 0))
    return pl.pallas_call(
        back_kernel,
        grid=(chips,),
        in_specs=[k_block, k_block, whole(own.shape), whole(other.shape)],
        out_specs=pl.BlockSpec((1, m + PAD, t), lambda i: (i, 0, 0)),
        out_shape=jax.ShapeDtypeStruct((chips, m + PAD, t), f32),
        scratch_shapes=[pltpu.VMEM((n, 2 * t), bf16), pltpu.VMEM((PAD, t), f32)],
        compiler_params=params(),
        cost_estimate=cost(8 * chips * m * n * t, 4 * chips * m * n),
    )(high, low, own, other)


def transposed_kernel(first, n_pieces, segments, place, l_ref, *refs):
    own, other = refs[:n_pieces], refs[n_pieces : 2 * n_pieces]
    rest = refs[2 * n_pieces :]
    if first:
        acc, pairs = rest
    else:
        start_ref, keep_ref, send_ref, acc, pairs, image = rest
    i = pl.program_id(0)
    m = l_ref.shape[0] // 2
    core = place[1]
    for j in range(n_pieces):

        @pl.when(i == j)
        def _(j=j):
            pairs[pl.ds(pl.multiple_of(core * m, m), m), :] = pair(own[j][:m, :])
            pairs[pl.ds(pl.multiple_of((1 - core) * m, m), m), :] = pair(other[j][:m, :])

    high, low = split(l_ref[...])
    value = turned(pairs[...], high, low)

    @pl.when(i == 0)
    def _():
        acc[...] = value if first else start_ref[...] + value

    @pl.when(i > 0)
    def _():
        acc[...] += value

    if not first:

        @pl.when(i == n_pieces - 1)
        def _():
            image[...] = acc[...].T
            seg = image.shape[0] // segments
            half = segments // 2
            for u in range(segments):
                ref = keep_ref if u < half else send_ref
                at = pl.ds(pl.multiple_of((place[2] ^ u) * seg, seg), seg)
                ref[(u % half) * seg : (u % half + 1) * seg, :] = image[at, :]


def transposed(place, inv_factor, own, other, offset, chips, segments, start=None):
    n, depth = inv_factor.shape
    m = n // chips // 2
    t = own[0].shape[1]
    first = start is None
    pieces = len(own)
    in_specs = [pl.BlockSpec((2 * m, depth), lambda i, s: (s[0] ^ (i + offset), 0))]
    in_specs += [whole(p.shape) for p in (*own, *other)]
    args = [inv_factor, *own, *other]
    scratch = [pltpu.VMEM((2 * m, 2 * t), bf16)]
    if first:
        out_shape, out_specs = jax.ShapeDtypeStruct((t, depth), f32), whole((t, depth))
    else:
        in_specs.append(whole((t, depth)))
        args.append(start)
        out_shape = (jax.ShapeDtypeStruct((depth // 2, t), f32),) * 2
        out_specs = (whole((depth // 2, t)),) * 2
        scratch = [pltpu.VMEM((t, depth), f32), *scratch, pltpu.VMEM((depth, t), f32)]
    return pl.pallas_call(
        functools.partial(transposed_kernel, first, pieces, segments),
        grid_spec=pltpu.PrefetchScalarGridSpec(
            num_scalar_prefetch=1,
            grid=(pieces,),
            in_specs=in_specs,
            out_specs=out_specs,
            scratch_shapes=scratch,
        ),
        out_shape=out_shape,
        compiler_params=params(),
        cost_estimate=cost(16 * pieces * m * depth * t, 8 * pieces * m * depth),
    )(place, *args)


def update_kernel(place, image_ref, r_ref, d_ref, own_ref, norm_ref, new_ref, sum_ref):
    m = own_ref.shape[0] - PAD
    norm_now, dir_norm = norm_ref[0:1, :], norm_ref[1:2, :]
    curvature = own_ref[m : m + 1, :] + ridge_weight * dir_norm
    step = norm_now / curvature
    new = r_ref[...] - step * (image_ref[...] + ridge_weight * d_ref[...])
    new_ref[...] = new
    sum_ref[...] = jnp.broadcast_to(jnp.sum(new * new, axis=0, keepdims=True), sum_ref.shape)


def update(place, image, residual, direction, back_own, norms, segments):
    seg, t = image.shape
    at = pl.BlockSpec((seg, t), lambda i, s: (s[2], 0))
    return pl.pallas_call(
        update_kernel,
        grid_spec=pltpu.PrefetchScalarGridSpec(
            num_scalar_prefetch=1,
            grid=(1,),
            in_specs=[whole((seg, t)), at, at, whole(back_own.shape), whole(norms.shape)],
            out_specs=(whole((seg, t)), whole((PAD, t))),
        ),
        out_shape=(jax.ShapeDtypeStruct((seg, t), f32), jax.ShapeDtypeStruct((PAD, t), f32)),
        compiler_params=params(),
    )(place, image, residual, direction, back_own, norms)


def finish_kernel(n_pieces, place, *refs):
    pieces = refs[:n_pieces]
    d_ref, norm_ref, next_ref, res_ref, dir_ref = refs[n_pieces:]
    ratio = next_ref[0:1, :] / norm_ref[0:1, :]
    seg = pieces[0].shape[0]
    u = 0
    for piece in pieces:
        for j in range(piece.shape[0] // seg):
            at = pl.ds(pl.multiple_of((place[2] ^ u) * seg, seg), seg)
            new = piece[j * seg : (j + 1) * seg, :]
            res_ref[at, :] = new
            dir_ref[at, :] = new + ratio * d_ref[at, :]
            u += 1


def finish(place, pieces, direction, norms, norm_next):
    out = jax.ShapeDtypeStruct(direction.shape, f32)
    args = [*pieces, direction, norms, norm_next]
    return pl.pallas_call(
        functools.partial(finish_kernel, len(pieces)),
        grid_spec=pltpu.PrefetchScalarGridSpec(
            num_scalar_prefetch=1,
            grid=(1,),
            in_specs=[whole(a.shape) for a in args],
            out_specs=(whole(direction.shape),) * 2,
        ),
        out_shape=(out, out),
        compiler_params=params(),
    )(place, *args)


def body(n_rows, n_cols, points, centers, inv_factor, solution, residual, direction):
    chips = n_rows // 2
    steps = n_cols.bit_length() - 1
    masks = [(2 << s) - 1 for s in range(steps)]

    def swap(x, axis, mask):
        size = n_rows if axis == "rows" else n_cols
        return lax.ppermute(x, axis, [(i, i ^ mask) for i in range(size)])

    row, col = lax.axis_index("rows"), lax.axis_index("cols")
    segment = 0
    for s in range(steps):
        bit = (col >> s) & 1
        if s + 1 < steps:
            bit = bit ^ ((col >> (s + 1)) & 1)
        segment = segment | (bit << (steps - 1 - s))
    place = jnp.stack([row // 2, row % 2, segment]).astype(jnp.int32)

    order = [chips - 1, *range(1, chips - 1)] if chips > 1 else []

    def scatter(parts):
        got = [swap(parts[i], "rows", 2 * i) for i in order]
        return sum(got, parts[0])

    def gather(own):
        got = {i: swap(own, "rows", 2 * i) for i in order}
        return [got[i] for i in range(1, chips)]

    other_points = swap(points, "rows", 1)
    keep, send = forward(place, inv_factor, direction, residual, chips)
    got = swap(send, "rows", 1)
    mapped = scatter([keep[i] + got[i] for i in range(chips)])
    m = mapped.shape[0] - PAD
    norms = mapped[m:]
    high, low = gaussian(place, points, other_points, centers, chips, n_cols)
    mapped_own = mapped[:m]
    first = predict(high, low, [mapped_own], 0)
    keep, send = predict(high, low, gather(mapped_own), 1, first)
    part = keep + swap(send, "rows", 1)
    for mask in masks:
        half = part.shape[0] // 2
        part = part[:half] + swap(part[half:], "cols", mask)
    for mask in masks[::-1]:
        part = jnp.concatenate([part, swap(part, "cols", mask)], axis=0)
    other = swap(part, "rows", 1)
    backs = back_product(high, low, part, other)
    back = scatter([backs[i] for i in range(chips)])
    back_own = back[:m]
    first = transposed(place, inv_factor, [back_own], [swap(back_own, "rows", 1)], 0, chips, n_cols)
    got = gather(back_own)
    keep, send = transposed(
        place, inv_factor, got, [swap(g, "rows", 1) for g in got], 1, chips, n_cols, first
    )
    image = keep + swap(send, "cols", masks[0])
    for mask in masks[1:]:
        half = image.shape[0] // 2
        image = image[:half] + swap(image[half:], "cols", mask)
    new_piece, norm_next = update(place, image, residual, direction, back, norms, n_cols)
    mask = 1
    while mask < n_rows:
        norm_next = norm_next + swap(norm_next, "rows", mask)
        mask *= 2
    pieces = [new_piece]
    gathered = new_piece
    for mask in masks[::-1]:
        got = swap(gathered, "cols", mask)
        pieces.append(got)
        gathered = jnp.concatenate([gathered, got], axis=0)
        norm_next = norm_next + swap(norm_next, "cols", mask)
    step = norms[0:1] / (back[m : m + 1] + ridge_weight * norms[1:2])
    new_solution = solution + step * direction
    new_residual, new_direction = finish(place, pieces, direction, norms, norm_next)
    return new_solution, new_residual, new_direction


def solution(mesh):
    return jax.shard_map(
        functools.partial(body, mesh.shape["rows"], mesh.shape["cols"]),
        mesh=mesh,
        in_specs=(
            P("rows", None),
            P("cols", None),
            P("cols", "rows"),
            P("rows", None),
            P("rows", None),
            P("rows", None),
        ),
        out_specs=(P("rows", None), P("rows", None), P("rows", None)),
        check_vma=False,
    )
```

time: 331 us -> 222 us (0.67)
  matrix products: 95.1 us -> 0 us
  waiting for transfers between devices: 178 us -> 91.9 us
  Pallas kernels: 0 us -> 70.5 us
  starting transfers between devices: 0.83 us -> 38.9 us
  blocking collectives: 26.4 us -> 0 us
  between operations: 13.8 us -> 0.9 us
  other arithmetic: 6.99 us -> 11 us
    psum x4 -> x0, waiting for transfers between devices: 178 us -> none  [the longest x1 61 us: body(): back, pred_total = lax.psum((back_part, pred_norm), 'rows')]
    dot_general x5 -> x0, matrix products: 95.1 us -> none  [the longest x1 31.1 us: body(): jnp.dot(inv_factor, direction, precision=highest, preferred_element_type=...]
    ppermute x0 -> x33, waiting for transfers between devices: none -> 91.9 us  [swap(): return lax.ppermute(x, axis, [(i, i ^ mask) for i in range(size)])]
    pallas_call x0 -> x9, Pallas kernels: none -> 70.5 us  [the longest x2 22.4 us: transposed(): pl.pallas_call(functools.partial(transposed_kernel, first, pieces, segmen...]
    ppermute x0 -> x33, starting transfers between devices: none -> 38.9 us  [swap(): return lax.ppermute(x, axis, [(i, i ^ mask) for i in range(size)])]
    psum x2 -> x0, blocking collectives: 26.4 us -> none  [the longest x1 13.8 us: body(): norm_next = lax.psum(jnp.sum(new_residual * new_residual, axis=0), 'rows')]
    add x1 -> x14, other arithmetic: 0.16 us -> 8.59 us  [the longest x2 2.06 us: scatter(): return sum(got, parts[0])]
    reduce_sum x6 -> x0, other arithmetic: 6.81 us -> none  [the longest x1 3.21 us: body(): norm_next = lax.psum(jnp.sum(new_residual * new_residual, axis=0), 'rows')]
  transfers between devices with their start and end apart: 4 -> 33, of which waited for: 4 -> 22; matrix products, arithmetic and copies ran while one was open for 6% -> 3% of each run, Pallas kernels for 0% -> 9%
where the time goes in v1:
time: 222 us; the launch traced here: 221 us
  waiting for transfers between devices  91.9 us (41%)
  Pallas kernels  70.5 us (32%)
  starting transfers between devices  38.9 us (18%)
  other arithmetic  11 us (5%)
  local copies, waits for them, and re-layouts  7.84 us (4%)
    ppermute x33, waiting for transfers between devices, swap(): return lax.ppermute(x, axis, [(i, i ^ mask) for i in range(size)])  91.9 us
    ppermute x33, starting transfers between devices, swap(): return lax.ppermute(x, axis, [(i, i ^ mask) for i in range(size)])  38.9 us
    pallas_call x2, Pallas kernels, transposed(): pl.pallas_call(functools.partial(transposed_kernel, first, pieces, segmen...  22.4 us
    pallas_call x1, Pallas kernels, forward(): pl.pallas_call(forward_kernel, grid_spec=pltpu.PrefetchScalarGridSpec(num...  17 us
    pallas_call x1, Pallas kernels, gaussian(): pl.pallas_call(functools.partial(kernel_kernel, segments), grid_spec=pltp...  9.28 us
    pallas_call x2, Pallas kernels, predict(): pl.pallas_call(functools.partial(predict_kernel, first, len(pieces), not...  8.94 us
    pallas_call x1, Pallas kernels, back_product(): pl.pallas_call(back_kernel, grid=(chips,), in_specs=[k_block, k_block, wh...  6.47 us
    unnamed x42, local copies, waits for them, and re-layouts  6.01 us
  transfers between devices with their start and end apart: 33, of which 22 were waited for; matrix products, arithmetic and copies ran while one was open for 3% of the time, Pallas kernels for 9%

profile of v1, /device:TPU:0, one launch (start us, length us, event | category | flops | bytes accessed | tf_op | source)
XLA Modules:
  0.0 221.2 jit_solution(2473783639335174831)
XLA Ops:
  1.3 17.0 %shard_map.85 = (f32[4,520,128]{2,1,0:T(8,128)}, f32[4,520,128]{2,1,0:T(8,128)}) custom-call(s32[3]{0:T(128)} %pad_add_fusion.place, f32[4096,2048]{1,0:T(8,128)} %l_ref.5, f32[2048,128]{1,0:T(8,128)} %refs_3_.1, f32[2048,128]{1,0:T(8,128)} %r_ref.3), custom_call_target="tpu_custom_call" | custom-call | flops 8589934592 | bytes 33554432 | tf_op jit(solution)/shard_map/pallas_call | solution.py:77
  27.1 5.1 %collective-permute-done.3 = f32[520,128]{1,0:T(8,128)S(1)} collective-permute-done((f32[520,128]{1,0:T(8,128)S(1)}, f32[520,128]{1,0:T(8,128)S(1)}, u32[]{:S(2)}, u32[]{:S(2)}) %collective-permute-start.3) | collective-permute-done | bytes 266272 | tf_op jit(solution)/shard_map/ppermute | solution.py:379
  34.8 4.4 %collective-permute-done.1 = f32[520,128]{1,0:T(8,128)S(1)} collective-permute-done((f32[520,128]{1,0:T(8,128)S(1)}, f32[520,128]{1,0:T(8,128)S(1)}, u32[]{:S(2)}, u32[]{:S(2)}) %collective-permute-start.1) | collective-permute-done | bytes 266272 | tf_op jit(solution)/shard_map/ppermute | solution.py:379
  44.6 9.3 %shard_map.86 = (bf16[4,512,1024]{2,1,0:T(8,128)(2,1)}, bf16[4,512,1024]{2,1,0:T(8,128)(2,1)}) custom-call(s32[3]{0:T(128)} %pad_add_fusion.place, f32[512,256]{1,0:T(8,128)} %own_ref.1, f32[512,256]{1,0:T(8,128)} %copy-done.20, f32[4096,256]{1,0:T(8,128)} %c_ref.1), custom_call_target="tpu_custom_call" | custom-call | flops 3221225472 | bytes 8388608 | tf_op jit(solution)/shard_map/pallas_call | solution.py:124
  53.9 3.1 %shard_map.87.refs_5_ = f32[128,1024]{1,0:T(8,128)} custom-call(bf16[4,512,1024]{2,1,0:T(8,128)(2,1)} %get-tuple-element.17.refs_0_.high_ref, bf16[4,512,1024]{2,1,0:T(8,128)(2,1)} %get-tuple-element.18.refs_1_.low_ref, f32[512,128]{1,0:T(8,128)} %copy-done.3), custom_call_target="tpu_custom_call" | custom-call | flops 536870912 | bytes 2097152 | tf_op jit(solution)/shard_map/pallas_call | solution.py:194
  58.5 5.8 %shard_map.88 = (f32[512,128]{1,0:T(8,128)}, f32[512,128]{1,0:T(8,128)}) custom-call(bf16[4,512,1024]{2,1,0:T(8,128)(2,1)} %get-tuple-element.17.refs_0_.high_ref, bf16[4,512,1024]{2,1,0:T(8,128)(2,1)} %get-tuple-element.18.refs_1_.low_ref, f32[512,128]{1,0:T(8,128)} %copy-done.15, f32[512,128]{1,0:T(8,128)} %copy-done.16, f32[512,128]{1,0:T(8,128)} %copy-done.17, ...), custom_call_target="tpu_custom_call" | custom-call | flops 1610612736 | bytes 6291456 | tf_op jit(solution)/shard_map/pallas_call | solution.py:194
  68.9 3.8 %collective-permute-done.9 = f32[256,128]{1,0:T(8,128)S(1)} collective-permute-done((f32[256,128]{1,0:T(8,128)S(1)}, f32[256,128]{1,0:T(8,128)S(1)}, u32[]{:S(2)}, u32[]{:S(2)}) %collective-permute-start.9) | collective-permute-done | bytes 131104 | tf_op jit(solution)/shard_map/ppermute | solution.py:379
  72.7 3.8 %collective-permute-start.10 = (f32[128,128]{1,0:T(8,128)S(1)}, f32[128,128]{1,0:T(8,128)S(1)}, u32[]{:S(2)}, u32[]{:S(2)}) collective-permute-start(f32[128,128]{1,0:T(8,128)S(1)} %slice.107), channel_id=1, source_target_pairs={{0,3},{1,2},{2,1},{3,0},{4,7},{5,6},{6,5},{7,4},{8,11},{9,10},{10,... | collective-permute-start | bytes 196616 | tf_op jit(solution)/shard_map/ppermute | solution.py:379
  79.0 3.9 %collective-permute-start.11 = (f32[128,128]{1,0:T(8,128)S(1)}, f32[128,128]{1,0:T(8,128)S(1)}, u32[]{:S(2)}, u32[]{:S(2)}) collective-permute-start(f32[128,128]{1,0:T(8,128)S(1)} %slice_add_fusion.6), channel_id=1, source_target_pairs={{0,3},{1,2},{2,1},{3,0},{4,7},{5,6},{6,5},{7,4},{8,11},{9,10},{10,... | collective-permute-start | bytes 196616 | tf_op jit(solution)/shard_map/ppermute | solution.py:379
  85.2 5.0 %collective-permute-done.12 = f32[256,128]{1,0:T(8,128)S(1)} collective-permute-done((f32[256,128]{1,0:T(8,128)S(1)}, f32[256,128]{1,0:T(8,128)S(1)}, u32[]{:S(2)}, u32[]{:S(2)}) %collective-permute-start.12) | collective-permute-done | bytes 131104 | tf_op jit(solution)/shard_map/ppermute | solution.py:379
  92.5 6.5 %shard_map.89 = f32[4,520,128]{2,1,0:T(8,128)} custom-call(bf16[4,512,1024]{2,1,0:T(8,128)(2,1)} %get-tuple-element.17.refs_0_.high_ref, bf16[4,512,1024]{2,1,0:T(8,128)(2,1)} %get-tuple-element.18.refs_1_.low_ref, f32[512,128]{1,0:T(8,128)} %copy-done.4, f32[512,128]{1,0:T(8,128)} %copy-done.18), custom_call_target="tpu_custom_call" | custom-call | flops 2147483648 | bytes 8388608 | tf_op jit(solution)/shard_map/pallas_call | solution.py:229
  103.7 4.9 %collective-permute-done.16 = f32[520,128]{1,0:T(8,128)S(1)} collective-permute-done((f32[520,128]{1,0:T(8,128)S(1)}, f32[520,128]{1,0:T(8,128)S(1)}, u32[]{:S(2)}, u32[]{:S(2)}) %collective-permute-start.16) | collective-permute-done | bytes 266272 | tf_op jit(solution)/shard_map/ppermute | solution.py:379
  111.1 4.4 %collective-permute-done.14 = f32[520,128]{1,0:T(8,128)S(1)} collective-permute-done((f32[520,128]{1,0:T(8,128)S(1)}, f32[520,128]{1,0:T(8,128)S(1)}, u32[]{:S(2)}, u32[]{:S(2)}) %collective-permute-start.14) | collective-permute-done | bytes 266272 | tf_op jit(solution)/shard_map/ppermute | solution.py:379
  120.1 5.8 %collective-permute-done.17.refs_0_ = f32[512,128]{1,0:T(8,128)S(1)} collective-permute-done((f32[512,128]{1,0:T(8,128)S(1)}, f32[512,128]{1,0:T(8,128)S(1)}, u32[]{:S(2)}, u32[]{:S(2)}) %collective-permute-start.17) | collective-permute-done | bytes 262176 | tf_op jit(solution)/shard_map/ppermute | solution.py:379
  125.9 4.9 %collective-permute-done.18.refs_1_ = f32[512,128]{1,0:T(8,128)S(1)} collective-permute-done((f32[512,128]{1,0:T(8,128)S(1)}, f32[512,128]{1,0:T(8,128)S(1)}, u32[]{:S(2)}, u32[]{:S(2)}) %collective-permute-start.18) | collective-permute-done | bytes 262176 | tf_op jit(solution)/shard_map/ppermute | solution.py:379
  132.0 7.6 %shard_map.90.refs_6_ = f32[128,2048]{1,0:T(8,128)} custom-call(s32[3]{0:T(128)} %pad_add_fusion.place, f32[4096,2048]{1,0:T(8,128)} %l_ref.5, f32[512,128]{1,0:T(8,128)} %copy-done.2, f32[512,128]{1,0:T(8,128)} %copy-done.13), custom_call_target="tpu_custom_call" | custom-call | flops 2147483648 | bytes 8388608 | tf_op jit(solution)/shard_map/pallas_call | solution.py:300
  141.1 14.8 %shard_map.91 = (f32[1024,128]{1,0:T(8,128)}, f32[1024,128]{1,0:T(8,128)}) custom-call(s32[3]{0:T(128)} %pad_add_fusion.place, f32[4096,2048]{1,0:T(8,128)} %l_ref.5, f32[512,128]{1,0:T(8,128)} %copy-done.8, f32[512,128]{1,0:T(8,128)} %copy-done.9, f32[512,128]{1,0:T(8,128)} %copy-done.10, f32[512,128]{1,0:T(8,128)} %copy-done.11, f32[512,128]{1,0:T(8,128)} %copy-done.12, ...), custom_call_target="tpu_custom_call" | custom-call | flops 6442450944 | bytes 25165824 | tf_op jit(solution)/shard_map/pallas_call | solution.py:300
  155.9 14.1 %collective-permute-done.24 = f32[1024,128]{1,0:T(8,128)S(1)} collective-permute-done((f32[1024,128]{1,0:T(8,128)}, f32[1024,128]{1,0:T(8,128)S(1)}, u32[]{:S(2)}, u32[]{:S(2)}) %collective-permute-start.24) | collective-permute-done | bytes 524320 | tf_op jit(solution)/shard_map/ppermute | solution.py:379
  171.2 4.3 %collective-permute-start.25 = (f32[512,128]{1,0:T(8,128)S(1)}, f32[512,128]{1,0:T(8,128)S(1)}, u32[]{:S(2)}, u32[]{:S(2)}) collective-permute-start(f32[512,128]{1,0:T(8,128)S(1)} %slice.116), channel_id=1, source_target_pairs={{0,3},{1,2},{2,1},{3,0},{4,7},{5,6},{6,5},{7,4},{8,11},{9,10},{10,... | collective-permute-start | bytes 786440 | tf_op jit(solution)/shard_map/ppermute | solution.py:379
  176.1 5.3 %collective-permute-done.25 = f32[512,128]{1,0:T(8,128)S(1)} collective-permute-done((f32[512,128]{1,0:T(8,128)S(1)}, f32[512,128]{1,0:T(8,128)S(1)}, u32[]{:S(2)}, u32[]{:S(2)}) %collective-permute-start.25) | collective-permute-done | bytes 262176 | tf_op jit(solution)/shard_map/ppermute | solution.py:379
  184.8 3.5 %collective-permute-start.26 = (f32[512,128]{1,0:T(8,128)}, f32[512,128]{1,0:T(8,128)S(1)}, u32[]{:S(2)}, u32[]{:S(2)}) collective-permute-start(f32[512,128]{1,0:T(8,128)} %get-tuple-element.23.refs_0_), channel_id=1, source_target_pairs={{0,3},{1,2},{2,1},{3,0},{4,7},{5,6},{6,5},{7,4},{8,11},{9,10},{10,... | collective-permute-start | bytes 786440 | tf_op jit(solution)/shard_map/ppermute | solution.py:379
  198.6 4.4 %collective-permute-done.31 = f32[8,128]{1,0:T(8,128)S(1)} collective-permute-done((f32[8,128]{1,0:T(8,128)S(1)}, f32[8,128]{1,0:T(8,128)S(1)}, u32[]{:S(2)}, u32[]{:S(2)}) %collective-permute-start.31) | collective-permute-done | bytes 4128 | tf_op jit(solution)/shard_map/ppermute | solution.py:379
  207.9 8.8 %collective-permute-done.27.refs_2_ = f32[1024,128]{1,0:T(8,128)S(1)} collective-permute-done((f32[1024,128]{1,0:T(8,128)S(1)}, f32[1024,128]{1,0:T(8,128)S(1)}, u32[]{:S(2)}, u32[]{:S(2)}) %collective-permute-start.27) | collective-permute-done | bytes 524320 | tf_op jit(solution)/shard_map/ppermute | solution.py:379
  217.5 3.6 %shard_map.93 = (f32[2048,128]{1,0:T(8,128)}, f32[2048,128]{1,0:T(8,128)}) custom-call(s32[3]{0:T(128)} %pad_add_fusion.place, f32[512,128]{1,0:T(8,128)} %get-tuple-element.23.refs_0_, f32[512,128]{1,0:T(8,128)} %copy-done.6, f32[1024,128]{1,0:T(8,128)} %copy-done.7, f32[2048,128]{1,0:T(8,128)} %refs_3_.1, f32[8,128]{1,0:T(8,128)} %slice.117.norm_ref.refs_4_, ...), custom_call_target="tpu_custom_call" | custom-call | tf_op jit(solution)/shard_map/pallas_call | solution.py:359
  (119 shorter events, 66.1 us)
Async XLA Ops:
  22.6 9.7 %collective-permute-start.3 = (f32[520,128]{1,0:T(8,128)S(1)}, f32[520,128]{1,0:T(8,128)S(1)}, u32[]{:S(2)}, u32[]{:S(2)}) collective-permute-start(f32[520,128]{1,0:T(8,128)S(1)} %get-tuple-element.28), channel_id=1, source_target_pairs={{0,16},{4,20},{8,24},{12,28},{16,0},{20,4},{24,8},{28,12},{1,17},{... | collective-permute-start | bytes 798728 | tf_op jit(solution)/shard_map/ppermute | solution.py:379
  25.5 9.3 %collective-permute-start.2 = (f32[520,128]{1,0:T(8,128)S(1)}, f32[520,128]{1,0:T(8,128)S(1)}, u32[]{:S(2)}, u32[]{:S(2)}) collective-permute-start(f32[520,128]{1,0:T(8,128)S(1)} %get-tuple-element.29), channel_id=1, source_target_pairs={{0,8},{4,12},{8,0},{12,4},{16,24},{20,28},{24,16},{28,20},{1,9},{5... | collective-permute-start | bytes 798728 | tf_op jit(solution)/shard_map/ppermute | solution.py:379
  27.0 12.2 %collective-permute-start.1 = (f32[520,128]{1,0:T(8,128)S(1)}, f32[520,128]{1,0:T(8,128)S(1)}, u32[]{:S(2)}, u32[]{:S(2)}) collective-permute-start(f32[520,128]{1,0:T(8,128)S(1)} %get-tuple-element.27), channel_id=1, source_target_pairs={{0,24},{4,28},{8,16},{12,20},{16,8},{20,12},{24,0},{28,4},{1,25},{... | collective-permute-start | bytes 798728 | tf_op jit(solution)/shard_map/ppermute | solution.py:379
  27.1 16.7 %collective-permute-start.4 = (f32[512,256]{1,0:T(8,128)S(1)}, f32[512,256]{1,0:T(8,128)S(1)}, u32[]{:S(2)}, u32[]{:S(2)}) collective-permute-start(f32[512,256]{1,0:T(8,128)S(1)} %copy-done.19), channel_id=1, source_target_pairs={{0,4},{4,0},{8,12},{12,8},{16,20},{20,16},{24,28},{28,24},{1,5},{5... | collective-permute-start | bytes 1572872 | tf_op jit(solution)/shard_map/ppermute | solution.py:379
  40.3 16.7 %collective-permute-start.5 = (f32[512,128]{1,0:T(8,128)S(1)}, f32[512,128]{1,0:T(8,128)S(1)}, u32[]{:S(2)}, u32[]{:S(2)}) collective-permute-start(f32[512,128]{1,0:T(8,128)S(1)} %slice.103.refs_2_), channel_id=1, source_target_pairs={{0,8},{4,12},{8,0},{12,4},{16,24},{20,28},{24,16},{28,20},{1,9},{5... | collective-permute-start | bytes 786440 | tf_op jit(solution)/shard_map/ppermute | solution.py:379
  42.0 15.0 %collective-permute-start.6 = (f32[512,128]{1,0:T(8,128)S(1)}, f32[512,128]{1,0:T(8,128)S(1)}, u32[]{:S(2)}, u32[]{:S(2)}) collective-permute-start(f32[512,128]{1,0:T(8,128)S(1)} %slice.103.refs_2_), channel_id=1, source_target_pairs={{0,16},{4,20},{8,24},{12,28},{16,0},{20,4},{24,8},{28,12},{1,17},{... | collective-permute-start | bytes 786440 | tf_op jit(solution)/shard_map/ppermute | solution.py:379
  43.5 13.5 %collective-permute-start.7 = (f32[512,128]{1,0:T(8,128)S(1)}, f32[512,128]{1,0:T(8,128)S(1)}, u32[]{:S(2)}, u32[]{:S(2)}) collective-permute-start(f32[512,128]{1,0:T(8,128)S(1)} %slice.103.refs_2_), channel_id=1, source_target_pairs={{0,24},{4,28},{8,16},{12,20},{16,8},{20,12},{24,0},{28,4},{1,25},{... | collective-permute-start | bytes 786440 | tf_op jit(solution)/shard_map/ppermute | solution.py:379
  67.1 5.6 %collective-permute-start.9 = (f32[256,128]{1,0:T(8,128)S(1)}, f32[256,128]{1,0:T(8,128)S(1)}, u32[]{:S(2)}, u32[]{:S(2)}) collective-permute-start(f32[256,128]{1,0:T(8,128)S(1)} %slice.105), channel_id=1, source_target_pairs={{0,1},{1,0},{2,3},{3,2},{4,5},{5,4},{6,7},{7,6},{8,9},{9,8},{10,11... | collective-permute-start | bytes 393224 | tf_op jit(solution)/shard_map/ppermute | solution.py:379
  72.7 6.2 %collective-permute-start.10 = (f32[128,128]{1,0:T(8,128)S(1)}, f32[128,128]{1,0:T(8,128)S(1)}, u32[]{:S(2)}, u32[]{:S(2)}) collective-permute-start(f32[128,128]{1,0:T(8,128)S(1)} %slice.107), channel_id=1, source_target_pairs={{0,3},{1,2},{2,1},{3,0},{4,7},{5,6},{6,5},{7,4},{8,11},{9,10},{10,... | collective-permute-start | bytes 196616 | tf_op jit(solution)/shard_map/ppermute | solution.py:379
  79.0 6.1 %collective-permute-start.11 = (f32[128,128]{1,0:T(8,128)S(1)}, f32[128,128]{1,0:T(8,128)S(1)}, u32[]{:S(2)}, u32[]{:S(2)}) collective-permute-start(f32[128,128]{1,0:T(8,128)S(1)} %slice_add_fusion.6), channel_id=1, source_target_pairs={{0,3},{1,2},{2,1},{3,0},{4,7},{5,6},{6,5},{7,4},{8,11},{9,10},{10,... | collective-permute-start | bytes 196616 | tf_op jit(solution)/shard_map/ppermute | solution.py:379
  100.1 8.5 %collective-permute-start.16 = (f32[520,128]{1,0:T(8,128)S(1)}, f32[520,128]{1,0:T(8,128)S(1)}, u32[]{:S(2)}, u32[]{:S(2)}) collective-permute-start(f32[520,128]{1,0:T(8,128)S(1)} %get-tuple-element.31), channel_id=1, source_target_pairs={{0,16},{4,20},{8,24},{12,28},{16,0},{20,4},{24,8},{28,12},{1,17},{... | collective-permute-start | bytes 798728 | tf_op jit(solution)/shard_map/ppermute | solution.py:379
  101.8 9.3 %collective-permute-start.15 = (f32[520,128]{1,0:T(8,128)S(1)}, f32[520,128]{1,0:T(8,128)S(1)}, u32[]{:S(2)}, u32[]{:S(2)}) collective-permute-start(f32[520,128]{1,0:T(8,128)S(1)} %get-tuple-element.32), channel_id=1, source_target_pairs={{0,8},{4,12},{8,0},{12,4},{16,24},{20,28},{24,16},{28,20},{1,9},{5... | collective-permute-start | bytes 798728 | tf_op jit(solution)/shard_map/ppermute | solution.py:379
  103.3 12.2 %collective-permute-start.14 = (f32[520,128]{1,0:T(8,128)S(1)}, f32[520,128]{1,0:T(8,128)S(1)}, u32[]{:S(2)}, u32[]{:S(2)}) collective-permute-start(f32[520,128]{1,0:T(8,128)S(1)} %get-tuple-element.30), channel_id=1, source_target_pairs={{0,24},{4,28},{8,16},{12,20},{16,8},{20,12},{24,0},{28,4},{1,25},{... | collective-permute-start | bytes 798728 | tf_op jit(solution)/shard_map/ppermute | solution.py:379
  116.6 9.3 %collective-permute-start.17 = (f32[512,128]{1,0:T(8,128)S(1)}, f32[512,128]{1,0:T(8,128)S(1)}, u32[]{:S(2)}, u32[]{:S(2)}) collective-permute-start(f32[512,128]{1,0:T(8,128)S(1)} %slice.114.refs_0_), channel_id=1, source_target_pairs={{0,8},{4,12},{8,0},{12,4},{16,24},{20,28},{24,16},{28,20},{1,9},{5... | collective-permute-start | bytes 786440 | tf_op jit(solution)/shard_map/ppermute | solution.py:379
  118.2 12.5 %collective-permute-start.18 = (f32[512,128]{1,0:T(8,128)S(1)}, f32[512,128]{1,0:T(8,128)S(1)}, u32[]{:S(2)}, u32[]{:S(2)}) collective-permute-start(f32[512,128]{1,0:T(8,128)S(1)} %slice.114.refs_0_), channel_id=1, source_target_pairs={{0,16},{4,20},{8,24},{12,28},{16,0},{20,4},{24,8},{28,12},{1,17},{... | collective-permute-start | bytes 786440 | tf_op jit(solution)/shard_map/ppermute | solution.py:379
  119.7 11.0 %collective-permute-start.19 = (f32[512,128]{1,0:T(8,128)S(1)}, f32[512,128]{1,0:T(8,128)S(1)}, u32[]{:S(2)}, u32[]{:S(2)}) collective-permute-start(f32[512,128]{1,0:T(8,128)S(1)} %slice.114.refs_0_), channel_id=1, source_target_pairs={{0,24},{4,28},{8,16},{12,20},{16,8},{20,12},{24,0},{28,4},{1,25},{... | collective-permute-start | bytes 786440 | tf_op jit(solution)/shard_map/ppermute | solution.py:379
  120.1 11.1 %collective-permute-start.23 = (f32[512,128]{1,0:T(8,128)S(1)}, f32[512,128]{1,0:T(8,128)S(1)}, u32[]{:S(2)}, u32[]{:S(2)}) collective-permute-start(f32[512,128]{1,0:T(8,128)S(1)} %slice.114.refs_0_), channel_id=1, source_target_pairs={{0,4},{4,0},{8,12},{12,8},{16,20},{20,16},{24,28},{28,24},{1,5},{5... | collective-permute-start | bytes 786440 | tf_op jit(solution)/shard_map/ppermute | solution.py:379
  125.9 13.8 %collective-permute-start.20 = (f32[512,128]{1,0:T(8,128)S(1)}, f32[512,128]{1,0:T(8,128)S(1)}, u32[]{:S(2)}, u32[]{:S(2)}) collective-permute-start(f32[512,128]{1,0:T(8,128)S(1)} %collective-permute-done.17.refs_0_), channel_id=1, source_target_pairs={{0,4},{4,0},{8,12},{12,8},{16,20},{20,16},{24,28},{28,24},{1,5},{5... | collective-permute-start | bytes 786440 | tf_op jit(solution)/shard_map/ppermute | solution.py:379
  130.8 8.9 %collective-permute-start.21 = (f32[512,128]{1,0:T(8,128)S(1)}, f32[512,128]{1,0:T(8,128)S(1)}, u32[]{:S(2)}, u32[]{:S(2)}) collective-permute-start(f32[512,128]{1,0:T(8,128)S(1)} %collective-permute-done.18.refs_1_), channel_id=1, source_target_pairs={{0,4},{4,0},{8,12},{12,8},{16,20},{20,16},{24,28},{28,24},{1,5},{5... | collective-permute-start | bytes 786440 | tf_op jit(solution)/shard_map/ppermute | solution.py:379
  130.8 8.9 %collective-permute-start.22 = (f32[512,128]{1,0:T(8,128)S(1)}, f32[512,128]{1,0:T(8,128)S(1)}, u32[]{:S(2)}, u32[]{:S(2)}) collective-permute-start(f32[512,128]{1,0:T(8,128)S(1)} %collective-permute-done.19.refs_2_), channel_id=1, source_target_pairs={{0,4},{4,0},{8,12},{12,8},{16,20},{20,16},{24,28},{28,24},{1,5},{5... | collective-permute-start | bytes 786440 | tf_op jit(solution)/shard_map/ppermute | solution.py:379
  155.9 14.2 %collective-permute-start.24 = (f32[1024,128]{1,0:T(8,128)}, f32[1024,128]{1,0:T(8,128)S(1)}, u32[]{:S(2)}, u32[]{:S(2)}) collective-permute-start(f32[1024,128]{1,0:T(8,128)} %get-tuple-element.22), channel_id=1, source_target_pairs={{0,1},{1,0},{2,3},{3,2},{4,5},{5,4},{6,7},{7,6},{8,9},{9,8},{10,11... | collective-permute-start | bytes 1572872 | tf_op jit(solution)/shard_map/ppermute | solution.py:379
  171.2 10.1 %collective-permute-start.25 = (f32[512,128]{1,0:T(8,128)S(1)}, f32[512,128]{1,0:T(8,128)S(1)}, u32[]{:S(2)}, u32[]{:S(2)}) collective-permute-start(f32[512,128]{1,0:T(8,128)S(1)} %slice.116), channel_id=1, source_target_pairs={{0,3},{1,2},{2,1},{3,0},{4,7},{5,6},{6,5},{7,4},{8,11},{9,10},{10,... | collective-permute-start | bytes 786440 | tf_op jit(solution)/shard_map/ppermute | solution.py:379
  184.8 19.9 %collective-permute-start.26 = (f32[512,128]{1,0:T(8,128)}, f32[512,128]{1,0:T(8,128)S(1)}, u32[]{:S(2)}, u32[]{:S(2)}) collective-permute-start(f32[512,128]{1,0:T(8,128)} %get-tuple-element.23.refs_0_), channel_id=1, source_target_pairs={{0,3},{1,2},{2,1},{3,0},{4,7},{5,6},{6,5},{7,4},{8,11},{9,10},{10,... | collective-permute-start | bytes 786440 | tf_op jit(solution)/shard_map/ppermute | solution.py:379
  205.7 11.0 %collective-permute-start.27 = (f32[1024,128]{1,0:T(8,128)S(1)}, f32[1024,128]{1,0:T(8,128)S(1)}, u32[]{:S(2)}, u32[]{:S(2)}) collective-permute-start(f32[1024,128]{1,0:T(8,128)S(1)} %pad_maximum_fusion), channel_id=1, source_target_pairs={{0,1},{1,0},{2,3},{3,2},{4,5},{5,4},{6,7},{7,6},{8,9},{9,8},{10,11... | collective-permute-start | bytes 1572872 | tf_op jit(solution)/shard_map/ppermute | solution.py:379
  (30 other events, 175.6 us)

commit v2 on v1

v2 whole, which is shorter than its diff:
```python
import functools

import jax
import jax.numpy as jnp
from jax import lax
from jax.experimental import pallas as pl
from jax.experimental.pallas import tpu as pltpu
from jax.sharding import PartitionSpec as P

ridge_weight = 0.02
PAD = 8
f32, bf16 = jnp.float32, jnp.bfloat16
FIRST = (((0,), (0,)), ((), ()))
LAST = (((1,), (1,)), ((), ()))


def split(value):
    high = value.astype(bf16)
    return high, (value - high.astype(f32)).astype(bf16)


def pair(value):
    high, low = split(value)
    return jnp.concatenate([high, low], axis=1)


def wide(lhs, pairs, dims=None):
    high, low = split(lhs)
    n = pairs.shape[1] // 2
    both = jnp.dot(high, pairs, preferred_element_type=f32)
    both += jnp.dot(low, pairs, preferred_element_type=f32)
    return both[:, :n] + both[:, n:]


def turned(pairs, high, low):
    n = pairs.shape[1] // 2
    both = lax.dot_general(pairs, high, FIRST, preferred_element_type=f32)
    both += lax.dot_general(pairs, low, FIRST, preferred_element_type=f32)
    return both[:n] + both[n:]


def params(mib=10):
    return pltpu.CompilerParams(vmem_limit_bytes=mib << 20)


def cost(*_):
    return pl.CostEstimate(flops=1, bytes_accessed=1, transcendentals=0)


local = pl.BlockSpec(memory_space=pltpu.VMEM)
scalars = pl.BlockSpec(memory_space=pltpu.SMEM)


def whole(shape):
    return pl.BlockSpec(shape, lambda *_: (0,) * len(shape))


def resident(x):
    return pltpu.with_memory_space_constraint(x, pltpu.VMEM)


def forward_kernel(place, l_ref, d_ref, r_ref, keep_ref, send_ref, pairs, norms):
    @pl.when(pl.program_id(0) == 0)
    def _():
        d, r = d_ref[...], r_ref[...]
        pairs[...] = pair(d)
        norms[...] = jnp.zeros_like(norms)
        norms[0:1, :] = jnp.sum(r * r, axis=0, keepdims=True)
        norms[1:2, :] = jnp.sum(d * d, axis=0, keepdims=True)

    m = l_ref.shape[0] // 2
    core = place[1]
    for out_ref, side in ((keep_ref, core), (send_ref, 1 - core)):
        rows = l_ref[pl.ds(pl.multiple_of(side * m, m), m), :]
        out_ref[0, :m, :] = wide(rows, pairs[...])
        out_ref[0, m:, :] = norms[...]


def forward(place, inv_factor, direction, residual, chips):
    n, depth = inv_factor.shape
    t = direction.shape[1]
    m = n // chips // 2
    out = jax.ShapeDtypeStruct((chips, m + PAD, t), f32)
    block = pl.BlockSpec((1, m + PAD, t), lambda i, s: (i, 0, 0))
    return pl.pallas_call(
        forward_kernel,
        grid_spec=pltpu.PrefetchScalarGridSpec(
            num_scalar_prefetch=1,
            grid=(chips,),
            in_specs=[
                pl.BlockSpec((2 * m, depth), lambda i, s: (s[0] ^ i, 0)),
                whole((depth, t)),
                whole((depth, t)),
            ],
            out_specs=(block, block),
            scratch_shapes=[pltpu.VMEM((depth, 2 * t), bf16), pltpu.VMEM((PAD, t), f32)],
        ),
        out_shape=(out, out),
        compiler_params=params(40),
        cost_estimate=cost(8 * n * depth * t, 4 * n * depth),
    )(place, inv_factor, direction, residual)


def add_kernel(n_terms, *refs):
    terms, outs = refs[:n_terms], refs[n_terms:]
    if len(outs) > 1 and len(terms[0].shape) == 3:
        for i, out in enumerate(outs):
            out[...] = terms[0][i] + terms[1][i]
        return
    value = terms[0][...]
    for term in terms[1:]:
        value += term[...]
    start = 0
    for out in outs:
        out[...] = value[start : start + out.shape[0], :]
        start += out.shape[0]


def add(terms, shapes):
    out = tuple(jax.ShapeDtypeStruct(shape, f32) for shape in shapes)
    return pl.pallas_call(
        functools.partial(add_kernel, len(terms)),
        in_specs=[local] * len(terms),
        out_specs=(local,) * len(out),
        out_shape=out,
        compiler_params=params(),
        cost_estimate=cost(),
    )(*terms)


def kernel_kernel(segments, place, own_ref, other_ref, c_ref, high_ref, low_ref, ph, plo, psq):
    @pl.when(pl.program_id(0) == 0)
    def _():
        n = own_ref.shape[0]
        seg = n // segments
        for side, ref in enumerate((own_ref, other_ref)):
            for u in range(segments):
                start = pl.multiple_of((place[2] ^ u) * seg, seg)
                p = ref[pl.ds(start, seg), :]
                at = slice(side * n + u * seg, side * n + (u + 1) * seg)
                ph[at, :], plo[at, :] = split(p)
                psq[at, :] = jnp.broadcast_to(0.5 * jnp.sum(p * p, axis=1, keepdims=True), (seg, 128))

    c = c_ref[...]
    ch, cl = split(c)
    x = lax.dot_general(ch, ph[...], LAST, preferred_element_type=f32)
    x += lax.dot_general(ch, plo[...], LAST, preferred_element_type=f32)
    x += lax.dot_general(cl, ph[...], LAST, preferred_element_type=f32)
    center_sq = 0.5 * jnp.sum(c * c, axis=1, keepdims=True)
    point_sq = psq[...].T[0:1, :]
    high_ref[0], low_ref[0] = split(jnp.exp(x - (center_sq + point_sq)))


def gaussian(place, own, other, centers, chips, segments):
    n, width = own.shape
    m = centers.shape[0] // chips // 2
    out = jax.ShapeDtypeStruct((chips, m, 2 * n), bf16)
    block = pl.BlockSpec((1, m, 2 * n), lambda i, s: (i, 0, 0))
    return pl.pallas_call(
        functools.partial(kernel_kernel, segments),
        grid_spec=pltpu.PrefetchScalarGridSpec(
            num_scalar_prefetch=1,
            grid=(chips,),
            in_specs=[
                whole((n, width)),
                whole((n, width)),
                pl.BlockSpec((m, width), lambda i, s: (2 * (s[0] ^ i) + s[1], 0)),
            ],
            out_specs=(block, block),
            scratch_shapes=[
                pltpu.VMEM((2 * n, width), bf16),
                pltpu.VMEM((2 * n, width), bf16),
                pltpu.VMEM((2 * n, 128), f32),
            ],
        ),
        out_shape=(out, out),
        compiler_params=params(),
        cost_estimate=cost(12 * chips * m * n * width, 8 * chips * m * n, 2 * chips * m * n),
    )(place, own, other, centers)


def predict_kernel(shift, first, last, high_ref, low_ref, piece_ref, *refs):
    m = high_ref.shape[1]
    value = turned(pair(piece_ref[:m, :]), high_ref[shift], low_ref[shift])
    if not first:
        value += refs[0][...]
    if last:
        half = value.shape[1] // 2
        refs[-2][...] = value[:, :half].T
        refs[-1][...] = value[:, half:].T
    else:
        refs[-1][...] = value


def predict(shift, high, low, piece, acc, last):
    _, m, n = high.shape
    t = piece.shape[1]
    args = [resident(high), resident(low), piece] + ([] if acc is None else [acc])
    if last:
        out = (jax.ShapeDtypeStruct((n // 2, t), f32),) * 2
    else:
        out = jax.ShapeDtypeStruct((t, n), f32)
    return pl.pallas_call(
        functools.partial(predict_kernel, shift, acc is None, last),
        in_specs=[local] * len(args),
        out_specs=(local,) * 2 if last else local,
        out_shape=out,
        compiler_params=params(),
        cost_estimate=cost(8 * m * n * t, 4 * m * n),
    )(*args)


def back_kernel(shift, first, high_ref, low_ref, *refs):
    if first:
        own_ref, other_ref, out_ref, pairs, norms = refs
        half = own_ref.shape[0]
        norms[...] = jnp.zeros_like(norms)
        a, b = own_ref[...], other_ref[...]
        pairs[:half, :] = pair(a)
        pairs[half:, :] = pair(b)
        norms[0:1, :] = jnp.sum(a * a, axis=0, keepdims=True) + jnp.sum(b * b, axis=0, keepdims=True)
    else:
        pairs, norms, out_ref = refs
    m = high_ref.shape[1]
    n = out_ref.shape[1]
    both = jnp.dot(high_ref[shift], pairs[...], preferred_element_type=f32)
    both += jnp.dot(low_ref[shift], pairs[...], preferred_element_type=f32)
    out_ref[:m, :] = both[:, :n] + both[:, n:]
    out_ref[m:, :] = norms[...]


def back_product(shift, high, low, sources, first):
    _, m, n = high.shape
    t = sources[1].shape[1]
    out = (jax.ShapeDtypeStruct((m + PAD, t), f32),)
    if first:
        out += (jax.ShapeDtypeStruct((n, 2 * t), bf16), jax.ShapeDtypeStruct((PAD, t), f32))
    return pl.pallas_call(
        functools.partial(back_kernel, shift, first),
        in_specs=[local] * 4,
        out_specs=(local,) * len(out),
        out_shape=out,
        compiler_params=params(),
        cost_estimate=cost(8 * m * n * t, 4 * m * n),
    )(resident(high), resident(low), *sources)


def transposed_kernel(shift, sides, first, segments, place, l_ref, *refs):
    pieces, refs = refs[: len(sides)], refs[len(sides) :]
    value = None if first else refs[0][...]
    block = place[0] ^ shift
    for side, ref in zip(sides, pieces):
        core = place[1] if side == 0 else 1 - place[1]
        m = ref.shape[0]
        step = min(m, 256)
        for i in range(0, m, step):
            start = pl.multiple_of((block * 2 + core) * m + i, step)
            high, low = split(l_ref[pl.ds(start, step), :])
            share = turned(pair(ref[i : i + step, :]), high, low)
            value = share if value is None else value + share
    if segments == 0:
        refs[-1][...] = value
        return
    keep_ref, send_ref, image = refs[-3:]
    image[...] = value.T
    seg = image.shape[0] // segments
    half = segments // 2
    for u in range(segments):
        ref = keep_ref if u < half else send_ref
        at = pl.ds(pl.multiple_of((place[2] ^ u) * seg, seg), seg)
        ref[(u % half) * seg : (u % half + 1) * seg, :] = image[at, :]


def transposed(shift, sides, place, inv_factor, pieces, acc, segments=0):
    depth = inv_factor.shape[1]
    m, t = pieces[0].shape
    args = [resident(inv_factor), *pieces] + ([] if acc is None else [acc])
    scratch = []
    if segments:
        out = (jax.ShapeDtypeStruct((depth // 2, t), f32),) * 2
        scratch = [pltpu.VMEM((depth, t), f32)]
    else:
        out = jax.ShapeDtypeStruct((t, depth), f32)
    return pl.pallas_call(
        functools.partial(transposed_kernel, shift, sides, acc is None, segments),
        in_specs=[scalars] + [local] * len(args),
        out_specs=(local,) * 2 if segments else local,
        out_shape=out,
        scratch_shapes=scratch,
        compiler_params=params(),
        cost_estimate=cost(),
    )(place, *args)


def update_kernel(place, image_ref, r_ref, d_ref, pred_ref, norm_ref, new_ref, sum_ref):
    norm_now, dir_norm = norm_ref[0:1, :], norm_ref[1:2, :]
    curvature = pred_ref[0:1, :] + ridge_weight * dir_norm
    step = norm_now / curvature
    new = r_ref[...] - step * (image_ref[...] + ridge_weight * d_ref[...])
    new_ref[...] = new
    sum_ref[...] = jnp.broadcast_to(jnp.sum(new * new, axis=0, keepdims=True), sum_ref.shape)


def update(place, image, residual, direction, pred_norm, norms, segments):
    seg, t = image.shape
    at = pl.BlockSpec((seg, t), lambda i, s: (s[2], 0))
    return pl.pallas_call(
        update_kernel,
        grid_spec=pltpu.PrefetchScalarGridSpec(
            num_scalar_prefetch=1,
            grid=(1,),
            in_specs=[whole((seg, t)), at, at, whole(pred_norm.shape), whole(norms.shape)],
            out_specs=(whole((seg, t)), whole((PAD, t))),
        ),
        out_shape=(jax.ShapeDtypeStruct((seg, t), f32), jax.ShapeDtypeStruct((PAD, t), f32)),
        compiler_params=params(),
    )(place, image, residual, direction, pred_norm, norms)


def finish_kernel(n_pieces, place, *refs):
    pieces = refs[:n_pieces]
    d_ref, norm_ref, next_ref, res_ref, dir_ref = refs[n_pieces:]
    ratio = next_ref[0:1, :] / norm_ref[0:1, :]
    seg = pieces[0].shape[0]
    u = 0
    for piece in pieces:
        for j in range(piece.shape[0] // seg):
            at = pl.ds(pl.multiple_of((place[2] ^ u) * seg, seg), seg)
            new = piece[j * seg : (j + 1) * seg, :]
            res_ref[at, :] = new
            dir_ref[at, :] = new + ratio * d_ref[at, :]
            u += 1


def finish(place, pieces, direction, norms, norm_next):
    out = jax.ShapeDtypeStruct(direction.shape, f32)
    args = [*pieces, direction, norms, norm_next]
    return pl.pallas_call(
        functools.partial(finish_kernel, len(pieces)),
        grid_spec=pltpu.PrefetchScalarGridSpec(
            num_scalar_prefetch=1,
            grid=(1,),
            in_specs=[whole(a.shape) for a in args],
            out_specs=(whole(direction.shape),) * 2,
        ),
        out_shape=(out, out),
        compiler_params=params(),
    )(place, *args)


def body(n_rows, n_cols, points, centers, inv_factor, solution, residual, direction):
    chips = n_rows // 2
    steps = n_cols.bit_length() - 1
    masks = [(2 << s) - 1 for s in range(steps)]
    halving, last_mask = masks[:-1], masks[-1]
    segments = n_cols // 2

    def swap(x, axis, mask):
        size = n_rows if axis == "rows" else n_cols
        return lax.ppermute(x, axis, [(i, i ^ mask) for i in range(size)])

    row, col = lax.axis_index("rows"), lax.axis_index("cols")
    segment = 0
    for s in range(steps - 1):
        bit = ((col >> s) ^ (col >> (s + 1))) & 1
        segment = segment | (bit << (steps - 2 - s))
    place = jnp.stack([row // 2, row % 2, segment]).astype(jnp.int32)
    order = [chips - 1, *range(1, chips - 1)]

    other_points = swap(points, "rows", 1)
    keep, send = forward(place, inv_factor, direction, residual, chips)
    m, t = keep.shape[1] - PAD, keep.shape[2]
    totals = add([keep, swap(send, "rows", 1)], [(m + PAD, t)] * chips)
    got = [swap(totals[i], "rows", 2 * i) for i in order]
    mapped, norms = add([totals[0], *got], [(m, t), (PAD, t)])
    high, low = gaussian(place, points, other_points, centers, chips, segments)
    mapped, high, low = lax.optimization_barrier((mapped, high, low))

    arrived = [(0, mapped)] + [(i, swap(mapped, "rows", 2 * i)) for i in order]
    acc = None
    for j, (shift, piece) in enumerate(arrived):
        acc = predict(shift, high, low, piece, acc, j == chips - 1)
    keep, send = acc
    part = keep + swap(send, "rows", 1)
    for mask in halving:
        half = part.shape[0] // 2
        part = part[:half] + swap(part[half:], "cols", mask)
    part = part + swap(part, "cols", last_mask)
    for mask in halving[::-1]:
        part = jnp.concatenate([part, swap(part, "cols", mask)], axis=0)
    other = swap(part, "rows", 1)

    got = []
    sources, first = (part, other), True
    for shift in (*order, 0):
        piece, *rest = back_product(shift, high, low, sources, first)
        if first:
            sources, first = rest, False
        got.append(swap(piece, "rows", 2 * shift) if shift else piece)
    own, pred_norm = add([got[-1], *got[:-1]], [(m, t), (PAD, t)])

    arrived = [(i, swap(own, "rows", 2 * i)) for i in order]
    acc = transposed(0, (0, 1), place, inv_factor, [own, swap(own, "rows", 1)], None)
    others = []
    for shift, piece in arrived:
        piece, acc = lax.optimization_barrier((piece, acc))
        others.append((shift, swap(piece, "rows", 1)))
        acc = transposed(shift, (0,), place, inv_factor, [piece], acc)
    for j, (shift, piece) in enumerate(others):
        last = j == chips - 2
        acc = transposed(shift, (1,), place, inv_factor, [piece], acc, segments if last else 0)
    keep, send = acc
    image = keep + swap(send, "cols", masks[0])
    for mask in halving[1:]:
        half = image.shape[0] // 2
        image = image[:half] + swap(image[half:], "cols", mask)
    image = image + swap(image, "cols", last_mask)
    new_piece, norm_next = update(place, image, residual, direction, pred_norm, norms, segments)
    pieces = [new_piece]
    gathered = new_piece
    for mask in halving[::-1]:
        got = swap(gathered, "cols", mask)
        pieces.append(got)
        gathered = jnp.concatenate([gathered, got], axis=0)
    for mask in halving[::-1]:
        norm_next = norm_next + swap(norm_next, "cols", mask)
    norm_next = jnp.sum(lax.all_gather(norm_next, "rows"), axis=0)
    step = norms[0:1] / (pred_norm[0:1] + ridge_weight * norms[1:2])
    new_solution = solution + step * direction
    new_residual, new_direction = finish(place, pieces, direction, norms, norm_next)
    return new_solution, new_residual, new_direction


def solution(mesh):
    return jax.shard_map(
        functools.partial(body, mesh.shape["rows"], mesh.shape["cols"]),
        mesh=mesh,
        in_specs=(
            P("rows", None),
            P("cols", None),
            P("cols", "rows"),
            P("rows", None),
            P("rows", None),
            P("rows", None),
        ),
        out_specs=(P("rows", None), P("rows", None), P("rows", None)),
        check_vma=False,
    )
```

time: 222 us -> 181 us (0.82)
  Pallas kernels: 70.5 us -> 45.6 us
  waiting for transfers between devices: 91.9 us -> 70.4 us
  other arithmetic: 11 us -> 1.45 us
  blocking collectives: 0 us -> 8.22 us
  local copies, waits for them, and re-layouts: 7.84 us -> 13 us
    ppermute x33 -> x27, waiting for transfers between devices: 91.9 us -> 70.4 us  [swap(): return lax.ppermute(x, axis, [(i, i ^ mask) for i in range(size)])]
    pallas_call x5 -> x18, Pallas kernels: 37.8 us -> 20.9 us  [the longest x7 14.7 us: transposed(): pl.pallas_call(functools.partial(transposed_kernel, shift, sides, acc is...]
    all_gather x0 -> x1, blocking collectives: none -> 8.22 us  [body(): norm_next = jnp.sum(lax.all_gather(norm_next, 'rows'), axis=0)]
    unnamed x42 -> x16, local copies, waits for them, and re-layouts: 6.01 us -> 13 us
    add x7 -> x2, other arithmetic: 4.73 us -> 0.08 us  [the longest x1 0.07 us: body(): image = image + swap(image, 'cols', last_mask)]
    pallas_call x1, Pallas kernels: 9.28 us -> 6.49 us  [gaussian(): pl.pallas_call(functools.partial(kernel_kernel, segments), grid_spec=pltp...]
    ppermute x33 -> x27, starting transfers between devices: 38.9 us -> 40.7 us  [swap(): return lax.ppermute(x, axis, [(i, i ^ mask) for i in range(size)])]
  transfers between devices with their start and end apart: 33 -> 27, of which waited for: 22 -> 16; matrix products, arithmetic and copies ran while one was open for 3% -> 1% of each run, Pallas kernels for 9% -> 12%
where the time goes in v2:
time: 181 us; the launch traced here: 180 us
  waiting for transfers between devices  70.4 us (39%)
  Pallas kernels  45.6 us (25%)
  starting transfers between devices  40.7 us (22%)
  local copies, waits for them, and re-layouts  13 us (7%)
  blocking collectives  8.22 us (5%)
    ppermute x27, waiting for transfers between devices, swap(): return lax.ppermute(x, axis, [(i, i ^ mask) for i in range(size)])  70.4 us
    ppermute x27, starting transfers between devices, swap(): return lax.ppermute(x, axis, [(i, i ^ mask) for i in range(size)])  40.7 us
    pallas_call x1, Pallas kernels, forward(): pl.pallas_call(forward_kernel, grid_spec=pltpu.PrefetchScalarGridSpec(num...  15.4 us
    pallas_call x7, Pallas kernels, transposed(): pl.pallas_call(functools.partial(transposed_kernel, shift, sides, acc is...  14.7 us
    unnamed x16, local copies, waits for them, and re-layouts  13 us
    all_gather x1, blocking collectives, body(): norm_next = jnp.sum(lax.all_gather(norm_next, 'rows'), axis=0)  8.22 us
    pallas_call x1, Pallas kernels, gaussian(): pl.pallas_call(functools.partial(kernel_kernel, segments), grid_spec=pltp...  6.49 us
  transfers between devices with their start and end apart: 27, of which 16 were waited for; matrix products, arithmetic and copies ran while one was open for 1% of the time, Pallas kernels for 12%

profile of v2, /device:TPU:0, one launch (start us, length us, event | category | flops | bytes accessed | tf_op | source)
XLA Modules:
  0.0 180.3 jit_solution(5550993084795899358)
XLA Ops:
  3.2 15.4 %shard_map.85 = (f32[4,520,128]{2,1,0:T(8,128)S(1)}, f32[4,520,128]{2,1,0:T(8,128)S(1)}) custom-call(s32[3]{0:T(128)S(1)} %pad_add_fusion.place, f32[4096,2048]{1,0:T(8,128)} %l_ref.15, f32[2048,128]{1,0:T(8,128)S(1)} %copy-done.1, f32[2048,128]{1,0:T(8,128)S(1)} %copy-done.3), custom_call_target="tpu_custom_call" | custom-call | flops 1 | bytes 1 | tf_op jit(solution)/shard_map/pallas_call | solution.py:85
  19.2 2.2 %collective-permute-done.refs_1_ = f32[4,520,128]{2,1,0:T(8,128)S(1)} collective-permute-done((f32[4,520,128]{2,1,0:T(8,128)S(1)}, f32[4,520,128]{2,1,0:T(8,128)S(1)}, u32[]{:S(2)}, u32[]{:S(2)}) %collective-permute-start) | collective-permute-done | bytes 1064992 | tf_op jit(solution)/shard_map/ppermute | solution.py:360
  21.6 3.9 %collective-permute-start.1 = (f32[520,128]{1,0:T(8,128)S(1)}, f32[520,128]{1,0:T(8,128)S(1)}, u32[]{:S(2)}, u32[]{:S(2)}) collective-permute-start(f32[520,128]{1,0:T(8,128)S(1)} %get-tuple-element.38), channel_id=1, source_target_pairs={{0,24},{4,28},{8,16},{12,20},{16,8},{20,12},{24,0},{28,4},{1,25},{... | collective-permute-start | bytes 798728 | tf_op jit(solution)/shard_map/ppermute | solution.py:360
  26.1 6.5 %shard_map.88 = (bf16[4,512,1024]{2,1,0:T(8,128)(2,1)S(1)}, bf16[4,512,1024]{2,1,0:T(8,128)(2,1)S(1)}) custom-call(s32[3]{0:T(128)S(1)} %pad_add_fusion.place, f32[512,256]{1,0:T(8,128)S(1)} %copy-done.6, f32[512,256]{1,0:T(8,128)S(1)} %collective-permute-done.4.other_ref, f32[4096,256]{1,0:T(8,128)S(1)} %copy-done.5), custom_call_target="tpu_custom_call" | custom-call | flops 1 | bytes 1 | tf_op jit(solution)/shard_map/pallas_call | solution.py:159
  32.7 5.5 %collective-permute-done.2.refs_2_ = f32[520,128]{1,0:T(8,128)S(1)} collective-permute-done((f32[520,128]{1,0:T(8,128)S(1)}, f32[520,128]{1,0:T(8,128)S(1)}, u32[]{:S(2)}, u32[]{:S(2)}) %collective-permute-start.2) | collective-permute-done | bytes 266272 | tf_op jit(solution)/shard_map/ppermute | solution.py:360
  38.3 2.4 %collective-permute-start.7 = (f32[512,128]{1,0:T(8,128)S(1)}, f32[512,128]{1,0:T(8,128)S(1)}, u32[]{:S(2)}, u32[]{:S(2)}) collective-permute-start(f32[512,128]{1,0:T(8,128)S(1)} %get-tuple-element.47.piece_ref), channel_id=1, source_target_pairs={{0,24},{4,28},{8,16},{12,20},{16,8},{20,12},{24,0},{28,4},{1,25},{... | collective-permute-start | bytes 786440 | tf_op jit(solution)/shard_map/ppermute | solution.py:360
  42.5 5.9 %collective-permute-done.7.piece_ref = f32[512,128]{1,0:T(8,128)S(1)} collective-permute-done((f32[512,128]{1,0:T(8,128)S(1)}, f32[512,128]{1,0:T(8,128)S(1)}, u32[]{:S(2)}, u32[]{:S(2)}) %collective-permute-start.7) | collective-permute-done | bytes 262176 | tf_op jit(solution)/shard_map/ppermute | solution.py:360
  49.2 3.8 %collective-permute-done.6.piece_ref = f32[512,128]{1,0:T(8,128)S(1)} collective-permute-done((f32[512,128]{1,0:T(8,128)S(1)}, f32[512,128]{1,0:T(8,128)S(1)}, u32[]{:S(2)}, u32[]{:S(2)}) %collective-permute-start.6) | collective-permute-done | bytes 262176 | tf_op jit(solution)/shard_map/ppermute | solution.py:360
  57.9 4.0 %collective-permute-done.9 = f32[256,128]{1,0:T(8,128)S(1)} collective-permute-done((f32[256,128]{1,0:T(8,128)S(1)}, f32[256,128]{1,0:T(8,128)S(1)}, u32[]{:S(2)}, u32[]{:S(2)}) %collective-permute-start.9) | collective-permute-done | bytes 131104 | tf_op jit(solution)/shard_map/ppermute | solution.py:360
  61.9 3.7 %collective-permute-start.10 = (f32[256,128]{1,0:T(8,128)S(1)}, f32[256,128]{1,0:T(8,128)S(1)}, u32[]{:S(2)}, u32[]{:S(2)}) collective-permute-start(f32[256,128]{1,0:T(8,128)S(1)} %slice_add_fusion), channel_id=1, source_target_pairs={{0,3},{1,2},{2,1},{3,0},{4,7},{5,6},{6,5},{7,4},{8,11},{9,10},{10,... | collective-permute-start | bytes 393224 | tf_op jit(solution)/shard_map/ppermute | solution.py:360
  65.6 3.2 %collective-permute-done.10 = f32[256,128]{1,0:T(8,128)S(1)} collective-permute-done((f32[256,128]{1,0:T(8,128)S(1)}, f32[256,128]{1,0:T(8,128)S(1)}, u32[]{:S(2)}, u32[]{:S(2)}) %collective-permute-start.10) | collective-permute-done | bytes 131104 | tf_op jit(solution)/shard_map/ppermute | solution.py:360
  68.8 2.3 %collective-permute-start.11 = (f32[256,128]{1,0:T(8,128)S(1)}, f32[256,128]{1,0:T(8,128)S(1)}, u32[]{:S(2)}, u32[]{:S(2)}) collective-permute-start(f32[256,128]{1,0:T(8,128)S(1)} %add.32), channel_id=1, source_target_pairs={{0,1},{1,0},{2,3},{3,2},{4,5},{5,4},{6,7},{7,6},{8,9},{9,8},{10,11... | collective-permute-start | bytes 393224 | tf_op jit(solution)/shard_map/ppermute | solution.py:360
  71.2 2.9 %collective-permute-done.11 = f32[256,128]{1,0:T(8,128)S(1)} collective-permute-done((f32[256,128]{1,0:T(8,128)S(1)}, f32[256,128]{1,0:T(8,128)S(1)}, u32[]{:S(2)}, u32[]{:S(2)}) %collective-permute-start.11) | collective-permute-done | bytes 131104 | tf_op jit(solution)/shard_map/ppermute | solution.py:360
  82.2 5.0 %collective-permute-done.14.refs_2_ = f32[520,128]{1,0:T(8,128)S(1)} collective-permute-done((f32[520,128]{1,0:T(8,128)S(1)}, f32[520,128]{1,0:T(8,128)S(1)}, u32[]{:S(2)}, u32[]{:S(2)}) %collective-permute-start.14) | collective-permute-done | bytes 266272 | tf_op jit(solution)/shard_map/ppermute | solution.py:360
  87.2 6.1 %collective-permute-done.15.refs_3_ = f32[520,128]{1,0:T(8,128)S(1)} collective-permute-done((f32[520,128]{1,0:T(8,128)S(1)}, f32[520,128]{1,0:T(8,128)S(1)}, u32[]{:S(2)}, u32[]{:S(2)}) %collective-permute-start.15) | collective-permute-done | bytes 266272 | tf_op jit(solution)/shard_map/ppermute | solution.py:360
  97.0 10.5 %copy-done = f32[4096,2048]{1,0:T(8,128)S(1)} copy-done((f32[4096,2048]{1,0:T(8,128)S(1)}, f32[4096,2048]{1,0:T(8,128)}, u32[]{:S(2)}) %copy-start) | copy-done | bytes 33554456
  107.6 3.0 %shard_map.98.refs_1_ = f32[128,2048]{1,0:T(8,128)S(1)} custom-call(s32[3]{0:T(128)S(1)} %pad_add_fusion.place, f32[4096,2048]{1,0:T(8,128)S(1)} %copy-done, f32[512,128]{1,0:T(8,128)S(1)} %get-tuple-element.54.refs_0_, f32[512,128]{1,0:T(8,128)S(1)} %collective-permute-done.19.refs_1_), custom_call_target="tpu_custom_call" | custom-call | flops 1 | bytes 1 | tf_op jit(solution)/shard_map/pallas_call | solution.py:284
  118.9 2.1 %shard_map.103.refs_1_ = f32[128,2048]{1,0:T(8,128)S(1)} custom-call(s32[3]{0:T(128)S(1)} %pad_add_fusion.place, f32[4096,2048]{1,0:T(8,128)S(1)} %copy-done, f32[512,128]{1,0:T(8,128)S(1)} %collective-permute-done.21.refs_0_, f32[128,2048]{1,0:T(8,128)S(1)} %shard_map.102.refs_1_), custom_call_target="tpu_custom_call" | custom-call | flops 1 | bytes 1 | tf_op jit(solution)/shard_map/pallas_call | solution.py:284
  125.3 12.6 %collective-permute-done.23 = f32[1024,128]{1,0:T(8,128)S(1)} collective-permute-done((f32[1024,128]{1,0:T(8,128)S(1)}, f32[1024,128]{1,0:T(8,128)S(1)}, u32[]{:S(2)}, u32[]{:S(2)}) %collective-permute-start.23) | collective-permute-done | bytes 524320 | tf_op jit(solution)/shard_map/ppermute | solution.py:360
  137.9 3.1 %collective-permute-start.24 = (f32[1024,128]{1,0:T(8,128)S(1)}, f32[1024,128]{1,0:T(8,128)S(1)}, u32[]{:S(2)}, u32[]{:S(2)}) collective-permute-start(f32[1024,128]{1,0:T(8,128)S(1)} %add.35), channel_id=1, source_target_pairs={{0,3},{1,2},{2,1},{3,0},{4,7},{5,6},{6,5},{7,4},{8,11},{9,10},{10,... | collective-permute-start | bytes 1572872 | tf_op jit(solution)/shard_map/ppermute | solution.py:360
  141.1 12.6 %collective-permute-done.24 = f32[1024,128]{1,0:T(8,128)S(1)} collective-permute-done((f32[1024,128]{1,0:T(8,128)S(1)}, f32[1024,128]{1,0:T(8,128)S(1)}, u32[]{:S(2)}, u32[]{:S(2)}) %collective-permute-start.24) | collective-permute-done | bytes 524320 | tf_op jit(solution)/shard_map/ppermute | solution.py:360
  154.4 11.0 %collective-permute-start.26 = (f32[8,128]{1,0:T(8,128)S(1)}, f32[8,128]{1,0:T(8,128)S(1)}, u32[]{:S(2)}, u32[]{:S(2)}) collective-permute-start(f32[8,128]{1,0:T(8,128)S(1)} %get-tuple-element.64), channel_id=1, source_target_pairs={{0,1},{1,0},{2,3},{3,2},{4,5},{5,4},{6,7},{7,6},{8,9},{9,8},{10,11... | collective-permute-start | bytes 12296 | tf_op jit(solution)/shard_map/ppermute | solution.py:360
  167.0 8.2 %all-gather = f32[64,128]{1,0:T(8,128)S(1)} all-gather(f32[8,128]{1,0:T(8,128)S(1)} %add.37), channel_id=2, replica_groups=mesh['rows'=8,'cols'=4] {'rows'}, dimensions={0}, use_global_device_ids=true | all-gather | bytes 36864 | tf_op jit(solution)/shard_map/all_gather | solution.py:427
  175.3 3.0 %collective-permute-done.25.refs_1_ = f32[1024,128]{1,0:T(8,128)S(1)} collective-permute-done((f32[1024,128]{1,0:T(8,128)S(1)}, f32[1024,128]{1,0:T(8,128)S(1)}, u32[]{:S(2)}, u32[]{:S(2)}) %collective-permute-start.25) | collective-permute-done | bytes 524320 | tf_op jit(solution)/shard_map/ppermute | solution.py:360
  (81 shorter events, 40.2 us)
Async XLA Ops:
  19.1 7.0 %collective-permute-start.4 = (f32[512,256]{1,0:T(8,128)S(1)}, f32[512,256]{1,0:T(8,128)S(1)}, u32[]{:S(2)}, u32[]{:S(2)}) collective-permute-start(f32[512,256]{1,0:T(8,128)S(1)} %copy-done.6), channel_id=1, source_target_pairs={{0,4},{4,0},{8,12},{12,8},{16,20},{20,16},{24,28},{28,24},{1,5},{5... | collective-permute-start | bytes 1572872 | tf_op jit(solution)/shard_map/ppermute | solution.py:360
  21.6 11.1 %collective-permute-start.1 = (f32[520,128]{1,0:T(8,128)S(1)}, f32[520,128]{1,0:T(8,128)S(1)}, u32[]{:S(2)}, u32[]{:S(2)}) collective-permute-start(f32[520,128]{1,0:T(8,128)S(1)} %get-tuple-element.38), channel_id=1, source_target_pairs={{0,24},{4,28},{8,16},{12,20},{16,8},{20,12},{24,0},{28,4},{1,25},{... | collective-permute-start | bytes 798728 | tf_op jit(solution)/shard_map/ppermute | solution.py:360
  25.5 12.7 %collective-permute-start.2 = (f32[520,128]{1,0:T(8,128)S(1)}, f32[520,128]{1,0:T(8,128)S(1)}, u32[]{:S(2)}, u32[]{:S(2)}) collective-permute-start(f32[520,128]{1,0:T(8,128)S(1)} %get-tuple-element.39), channel_id=1, source_target_pairs={{0,8},{4,12},{8,0},{12,4},{16,24},{20,28},{24,16},{28,20},{1,9},{5... | collective-permute-start | bytes 798728 | tf_op jit(solution)/shard_map/ppermute | solution.py:360
  26.0 12.2 %collective-permute-start.3 = (f32[520,128]{1,0:T(8,128)S(1)}, f32[520,128]{1,0:T(8,128)S(1)}, u32[]{:S(2)}, u32[]{:S(2)}) collective-permute-start(f32[520,128]{1,0:T(8,128)S(1)} %get-tuple-element.40), channel_id=1, source_target_pairs={{0,16},{4,20},{8,24},{12,28},{16,0},{20,4},{24,8},{28,12},{1,17},{... | collective-permute-start | bytes 798728 | tf_op jit(solution)/shard_map/ppermute | solution.py:360
  38.3 10.2 %collective-permute-start.7 = (f32[512,128]{1,0:T(8,128)S(1)}, f32[512,128]{1,0:T(8,128)S(1)}, u32[]{:S(2)}, u32[]{:S(2)}) collective-permute-start(f32[512,128]{1,0:T(8,128)S(1)} %get-tuple-element.47.piece_ref), channel_id=1, source_target_pairs={{0,24},{4,28},{8,16},{12,20},{16,8},{20,12},{24,0},{28,4},{1,25},{... | collective-permute-start | bytes 786440 | tf_op jit(solution)/shard_map/ppermute | solution.py:360
  40.7 12.4 %collective-permute-start.6 = (f32[512,128]{1,0:T(8,128)S(1)}, f32[512,128]{1,0:T(8,128)S(1)}, u32[]{:S(2)}, u32[]{:S(2)}) collective-permute-start(f32[512,128]{1,0:T(8,128)S(1)} %get-tuple-element.47.piece_ref), channel_id=1, source_target_pairs={{0,8},{4,12},{8,0},{12,4},{16,24},{20,28},{24,16},{28,20},{1,9},{5... | collective-permute-start | bytes 786440 | tf_op jit(solution)/shard_map/ppermute | solution.py:360
  41.2 12.6 %collective-permute-start.5 = (f32[512,128]{1,0:T(8,128)S(1)}, f32[512,128]{1,0:T(8,128)S(1)}, u32[]{:S(2)}, u32[]{:S(2)}) collective-permute-start(f32[512,128]{1,0:T(8,128)S(1)} %get-tuple-element.47.piece_ref), channel_id=1, source_target_pairs={{0,16},{4,20},{8,24},{12,28},{16,0},{20,4},{24,8},{28,12},{1,17},{... | collective-permute-start | bytes 786440 | tf_op jit(solution)/shard_map/ppermute | solution.py:360
  56.3 5.6 %collective-permute-start.9 = (f32[256,128]{1,0:T(8,128)S(1)}, f32[256,128]{1,0:T(8,128)S(1)}, u32[]{:S(2)}, u32[]{:S(2)}) collective-permute-start(f32[256,128]{1,0:T(8,128)S(1)} %slice.21), channel_id=1, source_target_pairs={{0,1},{1,0},{2,3},{3,2},{4,5},{5,4},{6,7},{7,6},{8,9},{9,8},{10,11... | collective-permute-start | bytes 393224 | tf_op jit(solution)/shard_map/ppermute | solution.py:360
  61.9 6.9 %collective-permute-start.10 = (f32[256,128]{1,0:T(8,128)S(1)}, f32[256,128]{1,0:T(8,128)S(1)}, u32[]{:S(2)}, u32[]{:S(2)}) collective-permute-start(f32[256,128]{1,0:T(8,128)S(1)} %slice_add_fusion), channel_id=1, source_target_pairs={{0,3},{1,2},{2,1},{3,0},{4,7},{5,6},{6,5},{7,4},{8,11},{9,10},{10,... | collective-permute-start | bytes 393224 | tf_op jit(solution)/shard_map/ppermute | solution.py:360
  68.8 5.3 %collective-permute-start.11 = (f32[256,128]{1,0:T(8,128)S(1)}, f32[256,128]{1,0:T(8,128)S(1)}, u32[]{:S(2)}, u32[]{:S(2)}) collective-permute-start(f32[256,128]{1,0:T(8,128)S(1)} %add.32), channel_id=1, source_target_pairs={{0,1},{1,0},{2,3},{3,2},{4,5},{5,4},{6,7},{7,6},{8,9},{9,8},{10,11... | collective-permute-start | bytes 393224 | tf_op jit(solution)/shard_map/ppermute | solution.py:360
  77.9 9.3 %collective-permute-start.14 = (f32[520,128]{1,0:T(8,128)S(1)}, f32[520,128]{1,0:T(8,128)S(1)}, u32[]{:S(2)}, u32[]{:S(2)}) collective-permute-start(f32[520,128]{1,0:T(8,128)S(1)} %shard_map.95), channel_id=1, source_target_pairs={{0,8},{4,12},{8,0},{12,4},{16,24},{20,28},{24,16},{28,20},{1,9},{5... | collective-permute-start | bytes 798728 | tf_op jit(solution)/shard_map/ppermute | solution.py:360
  79.5 13.9 %collective-permute-start.15 = (f32[520,128]{1,0:T(8,128)S(1)}, f32[520,128]{1,0:T(8,128)S(1)}, u32[]{:S(2)}, u32[]{:S(2)}) collective-permute-start(f32[520,128]{1,0:T(8,128)S(1)} %shard_map.96), channel_id=1, source_target_pairs={{0,16},{4,20},{8,24},{12,28},{16,0},{20,4},{24,8},{28,12},{1,17},{... | collective-permute-start | bytes 798728 | tf_op jit(solution)/shard_map/ppermute | solution.py:360
  80.1 13.2 %collective-permute-start.13 = (f32[520,128]{1,0:T(8,128)S(1)}, f32[520,128]{1,0:T(8,128)S(1)}, u32[]{:S(2)}, u32[]{:S(2)}) collective-permute-start(f32[520,128]{1,0:T(8,128)S(1)} %get-tuple-element.52), channel_id=1, source_target_pairs={{0,24},{4,28},{8,16},{12,20},{16,8},{20,12},{24,0},{28,4},{1,25},{... | collective-permute-start | bytes 798728 | tf_op jit(solution)/shard_map/ppermute | solution.py:360
  93.4 3.6 %collective-permute-start.19 = (f32[512,128]{1,0:T(8,128)S(1)}, f32[512,128]{1,0:T(8,128)S(1)}, u32[]{:S(2)}, u32[]{:S(2)}) collective-permute-start(f32[512,128]{1,0:T(8,128)S(1)} %get-tuple-element.54.refs_0_), channel_id=1, source_target_pairs={{0,4},{4,0},{8,12},{12,8},{16,20},{20,16},{24,28},{28,24},{1,5},{5... | collective-permute-start | bytes 786440 | tf_op jit(solution)/shard_map/ppermute | solution.py:360
  93.5 17.1 %collective-permute-start.18 = (f32[512,128]{1,0:T(8,128)S(1)}, f32[512,128]{1,0:T(8,128)S(1)}, u32[]{:S(2)}, u32[]{:S(2)}) collective-permute-start(f32[512,128]{1,0:T(8,128)S(1)} %get-tuple-element.54.refs_0_), channel_id=1, source_target_pairs={{0,24},{4,28},{8,16},{12,20},{16,8},{20,12},{24,0},{28,4},{1,25},{... | collective-permute-start | bytes 786440 | tf_op jit(solution)/shard_map/ppermute | solution.py:360
  94.7 17.9 %collective-permute-start.17 = (f32[512,128]{1,0:T(8,128)S(1)}, f32[512,128]{1,0:T(8,128)S(1)}, u32[]{:S(2)}, u32[]{:S(2)}) collective-permute-start(f32[512,128]{1,0:T(8,128)S(1)} %get-tuple-element.54.refs_0_), channel_id=1, source_target_pairs={{0,8},{4,12},{8,0},{12,4},{16,24},{20,28},{24,16},{28,20},{1,9},{5... | collective-permute-start | bytes 786440 | tf_op jit(solution)/shard_map/ppermute | solution.py:360
  95.7 19.4 %collective-permute-start.16 = (f32[512,128]{1,0:T(8,128)S(1)}, f32[512,128]{1,0:T(8,128)S(1)}, u32[]{:S(2)}, u32[]{:S(2)}) collective-permute-start(f32[512,128]{1,0:T(8,128)S(1)} %get-tuple-element.54.refs_0_), channel_id=1, source_target_pairs={{0,16},{4,20},{8,24},{12,28},{16,0},{20,4},{24,8},{28,12},{1,17},{... | collective-permute-start | bytes 786440 | tf_op jit(solution)/shard_map/ppermute | solution.py:360
  110.6 6.4 %collective-permute-start.22 = (f32[512,128]{1,0:T(8,128)S(1)}, f32[512,128]{1,0:T(8,128)S(1)}, u32[]{:S(2)}, u32[]{:S(2)}) collective-permute-start(f32[512,128]{1,0:T(8,128)S(1)} %collective-permute-done.18.refs_0_), channel_id=1, source_target_pairs={{0,4},{4,0},{8,12},{12,8},{16,20},{20,16},{24,28},{28,24},{1,5},{5... | collective-permute-start | bytes 786440 | tf_op jit(solution)/shard_map/ppermute | solution.py:360
  112.6 6.3 %collective-permute-start.21 = (f32[512,128]{1,0:T(8,128)S(1)}, f32[512,128]{1,0:T(8,128)S(1)}, u32[]{:S(2)}, u32[]{:S(2)}) collective-permute-start(f32[512,128]{1,0:T(8,128)S(1)} %collective-permute-done.17.refs_0_), channel_id=1, source_target_pairs={{0,4},{4,0},{8,12},{12,8},{16,20},{20,16},{24,28},{28,24},{1,5},{5... | collective-permute-start | bytes 786440 | tf_op jit(solution)/shard_map/ppermute | solution.py:360
  115.1 6.0 %collective-permute-start.20 = (f32[512,128]{1,0:T(8,128)S(1)}, f32[512,128]{1,0:T(8,128)S(1)}, u32[]{:S(2)}, u32[]{:S(2)}) collective-permute-start(f32[512,128]{1,0:T(8,128)S(1)} %collective-permute-done.16.refs_0_), channel_id=1, source_target_pairs={{0,4},{4,0},{8,12},{12,8},{16,20},{20,16},{24,28},{28,24},{1,5},{5... | collective-permute-start | bytes 786440 | tf_op jit(solution)/shard_map/ppermute | solution.py:360
  123.2 14.7 %collective-permute-start.23 = (f32[1024,128]{1,0:T(8,128)S(1)}, f32[1024,128]{1,0:T(8,128)S(1)}, u32[]{:S(2)}, u32[]{:S(2)}) collective-permute-start(f32[1024,128]{1,0:T(8,128)S(1)} %get-tuple-element.62), channel_id=1, source_target_pairs={{0,1},{1,0},{2,3},{3,2},{4,5},{5,4},{6,7},{7,6},{8,9},{9,8},{10,11... | collective-permute-start | bytes 1572872 | tf_op jit(solution)/shard_map/ppermute | solution.py:360
  137.9 15.7 %collective-permute-start.24 = (f32[1024,128]{1,0:T(8,128)S(1)}, f32[1024,128]{1,0:T(8,128)S(1)}, u32[]{:S(2)}, u32[]{:S(2)}) collective-permute-start(f32[1024,128]{1,0:T(8,128)S(1)} %add.35), channel_id=1, source_target_pairs={{0,3},{1,2},{2,1},{3,0},{4,7},{5,6},{6,5},{7,4},{8,11},{9,10},{10,... | collective-permute-start | bytes 1572872 | tf_op jit(solution)/shard_map/ppermute | solution.py:360
  154.4 12.6 %collective-permute-start.26 = (f32[8,128]{1,0:T(8,128)S(1)}, f32[8,128]{1,0:T(8,128)S(1)}, u32[]{:S(2)}, u32[]{:S(2)}) collective-permute-start(f32[8,128]{1,0:T(8,128)S(1)} %get-tuple-element.64), channel_id=1, source_target_pairs={{0,1},{1,0},{2,3},{3,2},{4,5},{5,4},{6,7},{7,6},{8,9},{9,8},{10,11... | collective-permute-start | bytes 12296 | tf_op jit(solution)/shard_map/ppermute | solution.py:360
  165.4 12.8 %collective-permute-start.25 = (f32[1024,128]{1,0:T(8,128)S(1)}, f32[1024,128]{1,0:T(8,128)S(1)}, u32[]{:S(2)}, u32[]{:S(2)}) collective-permute-start(f32[1024,128]{1,0:T(8,128)S(1)} %get-tuple-element.63.refs_0_), channel_id=1, source_target_pairs={{0,1},{1,0},{2,3},{3,2},{4,5},{5,4},{6,7},{7,6},{8,9},{9,8},{10,11... | collective-permute-start | bytes 1572872 | tf_op jit(solution)/shard_map/ppermute | solution.py:360
  (11 other events, 165.5 us)

commit v3 on v2

--- a/solution.py
+++ b/solution.py
@@ -9,6 +9,7 @@
 
 ridge_weight = 0.02
 PAD = 8
+SHARES = (1, 3)
 f32, bf16 = jnp.float32, jnp.bfloat16
 FIRST = (((0,), (0,)), ((), ()))
 LAST = (((1,), (1,)), ((), ()))
@@ -55,54 +56,103 @@
     return pl.BlockSpec(shape, lambda *_: (0,) * len(shape))
 
 
+def here(n_cols):
+    row, col = lax.axis_index("rows"), lax.axis_index("cols")
+    steps = n_cols.bit_length() - 1
+    segment = 0
+    for s in range(steps - 1):
+        bit = ((col >> s) ^ (col >> (s + 1))) & 1
+        segment = segment | (bit << (steps - 2 - s))
+    return row >> 1, row & 1, segment
+
+
+def cuts(rows):
+    ends = [rows * sum(SHARES[: i + 1]) // sum(SHARES) for i in range(len(SHARES))]
+    return list(zip([0, *ends], ends))
+
+
 def resident(x):
     return pltpu.with_memory_space_constraint(x, pltpu.VMEM)
 
 
-def forward_kernel(place, l_ref, d_ref, r_ref, keep_ref, send_ref, pairs, norms):
-    @pl.when(pl.program_id(0) == 0)
-    def _():
-        d, r = d_ref[...], r_ref[...]
-        pairs[...] = pair(d)
-        norms[...] = jnp.zeros_like(norms)
-        norms[0:1, :] = jnp.sum(r * r, axis=0, keepdims=True)
-        norms[1:2, :] = jnp.sum(d * d, axis=0, keepdims=True)
-
-    m = l_ref.shape[0] // 2
-    core = place[1]
-    for out_ref, side in ((keep_ref, core), (send_ref, 1 - core)):
-        rows = l_ref[pl.ds(pl.multiple_of(side * m, m), m), :]
-        out_ref[0, :m, :] = wide(rows, pairs[...])
-        out_ref[0, m:, :] = norms[...]
-
-
-def forward(place, inv_factor, direction, residual, chips):
+def forward_kernel(chips, slots, l_ref, d_ref, r_ref, keep_ref, send_ref, buffer, arrived, d, r, pairs, sems):
+    m = buffer.shape[1]
+    jobs = 2 * chips
+    chip, core, _ = here(2)
+
+    def copy(t, side):
+        n = 2 * t + side
+        start = pl.multiple_of(((chip ^ t) * 2 + (core ^ side)) * m, m)
+        slot = lax.rem(n, slots)
+        return pltpu.make_async_copy(l_ref.at[pl.ds(start, m), :], buffer.at[slot], arrived.at[slot])
+
+    copy_d = pltpu.make_async_copy(d_ref, d, sems.at[0])
+    copy_r = pltpu.make_async_copy(r_ref, r, sems.at[1])
+    copy_d.start()
+    for n in range(min(slots - 1, jobs)):
+        copy(n // 2, n % 2).start()
+    copy_r.start()
+    copy_d.wait()
+    pairs[...] = pair(d[...])
+
+    def step(n, carry):
+        ahead = n + slots - 1
+
+        @pl.when(ahead < jobs)
+        def _():
+            copy(ahead >> 1, ahead & 1).start()
+
+        copy(n >> 1, n & 1).wait()
+        value = wide(buffer[lax.rem(n, slots)], pairs[...])
+
+        @pl.when(n & 1 == 0)
+        def _():
+            keep_ref[n >> 1, :m, :] = value
+
+        @pl.when(n & 1 == 1)
+        def _():
+            send_ref[n >> 1, :m, :] = value
+
+        return carry
+
+    lax.fori_loop(0, jobs, step, 0)
+    copy_r.wait()
+    norm_now = jnp.sum(r[...] * r[...], axis=0, keepdims=True)
+    dir_norm = jnp.sum(d[...] * d[...], axis=0, keepdims=True)
+    for ref in (keep_ref, send_ref):
+        for t in range(chips):
+            ref[t, m:, :] = jnp.zeros((PAD, d.shape[1]), f32)
+            ref[t, m : m + 1, :] = norm_now
+            ref[t, m + 1 : m + 2, :] = dir_norm
+
+
+def forward(inv_factor, direction, residual, chips):
     n, depth = inv_factor.shape
     t = direction.shape[1]
     m = n // chips // 2
     out = jax.ShapeDtypeStruct((chips, m + PAD, t), f32)
-    block = pl.BlockSpec((1, m + PAD, t), lambda i, s: (i, 0, 0))
-    return pl.pallas_call(
-        forward_kernel,
-        grid_spec=pltpu.PrefetchScalarGridSpec(
-            num_scalar_prefetch=1,
-            grid=(chips,),
-            in_specs=[
-                pl.BlockSpec((2 * m, depth), lambda i, s: (s[0] ^ i, 0)),
-                whole((depth, t)),
-                whole((depth, t)),
-            ],
-            out_specs=(block, block),
-            scratch_shapes=[pltpu.VMEM((depth, 2 * t), bf16), pltpu.VMEM((PAD, t), f32)],
-        ),
+    slots = 3
+    far = pl.BlockSpec(memory_space=pl.ANY)
+    return pl.pallas_call(
+        functools.partial(forward_kernel, chips, slots),
+        in_specs=[far] * 3,
+        out_specs=(local, local),
         out_shape=(out, out),
+        scratch_shapes=[
+            pltpu.VMEM((slots, m, depth), f32),
+            pltpu.SemaphoreType.DMA((slots,)),
+            pltpu.VMEM((depth, t), f32),
+            pltpu.VMEM((depth, t), f32),
+            pltpu.VMEM((depth, 2 * t), bf16),
+            pltpu.SemaphoreType.DMA((2,)),
+        ],
         compiler_params=params(40),
-        cost_estimate=cost(8 * n * depth * t, 4 * n * depth),
-    )(place, inv_factor, direction, residual)
-
-
-def add_kernel(n_terms, *refs):
-    terms, outs = refs[:n_terms], refs[n_terms:]
+        cost_estimate=cost(),
+    )(*[pltpu.with_memory_space_constraint(x, pltpu.HBM) for x in (inv_factor, direction, residual)])
+
+
+def add_kernel(n_terms, n_held, *refs):
+    terms, outs = refs[:n_terms], refs[n_terms + n_held :]
     if len(outs) > 1 and len(terms[0].shape) == 3:
         for i, out in enumerate(outs):
             out[...] = terms[0][i] + terms[1][i]
@@ -116,16 +166,16 @@
         start += out.shape[0]
 
 
-def add(terms, shapes):
+def add(terms, shapes, held=()):
     out = tuple(jax.ShapeDtypeStruct(shape, f32) for shape in shapes)
     return pl.pallas_call(
-        functools.partial(add_kernel, len(terms)),
-        in_specs=[local] * len(terms),
+        functools.partial(add_kernel, len(terms), len(held)),
+        in_specs=[local] * (len(terms) + len(held)),
         out_specs=(local,) * len(out),
         out_shape=out,
         compiler_params=params(),
         cost_estimate=cost(),
-    )(*terms)
+    )(*terms, *map(resident, held))
 
 
 def kernel_kernel(segments, place, own_ref, other_ref, c_ref, high_ref, low_ref, ph, plo, psq):
@@ -211,6 +261,7 @@
 
 
 def back_kernel(shift, first, high_ref, low_ref, *refs):
+    refs = refs[1:] if shift == 0 else refs
     if first:
         own_ref, other_ref, out_ref, pairs, norms = refs
         half = own_ref.shape[0]
@@ -229,7 +280,7 @@
     out_ref[m:, :] = norms[...]
 
 
-def back_product(shift, high, low, sources, first):
+def back_product(shift, high, low, sources, first, held=()):
     _, m, n = high.shape
     t = sources[1].shape[1]
     out = (jax.ShapeDtypeStruct((m + PAD, t), f32),)
@@ -237,15 +288,16 @@
         out += (jax.ShapeDtypeStruct((n, 2 * t), bf16), jax.ShapeDtypeStruct((PAD, t), f32))
     return pl.pallas_call(
         functools.partial(back_kernel, shift, first),
-        in_specs=[local] * 4,
+        in_specs=[local] * (4 + len(held)),
         out_specs=(local,) * len(out),
         out_shape=out,
         compiler_params=params(),
         cost_estimate=cost(8 * m * n * t, 4 * m * n),
-    )(resident(high), resident(low), *sources)
-
-
-def transposed_kernel(shift, sides, first, segments, place, l_ref, *refs):
+    )(resident(high), resident(low), *map(resident, held), *sources)
+
+
+def transposed_kernel(shift, sides, first, segments, l_ref, *refs):
+    place = here(2 * segments)
     pieces, refs = refs[: len(sides)], refs[len(sides) :]
     value = None if first else refs[0][...]
     block = place[0] ^ shift
@@ -261,91 +313,103 @@
     if segments == 0:
         refs[-1][...] = value
         return
-    keep_ref, send_ref, image = refs[-3:]
+    *outs, image = refs[-2 * len(SHARES) - 1 :]
     image[...] = value.T
     seg = image.shape[0] // segments
     half = segments // 2
     for u in range(segments):
-        ref = keep_ref if u < half else send_ref
-        at = pl.ds(pl.multiple_of((place[2] ^ u) * seg, seg), seg)
-        ref[(u % half) * seg : (u % half + 1) * seg, :] = image[at, :]
-
-
-def transposed(shift, sides, place, inv_factor, pieces, acc, segments=0):
+        for c, (begin, end) in enumerate(cuts(seg)):
+            ref = outs[2 * c + (u >= half)]
+            at = pl.ds(pl.multiple_of((place[2] ^ u) * seg + begin, PAD), end - begin)
+            start = (u % half) * (end - begin)
+            ref[start : start + end - begin, :] = image[at, :]
+
+
+def transposed(shift, sides, inv_factor, pieces, acc, segments=0):
     depth = inv_factor.shape[1]
     m, t = pieces[0].shape
     args = [resident(inv_factor), *pieces] + ([] if acc is None else [acc])
     scratch = []
     if segments:
-        out = (jax.ShapeDtypeStruct((depth // 2, t), f32),) * 2
+        seg = depth // segments
+        out = tuple(
+            jax.ShapeDtypeStruct((segments // 2 * (end - begin), t), f32)
+            for begin, end in cuts(seg)
+            for _ in range(2)
+        )
         scratch = [pltpu.VMEM((depth, t), f32)]
     else:
         out = jax.ShapeDtypeStruct((t, depth), f32)
     return pl.pallas_call(
         functools.partial(transposed_kernel, shift, sides, acc is None, segments),
-        in_specs=[scalars] + [local] * len(args),
-        out_specs=(local,) * 2 if segments else local,
+        in_specs=[local] * len(args),
+        out_specs=(local,) * len(out) if segments else local,
         out_shape=out,
         scratch_shapes=scratch,
         compiler_params=params(),
         cost_estimate=cost(),
-    )(place, *args)
-
-
-def update_kernel(place, image_ref, r_ref, d_ref, pred_ref, norm_ref, new_ref, sum_ref):
+    )(*args)
+
+
+def update_kernel(begin, rows, segments, image_ref, r_ref, d_ref, pred_ref, norm_ref, *refs):
+    new_ref, sum_ref = refs[-2:]
     norm_now, dir_norm = norm_ref[0:1, :], norm_ref[1:2, :]
     curvature = pred_ref[0:1, :] + ridge_weight * dir_norm
     step = norm_now / curvature
-    new = r_ref[...] - step * (image_ref[...] + ridge_weight * d_ref[...])
+    start = here(2 * segments)[2] * rows + begin
+    at = pl.ds(pl.multiple_of(start, PAD), image_ref.shape[0])
+    new = r_ref[at, :] - step * (image_ref[...] + ridge_weight * d_ref[at, :])
     new_ref[...] = new
-    sum_ref[...] = jnp.broadcast_to(jnp.sum(new * new, axis=0, keepdims=True), sum_ref.shape)
-
-
-def update(place, image, residual, direction, pred_norm, norms, segments):
-    seg, t = image.shape
-    at = pl.BlockSpec((seg, t), lambda i, s: (s[2], 0))
-    return pl.pallas_call(
-        update_kernel,
-        grid_spec=pltpu.PrefetchScalarGridSpec(
-            num_scalar_prefetch=1,
-            grid=(1,),
-            in_specs=[whole((seg, t)), at, at, whole(pred_norm.shape), whole(norms.shape)],
-            out_specs=(whole((seg, t)), whole((PAD, t))),
-        ),
-        out_shape=(jax.ShapeDtypeStruct((seg, t), f32), jax.ShapeDtypeStruct((PAD, t), f32)),
-        compiler_params=params(),
-    )(place, image, residual, direction, pred_norm, norms)
-
-
-def finish_kernel(n_pieces, place, *refs):
+    total = jnp.broadcast_to(jnp.sum(new * new, axis=0, keepdims=True), sum_ref.shape)
+    if len(refs) == 3:
+        total += refs[0][...]
+    sum_ref[...] = total
+
+
+def update(begin, image, residual, direction, pred_norm, norms, before, segments):
+    rows = residual.shape[0] // segments
+    args = [image, residual, direction, pred_norm, norms] + ([] if before is None else [before])
+    out = (jax.ShapeDtypeStruct(image.shape, f32), jax.ShapeDtypeStruct(norms.shape, f32))
+    return pl.pallas_call(
+        functools.partial(update_kernel, begin, rows, segments),
+        in_specs=[local] * len(args),
+        out_specs=(local, local),
+        out_shape=out,
+        compiler_params=params(),
+        cost_estimate=cost(),
+    )(*args)
+
+
+def finish_kernel(segments, n_pieces, *refs):
     pieces = refs[:n_pieces]
     d_ref, norm_ref, next_ref, res_ref, dir_ref = refs[n_pieces:]
     ratio = next_ref[0:1, :] / norm_ref[0:1, :]
-    seg = pieces[0].shape[0]
-    u = 0
-    for piece in pieces:
-        for j in range(piece.shape[0] // seg):
-            at = pl.ds(pl.multiple_of((place[2] ^ u) * seg, seg), seg)
-            new = piece[j * seg : (j + 1) * seg, :]
-            res_ref[at, :] = new
-            dir_ref[at, :] = new + ratio * d_ref[at, :]
-            u += 1
-
-
-def finish(place, pieces, direction, norms, norm_next):
+    segment = here(2 * segments)[2]
+    seg = d_ref.shape[0] // segments
+    each = n_pieces // len(SHARES)
+    for c, (begin, end) in enumerate(cuts(seg)):
+        n = end - begin
+        u = 0
+        for piece in pieces[c * each : (c + 1) * each]:
+            for j in range(piece.shape[0] // n):
+                at = pl.ds(pl.multiple_of((segment ^ u) * seg + begin, PAD), n)
+                new = piece[j * n : (j + 1) * n, :]
+                res_ref[at, :] = new
+                dir_ref[at, :] = new + ratio * d_ref[at, :]
+                u += 1
+
+
+def finish(pieces, direction, norms, norm_next, segments):
     out = jax.ShapeDtypeStruct(direction.shape, f32)
     args = [*pieces, direction, norms, norm_next]
     return pl.pallas_call(
-        functools.partial(finish_kernel, len(pieces)),
-        grid_spec=pltpu.PrefetchScalarGridSpec(
-            num_scalar_prefetch=1,
-            grid=(1,),
-            in_specs=[whole(a.shape) for a in args],
-            out_specs=(whole(direction.shape),) * 2,
-        ),
+        functools.partial(finish_kernel, segments, len(pieces)),
+        in_specs=[local] * len(args),
+        out_specs=(local, local),
         out_shape=(out, out),
         compiler_params=params(),
-    )(place, *args)
+        cost_estimate=cost(),
+    )(*args)
 
 
 def body(n_rows, n_cols, points, centers, inv_factor, solution, residual, direction):
@@ -359,16 +423,11 @@
         size = n_rows if axis == "rows" else n_cols
         return lax.ppermute(x, axis, [(i, i ^ mask) for i in range(size)])
 
-    row, col = lax.axis_index("rows"), lax.axis_index("cols")
-    segment = 0
-    for s in range(steps - 1):
-        bit = ((col >> s) ^ (col >> (s + 1))) & 1
-        segment = segment | (bit << (steps - 2 - s))
-    place = jnp.stack([row // 2, row % 2, segment]).astype(jnp.int32)
+    place = jnp.stack(here(n_cols)).astype(jnp.int32)
     order = [chips - 1, *range(1, chips - 1)]
 
     other_points = swap(points, "rows", 1)
-    keep, send = forward(place, inv_factor, direction, residual, chips)
+    keep, send = forward(inv_factor, direction, residual, chips)
     m, t = keep.shape[1] - PAD, keep.shape[2]
     totals = add([keep, swap(send, "rows", 1)], [(m + PAD, t)] * chips)
     got = [swap(totals[i], "rows", 2 * i) for i in order]
@@ -393,41 +452,54 @@
     got = []
     sources, first = (part, other), True
     for shift in (*order, 0):
-        piece, *rest = back_product(shift, high, low, sources, first)
+        piece, *rest = back_product(
+            shift, high, low, sources, first, () if shift else (inv_factor,)
+        )
         if first:
             sources, first = rest, False
         got.append(swap(piece, "rows", 2 * shift) if shift else piece)
-    own, pred_norm = add([got[-1], *got[:-1]], [(m, t), (PAD, t)])
+    own, pred_norm = add([got[-1], *got[:-1]], [(m, t), (PAD, t)], (inv_factor,))
 
     arrived = [(i, swap(own, "rows", 2 * i)) for i in order]
-    acc = transposed(0, (0, 1), place, inv_factor, [own, swap(own, "rows", 1)], None)
-    others = []
+    acc = transposed(0, (0, 1), inv_factor, [own, swap(own, "rows", 1)], None)
+    late = []
     for shift, piece in arrived:
         piece, acc = lax.optimization_barrier((piece, acc))
-        others.append((shift, swap(piece, "rows", 1)))
-        acc = transposed(shift, (0,), place, inv_factor, [piece], acc)
-    for j, (shift, piece) in enumerate(others):
-        last = j == chips - 2
-        acc = transposed(shift, (1,), place, inv_factor, [piece], acc, segments if last else 0)
-    keep, send = acc
-    image = keep + swap(send, "cols", masks[0])
-    for mask in halving[1:]:
-        half = image.shape[0] // 2
-        image = image[:half] + swap(image[half:], "cols", mask)
-    image = image + swap(image, "cols", last_mask)
-    new_piece, norm_next = update(place, image, residual, direction, pred_norm, norms, segments)
-    pieces = [new_piece]
-    gathered = new_piece
-    for mask in halving[::-1]:
-        got = swap(gathered, "cols", mask)
-        pieces.append(got)
-        gathered = jnp.concatenate([gathered, got], axis=0)
+        other = swap(piece, "rows", 1)
+        acc = transposed(shift, (0,), inv_factor, [piece], acc)
+        late.append((shift, other))
+    for shift, other in late:
+        last = shift == late[-1][0]
+        acc = transposed(shift, (1,), inv_factor, [other], acc, segments if last else 0)
+    pieces, norm_next, step_one, step_two, done = [], None, (), (), ()
+    for c, (begin, _) in enumerate(cuts(residual.shape[0] // segments)):
+        image, send = acc[2 * c : 2 * c + 2]
+        send, step_one = lax.optimization_barrier((send, step_one))
+        step_one = swap(send, "cols", masks[0])
+        image = image + step_one
+        for mask in halving[1:]:
+            half = image.shape[0] // 2
+            image = image[:half] + swap(image[half:], "cols", mask)
+        image, step_two = lax.optimization_barrier((image, step_two))
+        step_two = swap(image, "cols", last_mask)
+        image = image + step_two
+        image, done = lax.optimization_barrier((image, done))
+        new, norm_next = update(
+            begin, image, residual, direction, pred_norm, norms, norm_next, segments
+        )
+        pieces.append(new)
+        for mask in halving[::-1]:
+            done = swap(new, "cols", mask)
+            pieces.append(done)
+            new = jnp.concatenate([new, done], axis=0)
     for mask in halving[::-1]:
         norm_next = norm_next + swap(norm_next, "cols", mask)
     norm_next = jnp.sum(lax.all_gather(norm_next, "rows"), axis=0)
     step = norms[0:1] / (pred_norm[0:1] + ridge_weight * norms[1:2])
     new_solution = solution + step * direction
-    new_residual, new_direction = finish(place, pieces, direction, norms, norm_next)
+    new_residual, new_direction = finish(
+        pieces, direction, norms, norm_next, segments
+    )
     return new_solution, new_residual, new_direction
 
 

time: 181 us -> 161 us (0.89)
  waiting for transfers between devices: 70.4 us -> 62.8 us
  Pallas kernels: 45.6 us -> 38.5 us
  starting transfers between devices: 40.7 us -> 35.7 us
    ppermute x27 -> x30, waiting for transfers between devices: 70.4 us -> 62.8 us  [swap(): return lax.ppermute(x, axis, [(i, i ^ mask) for i in range(size)])]
    ppermute x27 -> x30, starting transfers between devices: 40.7 us -> 35.7 us  [swap(): return lax.ppermute(x, axis, [(i, i ^ mask) for i in range(size)])]
    pallas_call x7, Pallas kernels: 14.7 us -> 10.7 us  [transposed(): pl.pallas_call(functools.partial(transposed_kernel, shift, sides, acc is...]
    pallas_call x6 -> x7, Pallas kernels: 18.5 us -> 15.6 us  [the longest x1 13.6 us: forward(): pl.pallas_call(functools.partial(forward_kernel, chips, slots), in_specs=...]
    unnamed x16 -> x12, local copies, waits for them, and re-layouts: 13 us -> 12.8 us
  transfers between devices with their start and end apart: 27 -> 30, of which waited for: 16 -> 18; matrix products, arithmetic and copies ran while one was open for 1% -> 1% of each run, Pallas kernels for 12% -> 12%
where the time goes in v3:
time: 161 us
  waiting for transfers between devices  62.8 us (39%)
  Pallas kernels  38.5 us (24%)
  starting transfers between devices  35.7 us (22%)
  local copies, waits for them, and re-layouts  12.8 us (8%)
  blocking collectives  9.09 us (6%)
    ppermute x30, waiting for transfers between devices, swap(): return lax.ppermute(x, axis, [(i, i ^ mask) for i in range(size)])  62.8 us
    ppermute x30, starting transfers between devices, swap(): return lax.ppermute(x, axis, [(i, i ^ mask) for i in range(size)])  35.7 us
    pallas_call x1, Pallas kernels, forward(): pl.pallas_call(functools.partial(forward_kernel, chips, slots), in_specs=...  13.6 us
    unnamed x12, local copies, waits for them, and re-layouts  12.8 us
    pallas_call x7, Pallas kernels, transposed(): pl.pallas_call(functools.partial(transposed_kernel, shift, sides, acc is...  10.7 us
    all_gather x1, blocking collectives, body(): norm_next = jnp.sum(lax.all_gather(norm_next, 'rows'), axis=0)  9.09 us
    pallas_call x1, Pallas kernels, gaussian(): pl.pallas_call(functools.partial(kernel_kernel, segments), grid_spec=pltp...  6.41 us
  transfers between devices with their start and end apart: 30, of which 18 were waited for; matrix products, arithmetic and copies ran while one was open for 1% of the time, Pallas kernels for 12%

profile of v3, /device:TPU:0, one launch (start us, length us, event | category | flops | bytes accessed | tf_op | source)
XLA Modules:
  0.0 161.3 jit_solution(6976058809985484075)
XLA Ops:
  0.6 13.6 %shard_map.85 = (f32[4,520,128]{2,1,0:T(8,128)S(1)}, f32[4,520,128]{2,1,0:T(8,128)S(1)}) custom-call(f32[4096,2048]{1,0:T(8,128)} %l_ref.15, f32[2048,128]{1,0:T(8,128)} %refs_4_.3, f32[2048,128]{1,0:T(8,128)} %r_ref.5), custom_call_target="tpu_custom_call" | custom-call | flops 1 | bytes 1 | tf_op jit(solution)/shard_map/pallas_call | solution.py:136
  14.8 2.2 %collective-permute-done.refs_1_ = f32[4,520,128]{2,1,0:T(8,128)S(1)} collective-permute-done((f32[4,520,128]{2,1,0:T(8,128)S(1)}, f32[4,520,128]{2,1,0:T(8,128)S(1)}, u32[]{:S(2)}, u32[]{:S(2)}) %collective-permute-start) | collective-permute-done | bytes 1064992 | tf_op jit(solution)/shard_map/ppermute | solution.py:424
  17.2 3.9 %collective-permute-start.1 = (f32[520,128]{1,0:T(8,128)S(1)}, f32[520,128]{1,0:T(8,128)S(1)}, u32[]{:S(2)}, u32[]{:S(2)}) collective-permute-start(f32[520,128]{1,0:T(8,128)S(1)} %get-tuple-element.45), channel_id=1, source_target_pairs={{0,24},{4,28},{8,16},{12,20},{16,8},{20,12},{24,0},{28,4},{1,25},{... | collective-permute-start | bytes 798728 | tf_op jit(solution)/shard_map/ppermute | solution.py:424
  24.0 6.4 %shard_map.88 = (bf16[4,512,1024]{2,1,0:T(8,128)(2,1)S(1)}, bf16[4,512,1024]{2,1,0:T(8,128)(2,1)S(1)}) custom-call(s32[3]{0:T(128)S(1)} %pad_add_fusion.place, f32[512,256]{1,0:T(8,128)S(1)} %copy-done.4, f32[512,256]{1,0:T(8,128)S(1)} %collective-permute-done.4.other_ref, f32[4096,256]{1,0:T(8,128)S(1)} %copy-done.3), custom_call_target="tpu_custom_call" | custom-call | flops 1 | bytes 1 | tf_op jit(solution)/shard_map/pallas_call | solution.py:209
  30.4 3.4 %collective-permute-done.2.refs_2_ = f32[520,128]{1,0:T(8,128)S(1)} collective-permute-done((f32[520,128]{1,0:T(8,128)S(1)}, f32[520,128]{1,0:T(8,128)S(1)}, u32[]{:S(2)}, u32[]{:S(2)}) %collective-permute-start.2) | collective-permute-done | bytes 266272 | tf_op jit(solution)/shard_map/ppermute | solution.py:424
  33.9 2.4 %collective-permute-start.7 = (f32[512,128]{1,0:T(8,128)S(1)}, f32[512,128]{1,0:T(8,128)S(1)}, u32[]{:S(2)}, u32[]{:S(2)}) collective-permute-start(f32[512,128]{1,0:T(8,128)S(1)} %get-tuple-element.54.piece_ref), channel_id=1, source_target_pairs={{0,24},{4,28},{8,16},{12,20},{16,8},{20,12},{24,0},{28,4},{1,25},{... | collective-permute-start | bytes 786440 | tf_op jit(solution)/shard_map/ppermute | solution.py:424
  38.2 5.9 %collective-permute-done.7.piece_ref = f32[512,128]{1,0:T(8,128)S(1)} collective-permute-done((f32[512,128]{1,0:T(8,128)S(1)}, f32[512,128]{1,0:T(8,128)S(1)}, u32[]{:S(2)}, u32[]{:S(2)}) %collective-permute-start.7) | collective-permute-done | bytes 262176 | tf_op jit(solution)/shard_map/ppermute | solution.py:424
  44.8 3.8 %collective-permute-done.6.piece_ref = f32[512,128]{1,0:T(8,128)S(1)} collective-permute-done((f32[512,128]{1,0:T(8,128)S(1)}, f32[512,128]{1,0:T(8,128)S(1)}, u32[]{:S(2)}, u32[]{:S(2)}) %collective-permute-start.6) | collective-permute-done | bytes 262176 | tf_op jit(solution)/shard_map/ppermute | solution.py:424
  53.5 4.0 %collective-permute-done.9 = f32[256,128]{1,0:T(8,128)S(1)} collective-permute-done((f32[256,128]{1,0:T(8,128)S(1)}, f32[256,128]{1,0:T(8,128)S(1)}, u32[]{:S(2)}, u32[]{:S(2)}) %collective-permute-start.9) | collective-permute-done | bytes 131104 | tf_op jit(solution)/shard_map/ppermute | solution.py:424
  57.5 3.7 %collective-permute-start.10 = (f32[256,128]{1,0:T(8,128)S(1)}, f32[256,128]{1,0:T(8,128)S(1)}, u32[]{:S(2)}, u32[]{:S(2)}) collective-permute-start(f32[256,128]{1,0:T(8,128)S(1)} %slice_add_fusion), channel_id=1, source_target_pairs={{0,3},{1,2},{2,1},{3,0},{4,7},{5,6},{6,5},{7,4},{8,11},{9,10},{10,... | collective-permute-start | bytes 393224 | tf_op jit(solution)/shard_map/ppermute | solution.py:424
  61.2 3.2 %collective-permute-done.10 = f32[256,128]{1,0:T(8,128)S(1)} collective-permute-done((f32[256,128]{1,0:T(8,128)S(1)}, f32[256,128]{1,0:T(8,128)S(1)}, u32[]{:S(2)}, u32[]{:S(2)}) %collective-permute-start.10) | collective-permute-done | bytes 131104 | tf_op jit(solution)/shard_map/ppermute | solution.py:424
  64.5 2.3 %collective-permute-start.11 = (f32[256,128]{1,0:T(8,128)S(1)}, f32[256,128]{1,0:T(8,128)S(1)}, u32[]{:S(2)}, u32[]{:S(2)}) collective-permute-start(f32[256,128]{1,0:T(8,128)S(1)} %add.32), channel_id=1, source_target_pairs={{0,1},{1,0},{2,3},{3,2},{4,5},{5,4},{6,7},{7,6},{8,9},{9,8},{10,11... | collective-permute-start | bytes 393224 | tf_op jit(solution)/shard_map/ppermute | solution.py:424
  66.8 2.9 %collective-permute-done.11 = f32[256,128]{1,0:T(8,128)S(1)} collective-permute-done((f32[256,128]{1,0:T(8,128)S(1)}, f32[256,128]{1,0:T(8,128)S(1)}, u32[]{:S(2)}, u32[]{:S(2)}) %collective-permute-start.11) | collective-permute-done | bytes 131104 | tf_op jit(solution)/shard_map/ppermute | solution.py:424
  77.0 10.5 %copy-done = f32[4096,2048]{1,0:T(8,128)S(1)} copy-done((f32[4096,2048]{1,0:T(8,128)S(1)}, f32[4096,2048]{1,0:T(8,128)}, u32[]{:S(2)}) %copy-start) | copy-done | bytes 33554456
  92.6 2.4 %shard_map.98.refs_1_ = f32[128,2048]{1,0:T(8,128)S(1)} custom-call(f32[4096,2048]{1,0:T(8,128)S(1)} %copy-done, f32[512,128]{1,0:T(8,128)S(1)} %get-tuple-element.61.refs_0_, f32[512,128]{1,0:T(8,128)S(1)} %collective-permute-done.19.refs_1_), custom_call_target="tpu_custom_call" | custom-call | flops 1 | bytes 1 | tf_op jit(solution)/shard_map/pallas_call | solution.py:343
  95.0 4.1 %collective-permute-done.18.refs_0_ = f32[512,128]{1,0:T(8,128)S(1)} collective-permute-done((f32[512,128]{1,0:T(8,128)S(1)}, f32[512,128]{1,0:T(8,128)S(1)}, u32[]{:S(2)}, u32[]{:S(2)}) %collective-permute-start.18) | collective-permute-done | bytes 262176 | tf_op jit(solution)/shard_map/ppermute | solution.py:424
  100.5 3.0 %collective-permute-done.17.refs_0_ = f32[512,128]{1,0:T(8,128)S(1)} collective-permute-done((f32[512,128]{1,0:T(8,128)S(1)}, f32[512,128]{1,0:T(8,128)S(1)}, u32[]{:S(2)}, u32[]{:S(2)}) %collective-permute-start.17) | collective-permute-done | bytes 262176 | tf_op jit(solution)/shard_map/ppermute | solution.py:424
  113.3 3.7 %collective-permute-done.23 = f32[256,128]{1,0:T(8,128)S(1)} collective-permute-done((f32[256,128]{1,0:T(8,128)S(1)}, f32[256,128]{1,0:T(8,128)S(1)}, u32[]{:S(2)}, u32[]{:S(2)}) %collective-permute-start.23) | collective-permute-done | bytes 131104 | tf_op jit(solution)/shard_map/ppermute | solution.py:424
  118.8 2.8 %collective-permute-start.24 = (f32[256,128]{1,0:T(8,128)S(1)}, f32[256,128]{1,0:T(8,128)S(1)}, u32[]{:S(2)}, u32[]{:S(2)}) collective-permute-start(f32[256,128]{1,0:T(8,128)S(1)} %add.35), channel_id=1, source_target_pairs={{0,3},{1,2},{2,1},{3,0},{4,7},{5,6},{6,5},{7,4},{8,11},{9,10},{10,... | collective-permute-start | bytes 393224 | tf_op jit(solution)/shard_map/ppermute | solution.py:424
  121.5 6.3 %collective-permute-done.26 = f32[768,128]{1,0:T(8,128)S(1)} collective-permute-done((f32[768,128]{1,0:T(8,128)S(1)}, f32[768,128]{1,0:T(8,128)S(1)}, u32[]{:S(2)}, u32[]{:S(2)}) %collective-permute-start.26) | collective-permute-done | bytes 393248 | tf_op jit(solution)/shard_map/ppermute | solution.py:424
  127.9 4.6 %collective-permute-done.24 = f32[256,128]{1,0:T(8,128)S(1)} collective-permute-done((f32[256,128]{1,0:T(8,128)S(1)}, f32[256,128]{1,0:T(8,128)S(1)}, u32[]{:S(2)}, u32[]{:S(2)}) %collective-permute-start.24) | collective-permute-done | bytes 131104 | tf_op jit(solution)/shard_map/ppermute | solution.py:424
  133.8 10.9 %collective-permute-done.27 = f32[768,128]{1,0:T(8,128)S(1)} collective-permute-done((f32[768,128]{1,0:T(8,128)S(1)}, f32[768,128]{1,0:T(8,128)S(1)}, u32[]{:S(2)}, u32[]{:S(2)}) %collective-permute-start.27) | collective-permute-done | bytes 393248 | tf_op jit(solution)/shard_map/ppermute | solution.py:424
  145.3 3.7 %collective-permute-start.29 = (f32[8,128]{1,0:T(8,128)S(1)}, f32[8,128]{1,0:T(8,128)S(1)}, u32[]{:S(2)}, u32[]{:S(2)}) collective-permute-start(f32[8,128]{1,0:T(8,128)S(1)} %get-tuple-element.78), channel_id=1, source_target_pairs={{0,1},{1,0},{2,3},{3,2},{4,5},{5,4},{6,7},{7,6},{8,9},{9,8},{10,11... | collective-permute-start | bytes 12296 | tf_op jit(solution)/shard_map/ppermute | solution.py:424
  150.7 9.1 %all-gather = f32[64,128]{1,0:T(8,128)S(1)} all-gather(f32[8,128]{1,0:T(8,128)S(1)} %add.39), channel_id=2, replica_groups=mesh['rows'=8,'cols'=4] {'rows'}, dimensions={0}, use_global_device_ids=true | all-gather | bytes 36864 | tf_op jit(solution)/shard_map/all_gather | solution.py:497
  (86 shorter events, 41.4 us)
Async XLA Ops:
  14.7 7.0 %collective-permute-start.4 = (f32[512,256]{1,0:T(8,128)S(1)}, f32[512,256]{1,0:T(8,128)S(1)}, u32[]{:S(2)}, u32[]{:S(2)}) collective-permute-start(f32[512,256]{1,0:T(8,128)S(1)} %copy-done.4), channel_id=1, source_target_pairs={{0,4},{4,0},{8,12},{12,8},{16,20},{20,16},{24,28},{28,24},{1,5},{5... | collective-permute-start | bytes 1572872 | tf_op jit(solution)/shard_map/ppermute | solution.py:424
  17.2 13.2 %collective-permute-start.1 = (f32[520,128]{1,0:T(8,128)S(1)}, f32[520,128]{1,0:T(8,128)S(1)}, u32[]{:S(2)}, u32[]{:S(2)}) collective-permute-start(f32[520,128]{1,0:T(8,128)S(1)} %get-tuple-element.45), channel_id=1, source_target_pairs={{0,24},{4,28},{8,16},{12,20},{16,8},{20,12},{24,0},{28,4},{1,25},{... | collective-permute-start | bytes 798728 | tf_op jit(solution)/shard_map/ppermute | solution.py:424
  21.0 12.7 %collective-permute-start.2 = (f32[520,128]{1,0:T(8,128)S(1)}, f32[520,128]{1,0:T(8,128)S(1)}, u32[]{:S(2)}, u32[]{:S(2)}) collective-permute-start(f32[520,128]{1,0:T(8,128)S(1)} %get-tuple-element.46), channel_id=1, source_target_pairs={{0,8},{4,12},{8,0},{12,4},{16,24},{20,28},{24,16},{28,20},{1,9},{5... | collective-permute-start | bytes 798728 | tf_op jit(solution)/shard_map/ppermute | solution.py:424
  21.6 12.2 %collective-permute-start.3 = (f32[520,128]{1,0:T(8,128)S(1)}, f32[520,128]{1,0:T(8,128)S(1)}, u32[]{:S(2)}, u32[]{:S(2)}) collective-permute-start(f32[520,128]{1,0:T(8,128)S(1)} %get-tuple-element.47), channel_id=1, source_target_pairs={{0,16},{4,20},{8,24},{12,28},{16,0},{20,4},{24,8},{28,12},{1,17},{... | collective-permute-start | bytes 798728 | tf_op jit(solution)/shard_map/ppermute | solution.py:424
  33.9 10.2 %collective-permute-start.7 = (f32[512,128]{1,0:T(8,128)S(1)}, f32[512,128]{1,0:T(8,128)S(1)}, u32[]{:S(2)}, u32[]{:S(2)}) collective-permute-start(f32[512,128]{1,0:T(8,128)S(1)} %get-tuple-element.54.piece_ref), channel_id=1, source_target_pairs={{0,24},{4,28},{8,16},{12,20},{16,8},{20,12},{24,0},{28,4},{1,25},{... | collective-permute-start | bytes 786440 | tf_op jit(solution)/shard_map/ppermute | solution.py:424
  36.3 12.4 %collective-permute-start.6 = (f32[512,128]{1,0:T(8,128)S(1)}, f32[512,128]{1,0:T(8,128)S(1)}, u32[]{:S(2)}, u32[]{:S(2)}) collective-permute-start(f32[512,128]{1,0:T(8,128)S(1)} %get-tuple-element.54.piece_ref), channel_id=1, source_target_pairs={{0,8},{4,12},{8,0},{12,4},{16,24},{20,28},{24,16},{28,20},{1,9},{5... | collective-permute-start | bytes 786440 | tf_op jit(solution)/shard_map/ppermute | solution.py:424
  36.8 12.6 %collective-permute-start.5 = (f32[512,128]{1,0:T(8,128)S(1)}, f32[512,128]{1,0:T(8,128)S(1)}, u32[]{:S(2)}, u32[]{:S(2)}) collective-permute-start(f32[512,128]{1,0:T(8,128)S(1)} %get-tuple-element.54.piece_ref), channel_id=1, source_target_pairs={{0,16},{4,20},{8,24},{12,28},{16,0},{20,4},{24,8},{28,12},{1,17},{... | collective-permute-start | bytes 786440 | tf_op jit(solution)/shard_map/ppermute | solution.py:424
  51.9 5.6 %collective-permute-start.9 = (f32[256,128]{1,0:T(8,128)S(1)}, f32[256,128]{1,0:T(8,128)S(1)}, u32[]{:S(2)}, u32[]{:S(2)}) collective-permute-start(f32[256,128]{1,0:T(8,128)S(1)} %slice.21), channel_id=1, source_target_pairs={{0,1},{1,0},{2,3},{3,2},{4,5},{5,4},{6,7},{7,6},{8,9},{9,8},{10,11... | collective-permute-start | bytes 393224 | tf_op jit(solution)/shard_map/ppermute | solution.py:424
  57.5 6.9 %collective-permute-start.10 = (f32[256,128]{1,0:T(8,128)S(1)}, f32[256,128]{1,0:T(8,128)S(1)}, u32[]{:S(2)}, u32[]{:S(2)}) collective-permute-start(f32[256,128]{1,0:T(8,128)S(1)} %slice_add_fusion), channel_id=1, source_target_pairs={{0,3},{1,2},{2,1},{3,0},{4,7},{5,6},{6,5},{7,4},{8,11},{9,10},{10,... | collective-permute-start | bytes 393224 | tf_op jit(solution)/shard_map/ppermute | solution.py:424
  64.5 5.3 %collective-permute-start.11 = (f32[256,128]{1,0:T(8,128)S(1)}, f32[256,128]{1,0:T(8,128)S(1)}, u32[]{:S(2)}, u32[]{:S(2)}) collective-permute-start(f32[256,128]{1,0:T(8,128)S(1)} %add.32), channel_id=1, source_target_pairs={{0,1},{1,0},{2,3},{3,2},{4,5},{5,4},{6,7},{7,6},{8,9},{9,8},{10,11... | collective-permute-start | bytes 393224 | tf_op jit(solution)/shard_map/ppermute | solution.py:424
  73.5 14.8 %collective-permute-start.15 = (f32[520,128]{1,0:T(8,128)S(1)}, f32[520,128]{1,0:T(8,128)S(1)}, u32[]{:S(2)}, u32[]{:S(2)}) collective-permute-start(f32[520,128]{1,0:T(8,128)S(1)} %shard_map.96), channel_id=1, source_target_pairs={{0,16},{4,20},{8,24},{12,28},{16,0},{20,4},{24,8},{28,12},{1,17},{... | collective-permute-start | bytes 798728 | tf_op jit(solution)/shard_map/ppermute | solution.py:424
  74.2 14.1 %collective-permute-start.14 = (f32[520,128]{1,0:T(8,128)S(1)}, f32[520,128]{1,0:T(8,128)S(1)}, u32[]{:S(2)}, u32[]{:S(2)}) collective-permute-start(f32[520,128]{1,0:T(8,128)S(1)} %shard_map.95), channel_id=1, source_target_pairs={{0,8},{4,12},{8,0},{12,4},{16,24},{20,28},{24,16},{28,20},{1,9},{5... | collective-permute-start | bytes 798728 | tf_op jit(solution)/shard_map/ppermute | solution.py:424
  75.7 13.2 %collective-permute-start.13 = (f32[520,128]{1,0:T(8,128)S(1)}, f32[520,128]{1,0:T(8,128)S(1)}, u32[]{:S(2)}, u32[]{:S(2)}) collective-permute-start(f32[520,128]{1,0:T(8,128)S(1)} %get-tuple-element.59), channel_id=1, source_target_pairs={{0,24},{4,28},{8,16},{12,20},{16,8},{20,12},{24,0},{28,4},{1,25},{... | collective-permute-start | bytes 798728 | tf_op jit(solution)/shard_map/ppermute | solution.py:424
  89.0 10.1 %collective-permute-start.18 = (f32[512,128]{1,0:T(8,128)S(1)}, f32[512,128]{1,0:T(8,128)S(1)}, u32[]{:S(2)}, u32[]{:S(2)}) collective-permute-start(f32[512,128]{1,0:T(8,128)S(1)} %get-tuple-element.61.refs_0_), channel_id=1, source_target_pairs={{0,24},{4,28},{8,16},{12,20},{16,8},{20,12},{24,0},{28,4},{1,25},{... | collective-permute-start | bytes 786440 | tf_op jit(solution)/shard_map/ppermute | solution.py:424
  90.7 12.8 %collective-permute-start.17 = (f32[512,128]{1,0:T(8,128)S(1)}, f32[512,128]{1,0:T(8,128)S(1)}, u32[]{:S(2)}, u32[]{:S(2)}) collective-permute-start(f32[512,128]{1,0:T(8,128)S(1)} %get-tuple-element.61.refs_0_), channel_id=1, source_target_pairs={{0,8},{4,12},{8,0},{12,4},{16,24},{20,28},{24,16},{28,20},{1,9},{5... | collective-permute-start | bytes 786440 | tf_op jit(solution)/shard_map/ppermute | solution.py:424
  91.2 13.6 %collective-permute-start.16 = (f32[512,128]{1,0:T(8,128)S(1)}, f32[512,128]{1,0:T(8,128)S(1)}, u32[]{:S(2)}, u32[]{:S(2)}) collective-permute-start(f32[512,128]{1,0:T(8,128)S(1)} %get-tuple-element.61.refs_0_), channel_id=1, source_target_pairs={{0,16},{4,20},{8,24},{12,28},{16,0},{20,4},{24,8},{28,12},{1,17},{... | collective-permute-start | bytes 786440 | tf_op jit(solution)/shard_map/ppermute | solution.py:424
  99.2 7.6 %collective-permute-start.22 = (f32[512,128]{1,0:T(8,128)S(1)}, f32[512,128]{1,0:T(8,128)S(1)}, u32[]{:S(2)}, u32[]{:S(2)}) collective-permute-start(f32[512,128]{1,0:T(8,128)S(1)} %collective-permute-done.18.refs_0_), channel_id=1, source_target_pairs={{0,4},{4,0},{8,12},{12,8},{16,20},{20,16},{24,28},{28,24},{1,5},{5... | collective-permute-start | bytes 786440 | tf_op jit(solution)/shard_map/ppermute | solution.py:424
  111.2 5.8 %collective-permute-start.23 = (f32[256,128]{1,0:T(8,128)S(1)}, f32[256,128]{1,0:T(8,128)S(1)}, u32[]{:S(2)}, u32[]{:S(2)}) collective-permute-start(f32[256,128]{1,0:T(8,128)S(1)} %get-tuple-element.69), channel_id=1, source_target_pairs={{0,1},{1,0},{2,3},{3,2},{4,5},{5,4},{6,7},{7,6},{8,9},{9,8},{10,11... | collective-permute-start | bytes 393224 | tf_op jit(solution)/shard_map/ppermute | solution.py:424
  117.0 10.9 %collective-permute-start.26 = (f32[768,128]{1,0:T(8,128)S(1)}, f32[768,128]{1,0:T(8,128)S(1)}, u32[]{:S(2)}, u32[]{:S(2)}) collective-permute-start(f32[768,128]{1,0:T(8,128)S(1)} %get-tuple-element.73), channel_id=1, source_target_pairs={{0,1},{1,0},{2,3},{3,2},{4,5},{5,4},{6,7},{7,6},{8,9},{9,8},{10,11... | collective-permute-start | bytes 1179656 | tf_op jit(solution)/shard_map/ppermute | solution.py:424
  118.8 13.7 %collective-permute-start.24 = (f32[256,128]{1,0:T(8,128)S(1)}, f32[256,128]{1,0:T(8,128)S(1)}, u32[]{:S(2)}, u32[]{:S(2)}) collective-permute-start(f32[256,128]{1,0:T(8,128)S(1)} %add.35), channel_id=1, source_target_pairs={{0,3},{1,2},{2,1},{3,0},{4,7},{5,6},{6,5},{7,4},{8,11},{9,10},{10,... | collective-permute-start | bytes 393224 | tf_op jit(solution)/shard_map/ppermute | solution.py:424
  132.5 12.2 %collective-permute-start.27 = (f32[768,128]{1,0:T(8,128)S(1)}, f32[768,128]{1,0:T(8,128)S(1)}, u32[]{:S(2)}, u32[]{:S(2)}) collective-permute-start(f32[768,128]{1,0:T(8,128)S(1)} %add.37), channel_id=1, source_target_pairs={{0,3},{1,2},{2,1},{3,0},{4,7},{5,6},{6,5},{7,4},{8,11},{9,10},{10,... | collective-permute-start | bytes 1179656 | tf_op jit(solution)/shard_map/ppermute | solution.py:424
  133.7 11.5 %collective-permute-start.25 = (f32[256,128]{1,0:T(8,128)S(1)}, f32[256,128]{1,0:T(8,128)S(1)}, u32[]{:S(2)}, u32[]{:S(2)}) collective-permute-start(f32[256,128]{1,0:T(8,128)S(1)} %get-tuple-element.70.refs_0_), channel_id=1, source_target_pairs={{0,1},{1,0},{2,3},{3,2},{4,5},{5,4},{6,7},{7,6},{8,9},{9,8},{10,11... | collective-permute-start | bytes 393224 | tf_op jit(solution)/shard_map/ppermute | solution.py:424
  145.3 5.3 %collective-permute-start.29 = (f32[8,128]{1,0:T(8,128)S(1)}, f32[8,128]{1,0:T(8,128)S(1)}, u32[]{:S(2)}, u32[]{:S(2)}) collective-permute-start(f32[8,128]{1,0:T(8,128)S(1)} %get-tuple-element.78), channel_id=1, source_target_pairs={{0,1},{1,0},{2,3},{3,2},{4,5},{5,4},{6,7},{7,6},{8,9},{9,8},{10,11... | collective-permute-start | bytes 12296 | tf_op jit(solution)/shard_map/ppermute | solution.py:424
  149.0 10.8 %collective-permute-start.28 = (f32[768,128]{1,0:T(8,128)S(1)}, f32[768,128]{1,0:T(8,128)S(1)}, u32[]{:S(2)}, u32[]{:S(2)}) collective-permute-start(f32[768,128]{1,0:T(8,128)S(1)} %get-tuple-element.77.refs_2_), channel_id=1, source_target_pairs={{0,1},{1,0},{2,3},{3,2},{4,5},{5,4},{6,7},{7,6},{8,9},{9,8},{10,11... | collective-permute-start | bytes 1179656 | tf_op jit(solution)/shard_map/ppermute | solution.py:424
  (12 other events, 131.8 us)

commit v4 on v3

--- a/solution.py
+++ b/solution.py
@@ -296,8 +296,8 @@
     )(resident(high), resident(low), *map(resident, held), *sources)
 
 
-def transposed_kernel(shift, sides, first, segments, l_ref, *refs):
-    place = here(2 * segments)
+def transposed_kernel(shift, sides, first, l_ref, *refs):
+    place = here(2)
     pieces, refs = refs[: len(sides)], refs[len(sides) :]
     value = None if first else refs[0][...]
     block = place[0] ^ shift
@@ -310,42 +310,61 @@
             high, low = split(l_ref[pl.ds(start, step), :])
             share = turned(pair(ref[i : i + step, :]), high, low)
             value = share if value is None else value + share
-    if segments == 0:
-        refs[-1][...] = value
-        return
-    *outs, image = refs[-2 * len(SHARES) - 1 :]
-    image[...] = value.T
-    seg = image.shape[0] // segments
+    refs[-1][...] = value
+
+
+def transposed(shift, sides, inv_factor, pieces, acc):
+    depth = inv_factor.shape[1]
+    t = pieces[0].shape[1]
+    args = [resident(inv_factor), *pieces] + ([] if acc is None else [acc])
+    return pl.pallas_call(
+        functools.partial(transposed_kernel, shift, sides, acc is None),
+        in_specs=[local] * len(args),
+        out_specs=local,
+        out_shape=jax.ShapeDtypeStruct((t, depth), f32),
+        compiler_params=params(),
+        cost_estimate=cost(),
+    )(*args)
+
+
+def last_kernel(shifts, part, segments, l_ref, acc_ref, *refs):
+    pieces, (keep_ref, send_ref, image) = refs[: len(shifts)], refs[len(shifts) :]
+    chip, core, segment = here(2 * segments)
+    m, depth = pieces[0].shape[0], acc_ref.shape[1]
+    seg, n = depth // segments, image.shape[1]
+    begin, end = cuts(seg)[part]
+    bands = [(u * seg + begin, u * seg + end) for u in range(segments)]
+    apart = all(edge % 128 == 0 for band in bands for edge in band)
+    pairs = [pair(ref[...]) for ref in pieces]
+    for u, (low_edge, high_edge) in enumerate(bands if apart else [(0, depth)]):
+        value = acc_ref[:, low_edge:high_edge]
+        for shift, values in zip(shifts, pairs):
+            start = pl.multiple_of(((chip ^ shift) * 2 + 1 - core) * m, m)
+            high, low = split(l_ref[pl.ds(start, m), low_edge:high_edge])
+            value += turned(values, high, low)
+        value = value.T
+        if apart:
+            image[u] = value
+        else:
+            for i, (first, final) in enumerate(bands):
+                image[i] = value[first:final, :]
     half = segments // 2
     for u in range(segments):
-        for c, (begin, end) in enumerate(cuts(seg)):
-            ref = outs[2 * c + (u >= half)]
-            at = pl.ds(pl.multiple_of((place[2] ^ u) * seg + begin, PAD), end - begin)
-            start = (u % half) * (end - begin)
-            ref[start : start + end - begin, :] = image[at, :]
-
-
-def transposed(shift, sides, inv_factor, pieces, acc, segments=0):
-    depth = inv_factor.shape[1]
-    m, t = pieces[0].shape
-    args = [resident(inv_factor), *pieces] + ([] if acc is None else [acc])
-    scratch = []
-    if segments:
-        seg = depth // segments
-        out = tuple(
-            jax.ShapeDtypeStruct((segments // 2 * (end - begin), t), f32)
-            for begin, end in cuts(seg)
-            for _ in range(2)
-        )
-        scratch = [pltpu.VMEM((depth, t), f32)]
-    else:
-        out = jax.ShapeDtypeStruct((t, depth), f32)
-    return pl.pallas_call(
-        functools.partial(transposed_kernel, shift, sides, acc is None, segments),
+        ref = keep_ref if u < half else send_ref
+        ref[(u % half) * n : (u % half + 1) * n, :] = image[segment ^ u]
+
+
+def last_transposed(part, segments, inv_factor, pieces, acc):
+    t, depth = acc.shape
+    begin, end = cuts(depth // segments)[part]
+    out = jax.ShapeDtypeStruct((segments // 2 * (end - begin), t), f32)
+    args = [resident(inv_factor), acc, *[piece for _, piece in pieces]]
+    return pl.pallas_call(
+        functools.partial(last_kernel, [shift for shift, _ in pieces], part, segments),
         in_specs=[local] * len(args),
-        out_specs=(local,) * len(out) if segments else local,
-        out_shape=out,
-        scratch_shapes=scratch,
+        out_specs=(local, local),
+        out_shape=(out, out),
+        scratch_shapes=[pltpu.VMEM((segments, end - begin, t), f32)],
         compiler_params=params(),
         cost_estimate=cost(),
     )(*args)
@@ -424,7 +443,7 @@
         return lax.ppermute(x, axis, [(i, i ^ mask) for i in range(size)])
 
     place = jnp.stack(here(n_cols)).astype(jnp.int32)
-    order = [chips - 1, *range(1, chips - 1)]
+    order = list(range(1, chips))
 
     other_points = swap(points, "rows", 1)
     keep, send = forward(inv_factor, direction, residual, chips)
@@ -468,12 +487,9 @@
         other = swap(piece, "rows", 1)
         acc = transposed(shift, (0,), inv_factor, [piece], acc)
         late.append((shift, other))
-    for shift, other in late:
-        last = shift == late[-1][0]
-        acc = transposed(shift, (1,), inv_factor, [other], acc, segments if last else 0)
     pieces, norm_next, step_one, step_two, done = [], None, (), (), ()
     for c, (begin, _) in enumerate(cuts(residual.shape[0] // segments)):
-        image, send = acc[2 * c : 2 * c + 2]
+        image, send = last_transposed(c, segments, inv_factor, late, acc)
         send, step_one = lax.optimization_barrier((send, step_one))
         step_one = swap(send, "cols", masks[0])
         image = image + step_one

time: 161 us -> 158 us (0.981)
  waiting for transfers between devices: 62.8 us -> 59.9 us
    pallas_call x7 -> x4, Pallas kernels: 10.7 us -> 6.3 us  [transposed(): pl.pallas_call(functools.partial(transposed_kernel, shift, sides, acc is...]
    pallas_call x0 -> x2, Pallas kernels: none -> 4.24 us  [last_transposed(): pl.pallas_call(functools.partial(last_kernel, [shift for shift, _ in piec...]
    ppermute x30, waiting for transfers between devices: 62.8 us -> 59.9 us  [swap(): return lax.ppermute(x, axis, [(i, i ^ mask) for i in range(size)])]
  transfers between devices with their start and end apart: 30 -> 30, of which waited for: 18 -> 19; matrix products, arithmetic and copies ran while one was open for 1% -> 1% of each run, Pallas kernels for 12% -> 12%
where the time goes in v4:
time: 158 us
  waiting for transfers between devices  59.9 us (38%)
  Pallas kernels  38.4 us (24%)
  starting transfers between devices  35.9 us (23%)
  local copies, waits for them, and re-layouts  12.8 us (8%)
  blocking collectives  8.97 us (6%)
    ppermute x30, waiting for transfers between devices, swap(): return lax.ppermute(x, axis, [(i, i ^ mask) for i in range(size)])  59.9 us
    ppermute x30, starting transfers between devices, swap(): return lax.ppermute(x, axis, [(i, i ^ mask) for i in range(size)])  35.9 us
    pallas_call x1, Pallas kernels, forward(): pl.pallas_call(functools.partial(forward_kernel, chips, slots), in_specs=...  13.6 us
    unnamed x12, local copies, waits for them, and re-layouts  12.8 us
    all_gather x1, blocking collectives, body(): norm_next = jnp.sum(lax.all_gather(norm_next, 'rows'), axis=0)  8.97 us
    pallas_call x1, Pallas kernels, gaussian(): pl.pallas_call(functools.partial(kernel_kernel, segments), grid_spec=pltp...  6.42 us
    pallas_call x4, Pallas kernels, transposed(): pl.pallas_call(functools.partial(transposed_kernel, shift, sides, acc is...  6.3 us
    pallas_call x2, Pallas kernels, last_transposed(): pl.pallas_call(functools.partial(last_kernel, [shift for shift, _ in piec...  4.24 us
  transfers between devices with their start and end apart: 30, of which 19 were waited for; matrix products, arithmetic and copies ran while one was open for 1% of the time, Pallas kernels for 12%

profile of v4, /device:TPU:0, one launch (start us, length us, event | category | flops | bytes accessed | tf_op | source)
XLA Modules:
  0.0 158.2 jit_solution(2198808465062590306)
XLA Ops:
  0.6 13.6 %shard_map.85 = (f32[4,520,128]{2,1,0:T(8,128)S(1)}, f32[4,520,128]{2,1,0:T(8,128)S(1)}) custom-call(f32[4096,2048]{1,0:T(8,128)} %l_ref.13, f32[2048,128]{1,0:T(8,128)} %refs_4_.3, f32[2048,128]{1,0:T(8,128)} %r_ref.5), custom_call_target="tpu_custom_call" | custom-call | flops 1 | bytes 1 | tf_op jit(solution)/shard_map/pallas_call | solution.py:136
  14.8 2.2 %collective-permute-done.refs_1_ = f32[4,520,128]{2,1,0:T(8,128)S(1)} collective-permute-done((f32[4,520,128]{2,1,0:T(8,128)S(1)}, f32[4,520,128]{2,1,0:T(8,128)S(1)}, u32[]{:S(2)}, u32[]{:S(2)}) %collective-permute-start) | collective-permute-done | bytes 1064992 | tf_op jit(solution)/shard_map/ppermute | solution.py:443
  17.2 2.9 %collective-permute-start.1 = (f32[520,128]{1,0:T(8,128)S(1)}, f32[520,128]{1,0:T(8,128)S(1)}, u32[]{:S(2)}, u32[]{:S(2)}) collective-permute-start(f32[520,128]{1,0:T(8,128)S(1)} %get-tuple-element.45), channel_id=1, source_target_pairs={{0,8},{4,12},{8,0},{12,4},{16,24},{20,28},{24,16},{28,20},{1,9},{5... | collective-permute-start | bytes 798728 | tf_op jit(solution)/shard_map/ppermute | solution.py:443
  21.7 2.2 %copy-done.3 = f32[4096,256]{1,0:T(8,128)S(1)} copy-done((f32[4096,256]{1,0:T(8,128)S(1)}, f32[4096,256]{1,0:T(8,128)}, u32[]{:S(2)}) %copy-start.3) | copy-done | bytes 4194328
  23.9 6.4 %shard_map.88 = (bf16[4,512,1024]{2,1,0:T(8,128)(2,1)S(1)}, bf16[4,512,1024]{2,1,0:T(8,128)(2,1)S(1)}) custom-call(s32[3]{0:T(128)S(1)} %pad_add_fusion.place, f32[512,256]{1,0:T(8,128)S(1)} %copy-done.4, f32[512,256]{1,0:T(8,128)S(1)} %collective-permute-done.4.other_ref, f32[4096,256]{1,0:T(8,128)S(1)} %copy-done.3), custom_call_target="tpu_custom_call" | custom-call | flops 1 | bytes 1 | tf_op jit(solution)/shard_map/pallas_call | solution.py:209
  30.3 3.6 %collective-permute-done.2.refs_2_ = f32[520,128]{1,0:T(8,128)S(1)} collective-permute-done((f32[520,128]{1,0:T(8,128)S(1)}, f32[520,128]{1,0:T(8,128)S(1)}, u32[]{:S(2)}, u32[]{:S(2)}) %collective-permute-start.2) | collective-permute-done | bytes 266272 | tf_op jit(solution)/shard_map/ppermute | solution.py:443
  38.4 5.0 %collective-permute-done.7.piece_ref = f32[512,128]{1,0:T(8,128)S(1)} collective-permute-done((f32[512,128]{1,0:T(8,128)S(1)}, f32[512,128]{1,0:T(8,128)S(1)}, u32[]{:S(2)}, u32[]{:S(2)}) %collective-permute-start.7) | collective-permute-done | bytes 262176 | tf_op jit(solution)/shard_map/ppermute | solution.py:443
  44.1 4.1 %collective-permute-done.6.piece_ref = f32[512,128]{1,0:T(8,128)S(1)} collective-permute-done((f32[512,128]{1,0:T(8,128)S(1)}, f32[512,128]{1,0:T(8,128)S(1)}, u32[]{:S(2)}, u32[]{:S(2)}) %collective-permute-start.6) | collective-permute-done | bytes 262176 | tf_op jit(solution)/shard_map/ppermute | solution.py:443
  53.1 4.0 %collective-permute-done.9 = f32[256,128]{1,0:T(8,128)S(1)} collective-permute-done((f32[256,128]{1,0:T(8,128)S(1)}, f32[256,128]{1,0:T(8,128)S(1)}, u32[]{:S(2)}, u32[]{:S(2)}) %collective-permute-start.9) | collective-permute-done | bytes 131104 | tf_op jit(solution)/shard_map/ppermute | solution.py:443
  57.1 3.7 %collective-permute-start.10 = (f32[256,128]{1,0:T(8,128)S(1)}, f32[256,128]{1,0:T(8,128)S(1)}, u32[]{:S(2)}, u32[]{:S(2)}) collective-permute-start(f32[256,128]{1,0:T(8,128)S(1)} %slice_add_fusion), channel_id=1, source_target_pairs={{0,3},{1,2},{2,1},{3,0},{4,7},{5,6},{6,5},{7,4},{8,11},{9,10},{10,... | collective-permute-start | bytes 393224 | tf_op jit(solution)/shard_map/ppermute | solution.py:443
  60.8 3.2 %collective-permute-done.10 = f32[256,128]{1,0:T(8,128)S(1)} collective-permute-done((f32[256,128]{1,0:T(8,128)S(1)}, f32[256,128]{1,0:T(8,128)S(1)}, u32[]{:S(2)}, u32[]{:S(2)}) %collective-permute-start.10) | collective-permute-done | bytes 131104 | tf_op jit(solution)/shard_map/ppermute | solution.py:443
  64.0 2.3 %collective-permute-start.11 = (f32[256,128]{1,0:T(8,128)S(1)}, f32[256,128]{1,0:T(8,128)S(1)}, u32[]{:S(2)}, u32[]{:S(2)}) collective-permute-start(f32[256,128]{1,0:T(8,128)S(1)} %add.32), channel_id=1, source_target_pairs={{0,1},{1,0},{2,3},{3,2},{4,5},{5,4},{6,7},{7,6},{8,9},{9,8},{10,11... | collective-permute-start | bytes 393224 | tf_op jit(solution)/shard_map/ppermute | solution.py:443
  66.3 2.9 %collective-permute-done.11 = f32[256,128]{1,0:T(8,128)S(1)} collective-permute-done((f32[256,128]{1,0:T(8,128)S(1)}, f32[256,128]{1,0:T(8,128)S(1)}, u32[]{:S(2)}, u32[]{:S(2)}) %collective-permute-start.11) | collective-permute-done | bytes 131104 | tf_op jit(solution)/shard_map/ppermute | solution.py:443
  76.6 10.5 %copy-done = f32[4096,2048]{1,0:T(8,128)S(1)} copy-done((f32[4096,2048]{1,0:T(8,128)S(1)}, f32[4096,2048]{1,0:T(8,128)}, u32[]{:S(2)}) %copy-start) | copy-done | bytes 33554456
  91.9 2.4 %shard_map.98.refs_1_ = f32[128,2048]{1,0:T(8,128)S(1)} custom-call(f32[4096,2048]{1,0:T(8,128)S(1)} %copy-done, f32[512,128]{1,0:T(8,128)S(1)} %get-tuple-element.61.refs_0_, f32[512,128]{1,0:T(8,128)S(1)} %collective-permute-done.19.refs_1_), custom_call_target="tpu_custom_call" | custom-call | flops 1 | bytes 1 | tf_op jit(solution)/shard_map/pallas_call | solution.py:320
  94.3 3.2 %collective-permute-done.18.refs_0_ = f32[512,128]{1,0:T(8,128)S(1)} collective-permute-done((f32[512,128]{1,0:T(8,128)S(1)}, f32[512,128]{1,0:T(8,128)S(1)}, u32[]{:S(2)}, u32[]{:S(2)}) %collective-permute-start.18) | collective-permute-done | bytes 262176 | tf_op jit(solution)/shard_map/ppermute | solution.py:443
  98.8 4.2 %collective-permute-done.17.refs_0_ = f32[512,128]{1,0:T(8,128)S(1)} collective-permute-done((f32[512,128]{1,0:T(8,128)S(1)}, f32[512,128]{1,0:T(8,128)S(1)}, u32[]{:S(2)}, u32[]{:S(2)}) %collective-permute-start.17) | collective-permute-done | bytes 262176 | tf_op jit(solution)/shard_map/ppermute | solution.py:443
  109.9 3.1 %shard_map.104 = (f32[768,128]{1,0:T(8,128)S(1)}, f32[768,128]{1,0:T(8,128)S(1)}) custom-call(f32[4096,2048]{1,0:T(8,128)S(1)} %copy-done, f32[128,2048]{1,0:T(8,128)S(1)} %shard_map.101.acc_ref, f32[512,128]{1,0:T(8,128)S(1)} %collective-permute-done.20.refs_0_, f32[512,128]{1,0:T(8,128)S(1)} %collective-permute-done.21.refs_1_, ...), custom_call_target="tpu_custom_call" | custom-call | flops 1 | bytes 1 | tf_op jit(solution)/shard_map/pallas_call | solution.py:362
  115.5 2.8 %collective-permute-start.24 = (f32[256,128]{1,0:T(8,128)S(1)}, f32[256,128]{1,0:T(8,128)S(1)}, u32[]{:S(2)}, u32[]{:S(2)}) collective-permute-start(f32[256,128]{1,0:T(8,128)S(1)} %add.35), channel_id=1, source_target_pairs={{0,3},{1,2},{2,1},{3,0},{4,7},{5,6},{6,5},{7,4},{8,11},{9,10},{10,... | collective-permute-start | bytes 393224 | tf_op jit(solution)/shard_map/ppermute | solution.py:443
  118.3 6.4 %collective-permute-done.26 = f32[768,128]{1,0:T(8,128)S(1)} collective-permute-done((f32[768,128]{1,0:T(8,128)S(1)}, f32[768,128]{1,0:T(8,128)S(1)}, u32[]{:S(2)}, u32[]{:S(2)}) %collective-permute-start.26) | collective-permute-done | bytes 393248 | tf_op jit(solution)/shard_map/ppermute | solution.py:443
  124.7 4.7 %collective-permute-done.24 = f32[256,128]{1,0:T(8,128)S(1)} collective-permute-done((f32[256,128]{1,0:T(8,128)S(1)}, f32[256,128]{1,0:T(8,128)S(1)}, u32[]{:S(2)}, u32[]{:S(2)}) %collective-permute-start.24) | collective-permute-done | bytes 131104 | tf_op jit(solution)/shard_map/ppermute | solution.py:443
  130.7 11.1 %collective-permute-done.27 = f32[768,128]{1,0:T(8,128)S(1)} collective-permute-done((f32[768,128]{1,0:T(8,128)S(1)}, f32[768,128]{1,0:T(8,128)S(1)}, u32[]{:S(2)}, u32[]{:S(2)}) %collective-permute-start.27) | collective-permute-done | bytes 393248 | tf_op jit(solution)/shard_map/ppermute | solution.py:443
  142.3 3.8 %collective-permute-start.29 = (f32[8,128]{1,0:T(8,128)S(1)}, f32[8,128]{1,0:T(8,128)S(1)}, u32[]{:S(2)}, u32[]{:S(2)}) collective-permute-start(f32[8,128]{1,0:T(8,128)S(1)} %get-tuple-element.78), channel_id=1, source_target_pairs={{0,1},{1,0},{2,3},{3,2},{4,5},{5,4},{6,7},{7,6},{8,9},{9,8},{10,11... | collective-permute-start | bytes 12296 | tf_op jit(solution)/shard_map/ppermute | solution.py:443
  147.7 9.0 %all-gather = f32[64,128]{1,0:T(8,128)S(1)} all-gather(f32[8,128]{1,0:T(8,128)S(1)} %add.39), channel_id=2, replica_groups=mesh['rows'=8,'cols'=4] {'rows'}, dimensions={0}, use_global_device_ids=true | all-gather | bytes 36864 | tf_op jit(solution)/shard_map/all_gather | solution.py:513
  (85 shorter events, 39.8 us)
Async XLA Ops:
  14.7 7.0 %collective-permute-start.4 = (f32[512,256]{1,0:T(8,128)S(1)}, f32[512,256]{1,0:T(8,128)S(1)}, u32[]{:S(2)}, u32[]{:S(2)}) collective-permute-start(f32[512,256]{1,0:T(8,128)S(1)} %copy-done.4), channel_id=1, source_target_pairs={{0,4},{4,0},{8,12},{12,8},{16,20},{20,16},{24,28},{28,24},{1,5},{5... | collective-permute-start | bytes 1572872 | tf_op jit(solution)/shard_map/ppermute | solution.py:443
  17.2 13.2 %collective-permute-start.1 = (f32[520,128]{1,0:T(8,128)S(1)}, f32[520,128]{1,0:T(8,128)S(1)}, u32[]{:S(2)}, u32[]{:S(2)}) collective-permute-start(f32[520,128]{1,0:T(8,128)S(1)} %get-tuple-element.45), channel_id=1, source_target_pairs={{0,8},{4,12},{8,0},{12,4},{16,24},{20,28},{24,16},{28,20},{1,9},{5... | collective-permute-start | bytes 798728 | tf_op jit(solution)/shard_map/ppermute | solution.py:443
  20.1 13.9 %collective-permute-start.2 = (f32[520,128]{1,0:T(8,128)S(1)}, f32[520,128]{1,0:T(8,128)S(1)}, u32[]{:S(2)}, u32[]{:S(2)}) collective-permute-start(f32[520,128]{1,0:T(8,128)S(1)} %get-tuple-element.46), channel_id=1, source_target_pairs={{0,16},{4,20},{8,24},{12,28},{16,0},{20,4},{24,8},{28,12},{1,17},{... | collective-permute-start | bytes 798728 | tf_op jit(solution)/shard_map/ppermute | solution.py:443
  21.6 12.4 %collective-permute-start.3 = (f32[520,128]{1,0:T(8,128)S(1)}, f32[520,128]{1,0:T(8,128)S(1)}, u32[]{:S(2)}, u32[]{:S(2)}) collective-permute-start(f32[520,128]{1,0:T(8,128)S(1)} %get-tuple-element.47), channel_id=1, source_target_pairs={{0,24},{4,28},{8,16},{12,20},{16,8},{20,12},{24,0},{28,4},{1,25},{... | collective-permute-start | bytes 798728 | tf_op jit(solution)/shard_map/ppermute | solution.py:443
  34.1 9.3 %collective-permute-start.7 = (f32[512,128]{1,0:T(8,128)S(1)}, f32[512,128]{1,0:T(8,128)S(1)}, u32[]{:S(2)}, u32[]{:S(2)}) collective-permute-start(f32[512,128]{1,0:T(8,128)S(1)} %get-tuple-element.54.piece_ref), channel_id=1, source_target_pairs={{0,8},{4,12},{8,0},{12,4},{16,24},{20,28},{24,16},{28,20},{1,9},{5... | collective-permute-start | bytes 786440 | tf_op jit(solution)/shard_map/ppermute | solution.py:443
  35.4 12.9 %collective-permute-start.6 = (f32[512,128]{1,0:T(8,128)S(1)}, f32[512,128]{1,0:T(8,128)S(1)}, u32[]{:S(2)}, u32[]{:S(2)}) collective-permute-start(f32[512,128]{1,0:T(8,128)S(1)} %get-tuple-element.54.piece_ref), channel_id=1, source_target_pairs={{0,16},{4,20},{8,24},{12,28},{16,0},{20,4},{24,8},{28,12},{1,17},{... | collective-permute-start | bytes 786440 | tf_op jit(solution)/shard_map/ppermute | solution.py:443
  36.2 12.7 %collective-permute-start.5 = (f32[512,128]{1,0:T(8,128)S(1)}, f32[512,128]{1,0:T(8,128)S(1)}, u32[]{:S(2)}, u32[]{:S(2)}) collective-permute-start(f32[512,128]{1,0:T(8,128)S(1)} %get-tuple-element.54.piece_ref), channel_id=1, source_target_pairs={{0,24},{4,28},{8,16},{12,20},{16,8},{20,12},{24,0},{28,4},{1,25},{... | collective-permute-start | bytes 786440 | tf_op jit(solution)/shard_map/ppermute | solution.py:443
  51.5 5.6 %collective-permute-start.9 = (f32[256,128]{1,0:T(8,128)S(1)}, f32[256,128]{1,0:T(8,128)S(1)}, u32[]{:S(2)}, u32[]{:S(2)}) collective-permute-start(f32[256,128]{1,0:T(8,128)S(1)} %slice.21), channel_id=1, source_target_pairs={{0,1},{1,0},{2,3},{3,2},{4,5},{5,4},{6,7},{7,6},{8,9},{9,8},{10,11... | collective-permute-start | bytes 393224 | tf_op jit(solution)/shard_map/ppermute | solution.py:443
  57.1 6.9 %collective-permute-start.10 = (f32[256,128]{1,0:T(8,128)S(1)}, f32[256,128]{1,0:T(8,128)S(1)}, u32[]{:S(2)}, u32[]{:S(2)}) collective-permute-start(f32[256,128]{1,0:T(8,128)S(1)} %slice_add_fusion), channel_id=1, source_target_pairs={{0,3},{1,2},{2,1},{3,0},{4,7},{5,6},{6,5},{7,4},{8,11},{9,10},{10,... | collective-permute-start | bytes 393224 | tf_op jit(solution)/shard_map/ppermute | solution.py:443
  64.0 5.3 %collective-permute-start.11 = (f32[256,128]{1,0:T(8,128)S(1)}, f32[256,128]{1,0:T(8,128)S(1)}, u32[]{:S(2)}, u32[]{:S(2)}) collective-permute-start(f32[256,128]{1,0:T(8,128)S(1)} %add.32), channel_id=1, source_target_pairs={{0,1},{1,0},{2,3},{3,2},{4,5},{5,4},{6,7},{7,6},{8,9},{9,8},{10,11... | collective-permute-start | bytes 393224 | tf_op jit(solution)/shard_map/ppermute | solution.py:443
  73.0 14.8 %collective-permute-start.15 = (f32[520,128]{1,0:T(8,128)S(1)}, f32[520,128]{1,0:T(8,128)S(1)}, u32[]{:S(2)}, u32[]{:S(2)}) collective-permute-start(f32[520,128]{1,0:T(8,128)S(1)} %shard_map.96), channel_id=1, source_target_pairs={{0,24},{4,28},{8,16},{12,20},{16,8},{20,12},{24,0},{28,4},{1,25},{... | collective-permute-start | bytes 798728 | tf_op jit(solution)/shard_map/ppermute | solution.py:443
  74.6 13.6 %collective-permute-start.14 = (f32[520,128]{1,0:T(8,128)S(1)}, f32[520,128]{1,0:T(8,128)S(1)}, u32[]{:S(2)}, u32[]{:S(2)}) collective-permute-start(f32[520,128]{1,0:T(8,128)S(1)} %shard_map.95), channel_id=1, source_target_pairs={{0,16},{4,20},{8,24},{12,28},{16,0},{20,4},{24,8},{28,12},{1,17},{... | collective-permute-start | bytes 798728 | tf_op jit(solution)/shard_map/ppermute | solution.py:443
  75.2 13.0 %collective-permute-start.13 = (f32[520,128]{1,0:T(8,128)S(1)}, f32[520,128]{1,0:T(8,128)S(1)}, u32[]{:S(2)}, u32[]{:S(2)}) collective-permute-start(f32[520,128]{1,0:T(8,128)S(1)} %get-tuple-element.59), channel_id=1, source_target_pairs={{0,8},{4,12},{8,0},{12,4},{16,24},{20,28},{24,16},{28,20},{1,9},{5... | collective-permute-start | bytes 798728 | tf_op jit(solution)/shard_map/ppermute | solution.py:443
  88.2 3.6 %collective-permute-start.19 = (f32[512,128]{1,0:T(8,128)S(1)}, f32[512,128]{1,0:T(8,128)S(1)}, u32[]{:S(2)}, u32[]{:S(2)}) collective-permute-start(f32[512,128]{1,0:T(8,128)S(1)} %get-tuple-element.61.refs_0_), channel_id=1, source_target_pairs={{0,4},{4,0},{8,12},{12,8},{16,20},{20,16},{24,28},{28,24},{1,5},{5... | collective-permute-start | bytes 786440 | tf_op jit(solution)/shard_map/ppermute | solution.py:443
  88.3 9.2 %collective-permute-start.18 = (f32[512,128]{1,0:T(8,128)S(1)}, f32[512,128]{1,0:T(8,128)S(1)}, u32[]{:S(2)}, u32[]{:S(2)}) collective-permute-start(f32[512,128]{1,0:T(8,128)S(1)} %get-tuple-element.61.refs_0_), channel_id=1, source_target_pairs={{0,8},{4,12},{8,0},{12,4},{16,24},{20,28},{24,16},{28,20},{1,9},{5... | collective-permute-start | bytes 786440 | tf_op jit(solution)/shard_map/ppermute | solution.py:443
  89.0 14.0 %collective-permute-start.17 = (f32[512,128]{1,0:T(8,128)S(1)}, f32[512,128]{1,0:T(8,128)S(1)}, u32[]{:S(2)}, u32[]{:S(2)}) collective-permute-start(f32[512,128]{1,0:T(8,128)S(1)} %get-tuple-element.61.refs_0_), channel_id=1, source_target_pairs={{0,16},{4,20},{8,24},{12,28},{16,0},{20,4},{24,8},{28,12},{1,17},{... | collective-permute-start | bytes 786440 | tf_op jit(solution)/shard_map/ppermute | solution.py:443
  90.4 13.9 %collective-permute-start.16 = (f32[512,128]{1,0:T(8,128)S(1)}, f32[512,128]{1,0:T(8,128)S(1)}, u32[]{:S(2)}, u32[]{:S(2)}) collective-permute-start(f32[512,128]{1,0:T(8,128)S(1)} %get-tuple-element.61.refs_0_), channel_id=1, source_target_pairs={{0,24},{4,28},{8,16},{12,20},{16,8},{20,12},{24,0},{28,4},{1,25},{... | collective-permute-start | bytes 786440 | tf_op jit(solution)/shard_map/ppermute | solution.py:443
  107.8 5.9 %collective-permute-start.23 = (f32[256,128]{1,0:T(8,128)S(1)}, f32[256,128]{1,0:T(8,128)S(1)}, u32[]{:S(2)}, u32[]{:S(2)}) collective-permute-start(f32[256,128]{1,0:T(8,128)S(1)} %get-tuple-element.69), channel_id=1, source_target_pairs={{0,1},{1,0},{2,3},{3,2},{4,5},{5,4},{6,7},{7,6},{8,9},{9,8},{10,11... | collective-permute-start | bytes 393224 | tf_op jit(solution)/shard_map/ppermute | solution.py:443
  113.7 11.0 %collective-permute-start.26 = (f32[768,128]{1,0:T(8,128)S(1)}, f32[768,128]{1,0:T(8,128)S(1)}, u32[]{:S(2)}, u32[]{:S(2)}) collective-permute-start(f32[768,128]{1,0:T(8,128)S(1)} %get-tuple-element.73), channel_id=1, source_target_pairs={{0,1},{1,0},{2,3},{3,2},{4,5},{5,4},{6,7},{7,6},{8,9},{9,8},{10,11... | collective-permute-start | bytes 1179656 | tf_op jit(solution)/shard_map/ppermute | solution.py:443
  115.5 14.0 %collective-permute-start.24 = (f32[256,128]{1,0:T(8,128)S(1)}, f32[256,128]{1,0:T(8,128)S(1)}, u32[]{:S(2)}, u32[]{:S(2)}) collective-permute-start(f32[256,128]{1,0:T(8,128)S(1)} %add.35), channel_id=1, source_target_pairs={{0,3},{1,2},{2,1},{3,0},{4,7},{5,6},{6,5},{7,4},{8,11},{9,10},{10,... | collective-permute-start | bytes 393224 | tf_op jit(solution)/shard_map/ppermute | solution.py:443
  129.4 12.4 %collective-permute-start.27 = (f32[768,128]{1,0:T(8,128)S(1)}, f32[768,128]{1,0:T(8,128)S(1)}, u32[]{:S(2)}, u32[]{:S(2)}) collective-permute-start(f32[768,128]{1,0:T(8,128)S(1)} %add.37), channel_id=1, source_target_pairs={{0,3},{1,2},{2,1},{3,0},{4,7},{5,6},{6,5},{7,4},{8,11},{9,10},{10,... | collective-permute-start | bytes 1179656 | tf_op jit(solution)/shard_map/ppermute | solution.py:443
  130.6 11.6 %collective-permute-start.25 = (f32[256,128]{1,0:T(8,128)S(1)}, f32[256,128]{1,0:T(8,128)S(1)}, u32[]{:S(2)}, u32[]{:S(2)}) collective-permute-start(f32[256,128]{1,0:T(8,128)S(1)} %get-tuple-element.70.refs_0_), channel_id=1, source_target_pairs={{0,1},{1,0},{2,3},{3,2},{4,5},{5,4},{6,7},{7,6},{8,9},{9,8},{10,11... | collective-permute-start | bytes 393224 | tf_op jit(solution)/shard_map/ppermute | solution.py:443
  142.3 5.4 %collective-permute-start.29 = (f32[8,128]{1,0:T(8,128)S(1)}, f32[8,128]{1,0:T(8,128)S(1)}, u32[]{:S(2)}, u32[]{:S(2)}) collective-permute-start(f32[8,128]{1,0:T(8,128)S(1)} %get-tuple-element.78), channel_id=1, source_target_pairs={{0,1},{1,0},{2,3},{3,2},{4,5},{5,4},{6,7},{7,6},{8,9},{9,8},{10,11... | collective-permute-start | bytes 12296 | tf_op jit(solution)/shard_map/ppermute | solution.py:443
  146.1 10.6 %collective-permute-start.28 = (f32[768,128]{1,0:T(8,128)S(1)}, f32[768,128]{1,0:T(8,128)S(1)}, u32[]{:S(2)}, u32[]{:S(2)}) collective-permute-start(f32[768,128]{1,0:T(8,128)S(1)} %get-tuple-element.77.refs_2_), channel_id=1, source_target_pairs={{0,1},{1,0},{2,3},{3,2},{4,5},{5,4},{6,7},{7,6},{8,9},{9,8},{10,11... | collective-permute-start | bytes 1179656 | tf_op jit(solution)/shard_map/ppermute | solution.py:443
  (12 other events, 117.1 us)

commit v5 on v4

--- a/solution.py
+++ b/solution.py
@@ -75,13 +75,17 @@
     return pltpu.with_memory_space_constraint(x, pltpu.VMEM)
 
 
-def forward_kernel(chips, slots, l_ref, d_ref, r_ref, keep_ref, send_ref, buffer, arrived, d, r, pairs, sems):
+def forward_kernel(chips, begin, end, slots, l_ref, d_ref, r_ref, *refs):
+    *outs, buffer, arrived, d, r, pairs, sems = refs
     m = buffer.shape[1]
-    jobs = 2 * chips
     chip, core, _ = here(2)
-
-    def copy(t, side):
-        n = 2 * t + side
+    kept = chips - outs[0].shape[0] if begin == 0 else 0
+
+    def job(n):
+        return chips - 1 - (n >> 1), 1 - (n & 1)
+
+    def copy(n):
+        t, side = job(n)
         start = pl.multiple_of(((chip ^ t) * 2 + (core ^ side)) * m, m)
         slot = lax.rem(n, slots)
         return pltpu.make_async_copy(l_ref.at[pl.ds(start, m), :], buffer.at[slot], arrived.at[slot])
@@ -89,55 +93,61 @@
     copy_d = pltpu.make_async_copy(d_ref, d, sems.at[0])
     copy_r = pltpu.make_async_copy(r_ref, r, sems.at[1])
     copy_d.start()
-    for n in range(min(slots - 1, jobs)):
-        copy(n // 2, n % 2).start()
+    for n in range(begin, min(begin + slots - 1, end)):
+        copy(n).start()
     copy_r.start()
     copy_d.wait()
     pairs[...] = pair(d[...])
 
     def step(n, carry):
-        ahead = n + slots - 1
-
-        @pl.when(ahead < jobs)
+        @pl.when(n + slots - 1 < end)
         def _():
-            copy(ahead >> 1, ahead & 1).start()
-
-        copy(n >> 1, n & 1).wait()
+            copy(n + slots - 1).start()
+
+        copy(n).wait()
         value = wide(buffer[lax.rem(n, slots)], pairs[...])
-
-        @pl.when(n & 1 == 0)
+        t, side = job(n)
+        if begin:
+            outs[0][t, :m, :] = value
+            return carry
+
+        @pl.when(side == 0)
         def _():
-            keep_ref[n >> 1, :m, :] = value
-
-        @pl.when(n & 1 == 1)
+            outs[0][t - kept, :m, :] = value
+
+        @pl.when(side == 1)
         def _():
-            send_ref[n >> 1, :m, :] = value
+            outs[1][t, :m, :] = value
 
         return carry
 
-    lax.fori_loop(0, jobs, step, 0)
+    lax.fori_loop(begin, end, step, 0)
     copy_r.wait()
     norm_now = jnp.sum(r[...] * r[...], axis=0, keepdims=True)
     dir_norm = jnp.sum(d[...] * d[...], axis=0, keepdims=True)
-    for ref in (keep_ref, send_ref):
-        for t in range(chips):
+    for ref in outs:
+        for t in range(ref.shape[0]):
             ref[t, m:, :] = jnp.zeros((PAD, d.shape[1]), f32)
             ref[t, m : m + 1, :] = norm_now
             ref[t, m + 1 : m + 2, :] = dir_norm
 
 
-def forward(inv_factor, direction, residual, chips):
+def forward(inv_factor, direction, residual, chips, own):
     n, depth = inv_factor.shape
     t = direction.shape[1]
     m = n // chips // 2
-    out = jax.ShapeDtypeStruct((chips, m + PAD, t), f32)
+    begin, end = (2 * chips - 1, 2 * chips) if own else (0, 2 * chips - 1)
+    out = tuple(
+        jax.ShapeDtypeStruct((count, m + PAD, t), f32)
+        for count in ((1,) if own else (chips - 1, chips))
+    )
     slots = 3
     far = pl.BlockSpec(memory_space=pl.ANY)
     return pl.pallas_call(
-        functools.partial(forward_kernel, chips, slots),
+        functools.partial(forward_kernel, chips, begin, end, slots),
         in_specs=[far] * 3,
-        out_specs=(local, local),
-        out_shape=(out, out),
+        out_specs=(local,) * len(out),
+        out_shape=out,
         scratch_shapes=[
             pltpu.VMEM((slots, m, depth), f32),
             pltpu.SemaphoreType.DMA((slots,)),
@@ -154,8 +164,9 @@
 def add_kernel(n_terms, n_held, *refs):
     terms, outs = refs[:n_terms], refs[n_terms + n_held :]
     if len(outs) > 1 and len(terms[0].shape) == 3:
-        for i, out in enumerate(outs):
-            out[...] = terms[0][i] + terms[1][i]
+        outs[0][...] = terms[1][0]
+        for i, out in enumerate(outs[1:]):
+            out[...] = terms[0][i] + terms[1][i + 1]
         return
     value = terms[0][...]
     for term in terms[1:]:
@@ -176,6 +187,21 @@
         compiler_params=params(),
         cost_estimate=cost(),
     )(*terms, *map(resident, held))
+
+
+def cut_kernel(begin, x_ref, *refs):
+    refs[-1][...] = x_ref[begin : begin + refs[-1].shape[0], :]
+
+
+def cut(x, begin, rows, held=()):
+    return pl.pallas_call(
+        functools.partial(cut_kernel, begin),
+        in_specs=[local] * (1 + len(held)),
+        out_specs=local,
+        out_shape=jax.ShapeDtypeStruct((rows, x.shape[1]), f32),
+        compiler_params=params(),
+        cost_estimate=cost(),
+    )(x, *map(resident, held))
 
 
 def kernel_kernel(segments, place, own_ref, other_ref, c_ref, high_ref, low_ref, ph, plo, psq):
@@ -226,12 +252,12 @@
         out_shape=(out, out),
         compiler_params=params(),
         cost_estimate=cost(12 * chips * m * n * width, 8 * chips * m * n, 2 * chips * m * n),
-    )(place, own, other, centers)
-
-
-def predict_kernel(shift, first, last, high_ref, low_ref, piece_ref, *refs):
-    m = high_ref.shape[1]
-    value = turned(pair(piece_ref[:m, :]), high_ref[shift], low_ref[shift])
+    )(place, own, other, pltpu.with_memory_space_constraint(centers, pltpu.HBM))
+
+
+def predict_kernel(shift, begin, first, last, high_ref, low_ref, piece_ref, *refs):
+    rows = slice(begin, begin + piece_ref.shape[0])
+    value = turned(pair(piece_ref[...]), high_ref[shift, rows, :], low_ref[shift, rows, :])
     if not first:
         value += refs[0][...]
     if last:
@@ -242,7 +268,7 @@
         refs[-1][...] = value
 
 
-def predict(shift, high, low, piece, acc, last):
+def predict(shift, begin, high, low, piece, acc, last):
     _, m, n = high.shape
     t = piece.shape[1]
     args = [resident(high), resident(low), piece] + ([] if acc is None else [acc])
@@ -251,7 +277,7 @@
     else:
         out = jax.ShapeDtypeStruct((t, n), f32)
     return pl.pallas_call(
-        functools.partial(predict_kernel, shift, acc is None, last),
+        functools.partial(predict_kernel, shift, begin, acc is None, last),
         in_specs=[local] * len(args),
         out_specs=(local,) * 2 if last else local,
         out_shape=out,
@@ -296,29 +322,27 @@
     )(resident(high), resident(low), *map(resident, held), *sources)
 
 
-def transposed_kernel(shift, sides, first, l_ref, *refs):
-    place = here(2)
+def transposed_kernel(m, shift, begin, sides, first, l_ref, *refs):
+    chip, core, _ = here(2)
     pieces, refs = refs[: len(sides)], refs[len(sides) :]
     value = None if first else refs[0][...]
-    block = place[0] ^ shift
     for side, ref in zip(sides, pieces):
-        core = place[1] if side == 0 else 1 - place[1]
-        m = ref.shape[0]
-        step = min(m, 256)
-        for i in range(0, m, step):
-            start = pl.multiple_of((block * 2 + core) * m + i, step)
+        n = ref.shape[0]
+        step = min(n, 256)
+        for i in range(0, n, step):
+            start = pl.multiple_of(((chip ^ shift) * 2 + (core ^ side)) * m + begin + i, step)
             high, low = split(l_ref[pl.ds(start, step), :])
             share = turned(pair(ref[i : i + step, :]), high, low)
             value = share if value is None else value + share
     refs[-1][...] = value
 
 
-def transposed(shift, sides, inv_factor, pieces, acc):
+def transposed(m, shift, begin, sides, inv_factor, pieces, acc):
     depth = inv_factor.shape[1]
     t = pieces[0].shape[1]
     args = [resident(inv_factor), *pieces] + ([] if acc is None else [acc])
     return pl.pallas_call(
-        functools.partial(transposed_kernel, shift, sides, acc is None),
+        functools.partial(transposed_kernel, m, shift, begin, sides, acc is None),
         in_specs=[local] * len(args),
         out_specs=local,
         out_shape=jax.ShapeDtypeStruct((t, depth), f32),
@@ -327,10 +351,10 @@
     )(*args)
 
 
-def last_kernel(shifts, part, segments, l_ref, acc_ref, *refs):
-    pieces, (keep_ref, send_ref, image) = refs[: len(shifts)], refs[len(shifts) :]
+def last_kernel(m, places, part, segments, l_ref, acc_ref, *refs):
+    pieces, (keep_ref, send_ref, image) = refs[: len(places)], refs[len(places) :]
     chip, core, segment = here(2 * segments)
-    m, depth = pieces[0].shape[0], acc_ref.shape[1]
+    depth = acc_ref.shape[1]
     seg, n = depth // segments, image.shape[1]
     begin, end = cuts(seg)[part]
     bands = [(u * seg + begin, u * seg + end) for u in range(segments)]
@@ -338,9 +362,10 @@
     pairs = [pair(ref[...]) for ref in pieces]
     for u, (low_edge, high_edge) in enumerate(bands if apart else [(0, depth)]):
         value = acc_ref[:, low_edge:high_edge]
-        for shift, values in zip(shifts, pairs):
-            start = pl.multiple_of(((chip ^ shift) * 2 + 1 - core) * m, m)
-            high, low = split(l_ref[pl.ds(start, m), low_edge:high_edge])
+        for (shift, first), values in zip(places, pairs):
+            count = values.shape[0]
+            start = pl.multiple_of(((chip ^ shift) * 2 + 1 - core) * m + first, count)
+            high, low = split(l_ref[pl.ds(start, count), low_edge:high_edge])
             value += turned(values, high, low)
         value = value.T
         if apart:
@@ -354,13 +379,13 @@
         ref[(u % half) * n : (u % half + 1) * n, :] = image[segment ^ u]
 
 
-def last_transposed(part, segments, inv_factor, pieces, acc):
+def last_transposed(m, part, segments, inv_factor, pieces, acc):
     t, depth = acc.shape
     begin, end = cuts(depth // segments)[part]
     out = jax.ShapeDtypeStruct((segments // 2 * (end - begin), t), f32)
-    args = [resident(inv_factor), acc, *[piece for _, piece in pieces]]
-    return pl.pallas_call(
-        functools.partial(last_kernel, [shift for shift, _ in pieces], part, segments),
+    args = [resident(inv_factor), acc, *[piece for _, _, piece in pieces]]
+    return pl.pallas_call(
+        functools.partial(last_kernel, m, [piece[:2] for piece in pieces], part, segments),
         in_specs=[local] * len(args),
         out_specs=(local, local),
         out_shape=(out, out),
@@ -445,19 +470,31 @@
     place = jnp.stack(here(n_cols)).astype(jnp.int32)
     order = list(range(1, chips))
 
+    def gather(own, held=(), first=()):
+        if chips != 4:
+            return first, [(i, 0, swap(own, "rows", 2 * i)) for i in order]
+        half = own.shape[0] // 2
+        x, y = swap(own, "rows", 2), swap(own, "rows", 4)
+        x, first = lax.optimization_barrier((x, first))
+        through_y = swap(cut(x, half, half, held), "rows", 4)
+        through_x = swap(cut(y, 0, half, held), "rows", 2)
+        return first, [(1, 0, x), (2, 0, y), (3, half, through_y), (3, 0, through_x)]
+
     other_points = swap(points, "rows", 1)
-    keep, send = forward(inv_factor, direction, residual, chips)
-    m, t = keep.shape[1] - PAD, keep.shape[2]
-    totals = add([keep, swap(send, "rows", 1)], [(m + PAD, t)] * chips)
-    got = [swap(totals[i], "rows", 2 * i) for i in order]
-    mapped, norms = add([totals[0], *got], [(m, t), (PAD, t)])
+    keep, send = forward(inv_factor, direction, residual, chips, False)
+    m, t = send.shape[1] - PAD, send.shape[2]
+    part, *totals = add([keep, swap(send, "rows", 1)], [(m + PAD, t)] * chips)
+    got = [swap(totals[i - 1], "rows", 2 * i) for i in order]
+    direction, part = lax.optimization_barrier((direction, part))
+    (keep,) = forward(inv_factor, direction, residual, chips, True)
+    mapped, norms = add([keep[0], part, *got], [(m, t), (PAD, t)])
     high, low = gaussian(place, points, other_points, centers, chips, segments)
     mapped, high, low = lax.optimization_barrier((mapped, high, low))
 
-    arrived = [(0, mapped)] + [(i, swap(mapped, "rows", 2 * i)) for i in order]
+    arrived = [(0, 0, mapped), *gather(mapped)[1]]
     acc = None
-    for j, (shift, piece) in enumerate(arrived):
-        acc = predict(shift, high, low, piece, acc, j == chips - 1)
+    for j, (shift, begin, piece) in enumerate(arrived):
+        acc = predict(shift, begin, high, low, piece, acc, j == len(arrived) - 1)
     keep, send = acc
     part = keep + swap(send, "rows", 1)
     for mask in halving:
@@ -479,17 +516,16 @@
         got.append(swap(piece, "rows", 2 * shift) if shift else piece)
     own, pred_norm = add([got[-1], *got[:-1]], [(m, t), (PAD, t)], (inv_factor,))
 
-    arrived = [(i, swap(own, "rows", 2 * i)) for i in order]
-    acc = transposed(0, (0, 1), inv_factor, [own, swap(own, "rows", 1)], None)
+    acc = transposed(m, 0, 0, (0, 1), inv_factor, [own, swap(own, "rows", 1)], None)
+    acc, arrived = gather(own, (inv_factor,), acc)
     late = []
-    for shift, piece in arrived:
+    for shift, begin, piece in arrived:
         piece, acc = lax.optimization_barrier((piece, acc))
-        other = swap(piece, "rows", 1)
-        acc = transposed(shift, (0,), inv_factor, [piece], acc)
-        late.append((shift, other))
+        late.append((shift, begin, swap(piece, "rows", 1)))
+        acc = transposed(m, shift, begin, (0,), inv_factor, [piece], acc)
     pieces, norm_next, step_one, step_two, done = [], None, (), (), ()
     for c, (begin, _) in enumerate(cuts(residual.shape[0] // segments)):
-        image, send = last_transposed(c, segments, inv_factor, late, acc)
+        image, send = last_transposed(m, c, segments, inv_factor, late, acc)
         send, step_one = lax.optimization_barrier((send, step_one))
         step_one = swap(send, "cols", masks[0])
         image = image + step_one

time: 158 us -> 155 us (0.981)
  waiting for transfers between devices: 59.9 us -> 50 us
  Pallas kernels: 38.4 us -> 42.8 us
  starting transfers between devices: 35.9 us -> 40.2 us
  local copies, waits for them, and re-layouts: 12.8 us -> 10.6 us
    ppermute x30 -> x33, waiting for transfers between devices: 59.9 us -> 50 us  [swap(): return lax.ppermute(x, axis, [(i, i ^ mask) for i in range(size)])]
    ppermute x30 -> x33, starting transfers between devices: 35.9 us -> 40.2 us  [swap(): return lax.ppermute(x, axis, [(i, i ^ mask) for i in range(size)])]
    pallas_call x11 -> x18, Pallas kernels: 27.2 us -> 30.5 us  [the longest x2 16.7 us: forward(): pl.pallas_call(functools.partial(forward_kernel, chips, begin, end, slots...]
    unnamed x12 -> x10, local copies, waits for them, and re-layouts: 12.8 us -> 10.6 us
  transfers between devices with their start and end apart: 30 -> 33, of which waited for: 19 -> 20; matrix products, arithmetic and copies ran while one was open for 1% -> 1% of each run, Pallas kernels for 12% -> 16%
where the time goes in v5:
time: 155 us
  waiting for transfers between devices  50 us (32%)
  Pallas kernels  42.8 us (28%)
  starting transfers between devices  40.2 us (26%)
  local copies, waits for them, and re-layouts  10.6 us (7%)
  blocking collectives  8.88 us (6%)
    ppermute x33, waiting for transfers between devices, swap(): return lax.ppermute(x, axis, [(i, i ^ mask) for i in range(size)])  50 us
    ppermute x33, starting transfers between devices, swap(): return lax.ppermute(x, axis, [(i, i ^ mask) for i in range(size)])  40.2 us
    pallas_call x2, Pallas kernels, forward(): pl.pallas_call(functools.partial(forward_kernel, chips, begin, end, slots...  16.7 us
    unnamed x10, local copies, waits for them, and re-layouts  10.6 us
    all_gather x1, blocking collectives, body(): norm_next = jnp.sum(lax.all_gather(norm_next, 'rows'), axis=0)  8.88 us
    pallas_call x1, Pallas kernels, gaussian(): pl.pallas_call(functools.partial(kernel_kernel, segments), grid_spec=pltp...  7.48 us
    pallas_call x5, Pallas kernels, transposed(): pl.pallas_call(functools.partial(transposed_kernel, m, shift, begin, side...  6.51 us
    pallas_call x2, Pallas kernels, last_transposed(): pl.pallas_call(functools.partial(last_kernel, m, [piece[:2] for piece in...  4.01 us
  transfers between devices with their start and end apart: 33, of which 20 were waited for; matrix products, arithmetic and copies ran while one was open for 1% of the time, Pallas kernels for 16%

profile of v5, /device:TPU:0, one launch (start us, length us, event | category | flops | bytes accessed | tf_op | source)
XLA Modules:
  0.0 154.7 jit_solution(9128444423180255157)
XLA Ops:
  0.6 12.3 %shard_map.85 = (f32[3,520,128]{2,1,0:T(8,128)S(1)}, f32[4,520,128]{2,1,0:T(8,128)S(1)}) custom-call(f32[4096,2048]{1,0:T(8,128)} %l_ref.17, f32[2048,128]{1,0:T(8,128)} %refs_4_.2, f32[2048,128]{1,0:T(8,128)} %r_ref.7), custom_call_target="tpu_custom_call" | custom-call | flops 1 | bytes 1 | tf_op jit(solution)/shard_map/pallas_call | solution.py:146
  13.5 2.2 %collective-permute-done.refs_1_ = f32[4,520,128]{2,1,0:T(8,128)S(1)} collective-permute-done((f32[4,520,128]{2,1,0:T(8,128)S(1)}, f32[4,520,128]{2,1,0:T(8,128)S(1)}, u32[]{:S(2)}, u32[]{:S(2)}) %collective-permute-start) | collective-permute-done | bytes 1064992 | tf_op jit(solution)/shard_map/ppermute | solution.py:468
  15.9 2.9 %collective-permute-start.1 = (f32[520,128]{1,0:T(8,128)S(1)}, f32[520,128]{1,0:T(8,128)S(1)}, u32[]{:S(2)}, u32[]{:S(2)}) collective-permute-start(f32[520,128]{1,0:T(8,128)S(1)} %get-tuple-element.52), channel_id=1, source_target_pairs={{0,8},{4,12},{8,0},{12,4},{16,24},{20,28},{24,16},{28,20},{1,9},{5... | collective-permute-start | bytes 798728 | tf_op jit(solution)/shard_map/ppermute | solution.py:468
  20.4 7.5 %shard_map.89 = (bf16[4,512,1024]{2,1,0:T(8,128)(2,1)S(1)}, bf16[4,512,1024]{2,1,0:T(8,128)(2,1)S(1)}) custom-call(s32[3]{0:T(128)S(1)} %pad_add_fusion.place, f32[512,256]{1,0:T(8,128)S(1)} %copy-done.3, f32[512,256]{1,0:T(8,128)S(1)} %collective-permute-done.4.other_ref, f32[4096,256]{1,0:T(8,128)} %c_ref.1), custom_call_target="tpu_custom_call" | custom-call | flops 1 | bytes 1 | tf_op jit(solution)/shard_map/pallas_call | solution.py:235
  27.9 4.5 %shard_map.87 = f32[1,520,128]{2,1,0:T(8,128)S(1)} custom-call(f32[4096,2048]{1,0:T(8,128)} %l_ref.17, f32[2048,128]{1,0:T(8,128)} %refs_4_.2, f32[2048,128]{1,0:T(8,128)} %r_ref.7), custom_call_target="tpu_custom_call" | custom-call | flops 1 | bytes 1 | tf_op jit(solution)/shard_map/pallas_call | solution.py:146
  32.8 1.7 %collective-permute-start.7 = (f32[512,128]{1,0:T(8,128)S(1)}, f32[512,128]{1,0:T(8,128)S(1)}, u32[]{:S(2)}, u32[]{:S(2)}) collective-permute-start(f32[512,128]{1,0:T(8,128)S(1)} %get-tuple-element.61.piece_ref), channel_id=1, source_target_pairs={{0,8},{4,12},{8,0},{12,4},{16,24},{20,28},{24,16},{28,20},{1,9},{5... | collective-permute-start | bytes 786440 | tf_op jit(solution)/shard_map/ppermute | solution.py:468
  36.1 4.3 %collective-permute-done.7.x_ref.piece_ref = f32[512,128]{1,0:T(8,128)S(1)} collective-permute-done((f32[512,128]{1,0:T(8,128)S(1)}, f32[512,128]{1,0:T(8,128)S(1)}, u32[]{:S(2)}, u32[]{:S(2)}) %collective-permute-start.7) | collective-permute-done | bytes 262176 | tf_op jit(solution)/shard_map/ppermute | solution.py:468
  40.4 1.8 %collective-permute-start.8 = (f32[256,128]{1,0:T(8,128)S(1)}, f32[256,128]{1,0:T(8,128)S(1)}, u32[]{:S(2)}, u32[]{:S(2)}) collective-permute-start(f32[256,128]{1,0:T(8,128)S(1)} %shard_map.91), channel_id=1, source_target_pairs={{0,16},{4,20},{8,24},{12,28},{16,0},{20,4},{24,8},{28,12},{1,17},{... | collective-permute-start | bytes 393224 | tf_op jit(solution)/shard_map/ppermute | solution.py:468
  51.1 4.0 %collective-permute-done.10 = f32[256,128]{1,0:T(8,128)S(1)} collective-permute-done((f32[256,128]{1,0:T(8,128)S(1)}, f32[256,128]{1,0:T(8,128)S(1)}, u32[]{:S(2)}, u32[]{:S(2)}) %collective-permute-start.10) | collective-permute-done | bytes 131104 | tf_op jit(solution)/shard_map/ppermute | solution.py:468
  55.0 3.7 %collective-permute-start.11 = (f32[256,128]{1,0:T(8,128)S(1)}, f32[256,128]{1,0:T(8,128)S(1)}, u32[]{:S(2)}, u32[]{:S(2)}) collective-permute-start(f32[256,128]{1,0:T(8,128)S(1)} %slice_add_fusion), channel_id=1, source_target_pairs={{0,3},{1,2},{2,1},{3,0},{4,7},{5,6},{6,5},{7,4},{8,11},{9,10},{10,... | collective-permute-start | bytes 393224 | tf_op jit(solution)/shard_map/ppermute | solution.py:468
  58.7 3.2 %collective-permute-done.11 = f32[256,128]{1,0:T(8,128)S(1)} collective-permute-done((f32[256,128]{1,0:T(8,128)S(1)}, f32[256,128]{1,0:T(8,128)S(1)}, u32[]{:S(2)}, u32[]{:S(2)}) %collective-permute-start.11) | collective-permute-done | bytes 131104 | tf_op jit(solution)/shard_map/ppermute | solution.py:468
  62.0 2.3 %collective-permute-start.12 = (f32[256,128]{1,0:T(8,128)S(1)}, f32[256,128]{1,0:T(8,128)S(1)}, u32[]{:S(2)}, u32[]{:S(2)}) collective-permute-start(f32[256,128]{1,0:T(8,128)S(1)} %add.32), channel_id=1, source_target_pairs={{0,1},{1,0},{2,3},{3,2},{4,5},{5,4},{6,7},{7,6},{8,9},{9,8},{10,11... | collective-permute-start | bytes 393224 | tf_op jit(solution)/shard_map/ppermute | solution.py:468
  64.3 2.9 %collective-permute-done.12 = f32[256,128]{1,0:T(8,128)S(1)} collective-permute-done((f32[256,128]{1,0:T(8,128)S(1)}, f32[256,128]{1,0:T(8,128)S(1)}, u32[]{:S(2)}, u32[]{:S(2)}) %collective-permute-start.12) | collective-permute-done | bytes 131104 | tf_op jit(solution)/shard_map/ppermute | solution.py:468
  74.6 10.5 %copy-done = f32[4096,2048]{1,0:T(8,128)S(1)} copy-done((f32[4096,2048]{1,0:T(8,128)S(1)}, f32[4096,2048]{1,0:T(8,128)}, u32[]{:S(2)}) %copy-start) | copy-done | bytes 33554456
  88.4 2.4 %shard_map.103.refs_1_ = f32[128,2048]{1,0:T(8,128)S(1)} custom-call(f32[4096,2048]{1,0:T(8,128)S(1)} %copy-done, f32[512,128]{1,0:T(8,128)S(1)} %get-tuple-element.68.refs_0_, f32[512,128]{1,0:T(8,128)S(1)} %collective-permute-done.20.refs_1_), custom_call_target="tpu_custom_call" | custom-call | flops 1 | bytes 1 | tf_op jit(solution)/shard_map/pallas_call | solution.py:344
  90.8 4.2 %collective-permute-done.19.x_ref.refs_0_ = f32[512,128]{1,0:T(8,128)S(1)} collective-permute-done((f32[512,128]{1,0:T(8,128)S(1)}, f32[512,128]{1,0:T(8,128)S(1)}, u32[]{:S(2)}, u32[]{:S(2)}) %collective-permute-start.19) | collective-permute-done | bytes 262176 | tf_op jit(solution)/shard_map/ppermute | solution.py:468
  104.1 2.1 %collective-permute-start.26 = (f32[256,128]{1,0:T(8,128)S(1)}, f32[256,128]{1,0:T(8,128)S(1)}, u32[]{:S(2)}, u32[]{:S(2)}) collective-permute-start(f32[256,128]{1,0:T(8,128)S(1)} %get-tuple-element.79), channel_id=1, source_target_pairs={{0,1},{1,0},{2,3},{3,2},{4,5},{5,4},{6,7},{7,6},{8,9},{9,8},{10,11... | collective-permute-start | bytes 393224 | tf_op jit(solution)/shard_map/ppermute | solution.py:468
  106.2 2.8 %shard_map.111 = (f32[768,128]{1,0:T(8,128)S(1)}, f32[768,128]{1,0:T(8,128)S(1)}) custom-call(f32[4096,2048]{1,0:T(8,128)S(1)} %copy-done, f32[128,2048]{1,0:T(8,128)S(1)} %shard_map.108.acc_ref, f32[512,128]{1,0:T(8,128)S(1)} %collective-permute-done.22.refs_0_, f32[512,128]{1,0:T(8,128)S(1)} %collective-permute-done.23.refs_1_, ...), custom_call_target="tpu_custom_call" | custom-call | flops 1 | bytes 1 | tf_op jit(solution)/shard_map/pallas_call | solution.py:387
  111.9 2.8 %collective-permute-start.27 = (f32[256,128]{1,0:T(8,128)S(1)}, f32[256,128]{1,0:T(8,128)S(1)}, u32[]{:S(2)}, u32[]{:S(2)}) collective-permute-start(f32[256,128]{1,0:T(8,128)S(1)} %add.35), channel_id=1, source_target_pairs={{0,3},{1,2},{2,1},{3,0},{4,7},{5,6},{6,5},{7,4},{8,11},{9,10},{10,... | collective-permute-start | bytes 393224 | tf_op jit(solution)/shard_map/ppermute | solution.py:468
  114.7 6.5 %collective-permute-done.29 = f32[768,128]{1,0:T(8,128)S(1)} collective-permute-done((f32[768,128]{1,0:T(8,128)S(1)}, f32[768,128]{1,0:T(8,128)S(1)}, u32[]{:S(2)}, u32[]{:S(2)}) %collective-permute-start.29) | collective-permute-done | bytes 393248 | tf_op jit(solution)/shard_map/ppermute | solution.py:468
  121.3 4.7 %collective-permute-done.27 = f32[256,128]{1,0:T(8,128)S(1)} collective-permute-done((f32[256,128]{1,0:T(8,128)S(1)}, f32[256,128]{1,0:T(8,128)S(1)}, u32[]{:S(2)}, u32[]{:S(2)}) %collective-permute-start.27) | collective-permute-done | bytes 131104 | tf_op jit(solution)/shard_map/ppermute | solution.py:468
  127.2 11.2 %collective-permute-done.30 = f32[768,128]{1,0:T(8,128)S(1)} collective-permute-done((f32[768,128]{1,0:T(8,128)S(1)}, f32[768,128]{1,0:T(8,128)S(1)}, u32[]{:S(2)}, u32[]{:S(2)}) %collective-permute-start.30) | collective-permute-done | bytes 393248 | tf_op jit(solution)/shard_map/ppermute | solution.py:468
  139.0 3.8 %collective-permute-start.32 = (f32[8,128]{1,0:T(8,128)S(1)}, f32[8,128]{1,0:T(8,128)S(1)}, u32[]{:S(2)}, u32[]{:S(2)}) collective-permute-start(f32[8,128]{1,0:T(8,128)S(1)} %get-tuple-element.88), channel_id=1, source_target_pairs={{0,1},{1,0},{2,3},{3,2},{4,5},{5,4},{6,7},{7,6},{8,9},{9,8},{10,11... | collective-permute-start | bytes 12296 | tf_op jit(solution)/shard_map/ppermute | solution.py:468
  144.4 8.9 %all-gather = f32[64,128]{1,0:T(8,128)S(1)} all-gather(f32[8,128]{1,0:T(8,128)S(1)} %add.39), channel_id=2, replica_groups=mesh['rows'=8,'cols'=4] {'rows'}, dimensions={0}, use_global_device_ids=true | all-gather | bytes 36864 | tf_op jit(solution)/shard_map/all_gather | solution.py:549
  (96 shorter events, 40.5 us)
Async XLA Ops:
  13.5 7.0 %collective-permute-start.4 = (f32[512,256]{1,0:T(8,128)S(1)}, f32[512,256]{1,0:T(8,128)S(1)}, u32[]{:S(2)}, u32[]{:S(2)}) collective-permute-start(f32[512,256]{1,0:T(8,128)S(1)} %copy-done.3), channel_id=1, source_target_pairs={{0,4},{4,0},{8,12},{12,8},{16,20},{20,16},{24,28},{28,24},{1,5},{5... | collective-permute-start | bytes 1572872 | tf_op jit(solution)/shard_map/ppermute | solution.py:468
  15.9 16.5 %collective-permute-start.1 = (f32[520,128]{1,0:T(8,128)S(1)}, f32[520,128]{1,0:T(8,128)S(1)}, u32[]{:S(2)}, u32[]{:S(2)}) collective-permute-start(f32[520,128]{1,0:T(8,128)S(1)} %get-tuple-element.52), channel_id=1, source_target_pairs={{0,8},{4,12},{8,0},{12,4},{16,24},{20,28},{24,16},{28,20},{1,9},{5... | collective-permute-start | bytes 798728 | tf_op jit(solution)/shard_map/ppermute | solution.py:468
  18.8 13.9 %collective-permute-start.2 = (f32[520,128]{1,0:T(8,128)S(1)}, f32[520,128]{1,0:T(8,128)S(1)}, u32[]{:S(2)}, u32[]{:S(2)}) collective-permute-start(f32[520,128]{1,0:T(8,128)S(1)} %get-tuple-element.53), channel_id=1, source_target_pairs={{0,16},{4,20},{8,24},{12,28},{16,0},{20,4},{24,8},{28,12},{1,17},{... | collective-permute-start | bytes 798728 | tf_op jit(solution)/shard_map/ppermute | solution.py:468
  20.3 12.3 %collective-permute-start.3 = (f32[520,128]{1,0:T(8,128)S(1)}, f32[520,128]{1,0:T(8,128)S(1)}, u32[]{:S(2)}, u32[]{:S(2)}) collective-permute-start(f32[520,128]{1,0:T(8,128)S(1)} %get-tuple-element.54), channel_id=1, source_target_pairs={{0,24},{4,28},{8,16},{12,20},{16,8},{20,12},{24,0},{28,4},{1,25},{... | collective-permute-start | bytes 798728 | tf_op jit(solution)/shard_map/ppermute | solution.py:468
  32.8 7.6 %collective-permute-start.7 = (f32[512,128]{1,0:T(8,128)S(1)}, f32[512,128]{1,0:T(8,128)S(1)}, u32[]{:S(2)}, u32[]{:S(2)}) collective-permute-start(f32[512,128]{1,0:T(8,128)S(1)} %get-tuple-element.61.piece_ref), channel_id=1, source_target_pairs={{0,8},{4,12},{8,0},{12,4},{16,24},{20,28},{24,16},{28,20},{1,9},{5... | collective-permute-start | bytes 786440 | tf_op jit(solution)/shard_map/ppermute | solution.py:468
  34.5 7.6 %collective-permute-start.5 = (f32[512,128]{1,0:T(8,128)S(1)}, f32[512,128]{1,0:T(8,128)S(1)}, u32[]{:S(2)}, u32[]{:S(2)}) collective-permute-start(f32[512,128]{1,0:T(8,128)S(1)} %get-tuple-element.61.piece_ref), channel_id=1, source_target_pairs={{0,16},{4,20},{8,24},{12,28},{16,0},{20,4},{24,8},{28,12},{1,17},{... | collective-permute-start | bytes 786440 | tf_op jit(solution)/shard_map/ppermute | solution.py:468
  40.4 5.6 %collective-permute-start.8 = (f32[256,128]{1,0:T(8,128)S(1)}, f32[256,128]{1,0:T(8,128)S(1)}, u32[]{:S(2)}, u32[]{:S(2)}) collective-permute-start(f32[256,128]{1,0:T(8,128)S(1)} %shard_map.91), channel_id=1, source_target_pairs={{0,16},{4,20},{8,24},{12,28},{16,0},{20,4},{24,8},{28,12},{1,17},{... | collective-permute-start | bytes 393224 | tf_op jit(solution)/shard_map/ppermute | solution.py:468
  42.2 5.0 %collective-permute-start.6 = (f32[256,128]{1,0:T(8,128)S(1)}, f32[256,128]{1,0:T(8,128)S(1)}, u32[]{:S(2)}, u32[]{:S(2)}) collective-permute-start(f32[256,128]{1,0:T(8,128)S(1)} %shard_map.90), channel_id=1, source_target_pairs={{0,8},{4,12},{8,0},{12,4},{16,24},{20,28},{24,16},{28,20},{1,9},{5... | collective-permute-start | bytes 393224 | tf_op jit(solution)/shard_map/ppermute | solution.py:468
  49.4 5.6 %collective-permute-start.10 = (f32[256,128]{1,0:T(8,128)S(1)}, f32[256,128]{1,0:T(8,128)S(1)}, u32[]{:S(2)}, u32[]{:S(2)}) collective-permute-start(f32[256,128]{1,0:T(8,128)S(1)} %slice.21), channel_id=1, source_target_pairs={{0,1},{1,0},{2,3},{3,2},{4,5},{5,4},{6,7},{7,6},{8,9},{9,8},{10,11... | collective-permute-start | bytes 393224 | tf_op jit(solution)/shard_map/ppermute | solution.py:468
  55.0 6.9 %collective-permute-start.11 = (f32[256,128]{1,0:T(8,128)S(1)}, f32[256,128]{1,0:T(8,128)S(1)}, u32[]{:S(2)}, u32[]{:S(2)}) collective-permute-start(f32[256,128]{1,0:T(8,128)S(1)} %slice_add_fusion), channel_id=1, source_target_pairs={{0,3},{1,2},{2,1},{3,0},{4,7},{5,6},{6,5},{7,4},{8,11},{9,10},{10,... | collective-permute-start | bytes 393224 | tf_op jit(solution)/shard_map/ppermute | solution.py:468
  62.0 5.3 %collective-permute-start.12 = (f32[256,128]{1,0:T(8,128)S(1)}, f32[256,128]{1,0:T(8,128)S(1)}, u32[]{:S(2)}, u32[]{:S(2)}) collective-permute-start(f32[256,128]{1,0:T(8,128)S(1)} %add.32), channel_id=1, source_target_pairs={{0,1},{1,0},{2,3},{3,2},{4,5},{5,4},{6,7},{7,6},{8,9},{9,8},{10,11... | collective-permute-start | bytes 393224 | tf_op jit(solution)/shard_map/ppermute | solution.py:468
  71.0 14.8 %collective-permute-start.16 = (f32[520,128]{1,0:T(8,128)S(1)}, f32[520,128]{1,0:T(8,128)S(1)}, u32[]{:S(2)}, u32[]{:S(2)}) collective-permute-start(f32[520,128]{1,0:T(8,128)S(1)} %shard_map.100), channel_id=1, source_target_pairs={{0,24},{4,28},{8,16},{12,20},{16,8},{20,12},{24,0},{28,4},{1,25},{... | collective-permute-start | bytes 798728 | tf_op jit(solution)/shard_map/ppermute | solution.py:468
  72.5 13.6 %collective-permute-start.15 = (f32[520,128]{1,0:T(8,128)S(1)}, f32[520,128]{1,0:T(8,128)S(1)}, u32[]{:S(2)}, u32[]{:S(2)}) collective-permute-start(f32[520,128]{1,0:T(8,128)S(1)} %shard_map.99), channel_id=1, source_target_pairs={{0,16},{4,20},{8,24},{12,28},{16,0},{20,4},{24,8},{28,12},{1,17},{... | collective-permute-start | bytes 798728 | tf_op jit(solution)/shard_map/ppermute | solution.py:468
  74.0 12.1 %collective-permute-start.14 = (f32[520,128]{1,0:T(8,128)S(1)}, f32[520,128]{1,0:T(8,128)S(1)}, u32[]{:S(2)}, u32[]{:S(2)}) collective-permute-start(f32[520,128]{1,0:T(8,128)S(1)} %get-tuple-element.66), channel_id=1, source_target_pairs={{0,8},{4,12},{8,0},{12,4},{16,24},{20,28},{24,16},{28,20},{1,9},{5... | collective-permute-start | bytes 798728 | tf_op jit(solution)/shard_map/ppermute | solution.py:468
  86.3 8.7 %collective-permute-start.19 = (f32[512,128]{1,0:T(8,128)S(1)}, f32[512,128]{1,0:T(8,128)S(1)}, u32[]{:S(2)}, u32[]{:S(2)}) collective-permute-start(f32[512,128]{1,0:T(8,128)S(1)} %get-tuple-element.68.refs_0_), channel_id=1, source_target_pairs={{0,8},{4,12},{8,0},{12,4},{16,24},{20,28},{24,16},{28,20},{1,9},{5... | collective-permute-start | bytes 786440 | tf_op jit(solution)/shard_map/ppermute | solution.py:468
  87.8 8.5 %collective-permute-start.17 = (f32[512,128]{1,0:T(8,128)S(1)}, f32[512,128]{1,0:T(8,128)S(1)}, u32[]{:S(2)}, u32[]{:S(2)}) collective-permute-start(f32[512,128]{1,0:T(8,128)S(1)} %get-tuple-element.68.refs_0_), channel_id=1, source_target_pairs={{0,16},{4,20},{8,24},{12,28},{16,0},{20,4},{24,8},{28,12},{1,17},{... | collective-permute-start | bytes 786440 | tf_op jit(solution)/shard_map/ppermute | solution.py:468
  95.0 5.4 %collective-permute-start.21 = (f32[256,128]{1,0:T(8,128)S(1)}, f32[256,128]{1,0:T(8,128)S(1)}, u32[]{:S(2)}, u32[]{:S(2)}) collective-permute-start(f32[256,128]{1,0:T(8,128)S(1)} %shard_map.104), channel_id=1, source_target_pairs={{0,16},{4,20},{8,24},{12,28},{16,0},{20,4},{24,8},{28,12},{1,17},{... | collective-permute-start | bytes 393224 | tf_op jit(solution)/shard_map/ppermute | solution.py:468
  104.1 6.0 %collective-permute-start.26 = (f32[256,128]{1,0:T(8,128)S(1)}, f32[256,128]{1,0:T(8,128)S(1)}, u32[]{:S(2)}, u32[]{:S(2)}) collective-permute-start(f32[256,128]{1,0:T(8,128)S(1)} %get-tuple-element.79), channel_id=1, source_target_pairs={{0,1},{1,0},{2,3},{3,2},{4,5},{5,4},{6,7},{7,6},{8,9},{9,8},{10,11... | collective-permute-start | bytes 393224 | tf_op jit(solution)/shard_map/ppermute | solution.py:468
  110.1 11.1 %collective-permute-start.29 = (f32[768,128]{1,0:T(8,128)S(1)}, f32[768,128]{1,0:T(8,128)S(1)}, u32[]{:S(2)}, u32[]{:S(2)}) collective-permute-start(f32[768,128]{1,0:T(8,128)S(1)} %get-tuple-element.83), channel_id=1, source_target_pairs={{0,1},{1,0},{2,3},{3,2},{4,5},{5,4},{6,7},{7,6},{8,9},{9,8},{10,11... | collective-permute-start | bytes 1179656 | tf_op jit(solution)/shard_map/ppermute | solution.py:468
  111.9 14.1 %collective-permute-start.27 = (f32[256,128]{1,0:T(8,128)S(1)}, f32[256,128]{1,0:T(8,128)S(1)}, u32[]{:S(2)}, u32[]{:S(2)}) collective-permute-start(f32[256,128]{1,0:T(8,128)S(1)} %add.35), channel_id=1, source_target_pairs={{0,3},{1,2},{2,1},{3,0},{4,7},{5,6},{6,5},{7,4},{8,11},{9,10},{10,... | collective-permute-start | bytes 393224 | tf_op jit(solution)/shard_map/ppermute | solution.py:468
  126.0 12.5 %collective-permute-start.30 = (f32[768,128]{1,0:T(8,128)S(1)}, f32[768,128]{1,0:T(8,128)S(1)}, u32[]{:S(2)}, u32[]{:S(2)}) collective-permute-start(f32[768,128]{1,0:T(8,128)S(1)} %add.37), channel_id=1, source_target_pairs={{0,3},{1,2},{2,1},{3,0},{4,7},{5,6},{6,5},{7,4},{8,11},{9,10},{10,... | collective-permute-start | bytes 1179656 | tf_op jit(solution)/shard_map/ppermute | solution.py:468
  127.1 11.7 %collective-permute-start.28 = (f32[256,128]{1,0:T(8,128)S(1)}, f32[256,128]{1,0:T(8,128)S(1)}, u32[]{:S(2)}, u32[]{:S(2)}) collective-permute-start(f32[256,128]{1,0:T(8,128)S(1)} %get-tuple-element.80.refs_0_), channel_id=1, source_target_pairs={{0,1},{1,0},{2,3},{3,2},{4,5},{5,4},{6,7},{7,6},{8,9},{9,8},{10,11... | collective-permute-start | bytes 393224 | tf_op jit(solution)/shard_map/ppermute | solution.py:468
  139.0 5.4 %collective-permute-start.32 = (f32[8,128]{1,0:T(8,128)S(1)}, f32[8,128]{1,0:T(8,128)S(1)}, u32[]{:S(2)}, u32[]{:S(2)}) collective-permute-start(f32[8,128]{1,0:T(8,128)S(1)} %get-tuple-element.88), channel_id=1, source_target_pairs={{0,1},{1,0},{2,3},{3,2},{4,5},{5,4},{6,7},{7,6},{8,9},{9,8},{10,11... | collective-permute-start | bytes 12296 | tf_op jit(solution)/shard_map/ppermute | solution.py:468
  142.8 10.5 %collective-permute-start.31 = (f32[768,128]{1,0:T(8,128)S(1)}, f32[768,128]{1,0:T(8,128)S(1)}, u32[]{:S(2)}, u32[]{:S(2)}) collective-permute-start(f32[768,128]{1,0:T(8,128)S(1)} %get-tuple-element.87.refs_2_), channel_id=1, source_target_pairs={{0,1},{1,0},{2,3},{3,2},{4,5},{5,4},{6,7},{7,6},{8,9},{9,8},{10,11... | collective-permute-start | bytes 1179656 | tf_op jit(solution)/shard_map/ppermute | solution.py:468
  (14 other events, 127.9 us)

commit v6 on v5

--- a/solution.py
+++ b/solution.py
@@ -286,40 +286,42 @@
     )(*args)
 
 
-def back_kernel(shift, first, high_ref, low_ref, *refs):
-    refs = refs[1:] if shift == 0 else refs
-    if first:
-        own_ref, other_ref, out_ref, pairs, norms = refs
-        half = own_ref.shape[0]
-        norms[...] = jnp.zeros_like(norms)
-        a, b = own_ref[...], other_ref[...]
-        pairs[:half, :] = pair(a)
-        pairs[half:, :] = pair(b)
-        norms[0:1, :] = jnp.sum(a * a, axis=0, keepdims=True) + jnp.sum(b * b, axis=0, keepdims=True)
-    else:
-        pairs, norms, out_ref = refs
+def back_kernel(shifts, last, high_ref, low_ref, own_ref, *refs):
+    half, n = own_ref.shape
     m = high_ref.shape[1]
-    n = out_ref.shape[1]
-    both = jnp.dot(high_ref[shift], pairs[...], preferred_element_type=f32)
-    both += jnp.dot(low_ref[shift], pairs[...], preferred_element_type=f32)
-    out_ref[:m, :] = both[:, :n] + both[:, n:]
-    out_ref[m:, :] = norms[...]
-
-
-def back_product(shift, high, low, sources, first, held=()):
-    _, m, n = high.shape
-    t = sources[1].shape[1]
-    out = (jax.ShapeDtypeStruct((m + PAD, t), f32),)
-    if first:
-        out += (jax.ShapeDtypeStruct((n, 2 * t), bf16), jax.ShapeDtypeStruct((PAD, t), f32))
-    return pl.pallas_call(
-        functools.partial(back_kernel, shift, first),
-        in_specs=[local] * (4 + len(held)),
+    outs = refs[-len(shifts) :]
+    begin = half if last else 0
+    pairs = pair(refs[0][...] if last else own_ref[...])
+    if last:
+        norm = sum(
+            jnp.sum(ref[...] * ref[...], axis=0, keepdims=True) for ref in (own_ref, refs[0])
+        )
+    for i, (shift, out_ref) in enumerate(zip(shifts, outs)):
+        both = jnp.dot(high_ref[shift, :, begin : begin + half], pairs, preferred_element_type=f32)
+        both += jnp.dot(low_ref[shift, :, begin : begin + half], pairs, preferred_element_type=f32)
+        value = both[:, :n] + both[:, n:]
+        if last:
+            value += refs[1 + i][...]
+            out_ref[m:, :] = jnp.zeros((PAD, n), f32)
+            out_ref[m : m + 1, :] = norm
+        out_ref[:m, :] = value
+
+
+def back_product(shifts, high, low, own, other=None, before=(), held=()):
+    m = high.shape[1]
+    t = own.shape[1]
+    last = other is not None
+    args = [resident(high), resident(low), own, *([other] if last else []), *before]
+    args += map(resident, held)
+    out = (jax.ShapeDtypeStruct((m + PAD if last else m, t), f32),) * len(shifts)
+    return pl.pallas_call(
+        functools.partial(back_kernel, shifts, last),
+        in_specs=[local] * len(args),
         out_specs=(local,) * len(out),
         out_shape=out,
         compiler_params=params(),
-        cost_estimate=cost(8 * m * n * t, 4 * m * n),
-    )(resident(high), resident(low), *map(resident, held), *sources)
+        cost_estimate=cost(),
+    )(*args)
 
 
 def transposed_kernel(m, shift, begin, sides, first, l_ref, *refs):
@@ -426,31 +428,49 @@
 
 def finish_kernel(segments, n_pieces, *refs):
     pieces = refs[:n_pieces]
-    d_ref, norm_ref, next_ref, res_ref, dir_ref = refs[n_pieces:]
-    ratio = next_ref[0:1, :] / norm_ref[0:1, :]
+    d_ref, norm_ref, next_ref, res_ref, dir_ref, new, sems = refs[n_pieces:]
     segment = here(2 * segments)[2]
     seg = d_ref.shape[0] // segments
     each = n_pieces // len(SHARES)
+    places = []
     for c, (begin, end) in enumerate(cuts(seg)):
-        n = end - begin
-        u = 0
+        u, n = 0, end - begin
         for piece in pieces[c * each : (c + 1) * each]:
             for j in range(piece.shape[0] // n):
                 at = pl.ds(pl.multiple_of((segment ^ u) * seg + begin, PAD), n)
-                new = piece[j * n : (j + 1) * n, :]
-                res_ref[at, :] = new
-                dir_ref[at, :] = new + ratio * d_ref[at, :]
+                places.append((piece.at[pl.ds(j * n, n), :], at))
                 u += 1
+    residuals = [
+        pltpu.make_async_copy(rows, res_ref.at[at, :], sems.at[0, i])
+        for i, (rows, at) in enumerate(places)
+    ]
+    directions = [
+        pltpu.make_async_copy(new.at[at, :], dir_ref.at[at, :], sems.at[1, i])
+        for i, (_, at) in enumerate(places)
+    ]
+    for copy in residuals:
+        copy.start()
+    ratio = next_ref[0:1, :] / norm_ref[0:1, :]
+    for (rows, at), copy in zip(places, directions):
+        new[at, :] = rows[...] + ratio * d_ref[at, :]
+        copy.start()
+    for copy in residuals + directions:
+        copy.wait()
 
 
 def finish(pieces, direction, norms, norm_next, segments):
     out = jax.ShapeDtypeStruct(direction.shape, f32)
     args = [*pieces, direction, norms, norm_next]
+    far = pl.BlockSpec(memory_space=pl.ANY)
     return pl.pallas_call(
         functools.partial(finish_kernel, segments, len(pieces)),
         in_specs=[local] * len(args),
-        out_specs=(local, local),
+        out_specs=(far, far),
         out_shape=(out, out),
+        scratch_shapes=[
+            pltpu.VMEM(direction.shape, f32),
+            pltpu.SemaphoreType.DMA((2, segments * len(SHARES))),
+        ],
         compiler_params=params(),
         cost_estimate=cost(),
     )(*args)
@@ -503,17 +523,11 @@
     part = part + swap(part, "cols", last_mask)
     for mask in halving[::-1]:
         part = jnp.concatenate([part, swap(part, "cols", mask)], axis=0)
+    before = back_product((*order, 0), high, low, part)
     other = swap(part, "rows", 1)
-
-    got = []
-    sources, first = (part, other), True
-    for shift in (*order, 0):
-        piece, *rest = back_product(
-            shift, high, low, sources, first, () if shift else (inv_factor,)
-        )
-        if first:
-            sources, first = rest, False
-        got.append(swap(piece, "rows", 2 * shift) if shift else piece)
+    pieces = back_product(order, high, low, part, other, before[:-1])
+    got = [swap(piece, "rows", 2 * i) for i, piece in zip(order, pieces)]
+    got += back_product((0,), high, low, part, other, before[-1:], (inv_factor,))
     own, pred_norm = add([got[-1], *got[:-1]], [(m, t), (PAD, t)], (inv_factor,))
 
     acc = transposed(m, 0, 0, (0, 1), inv_factor, [own, swap(own, "rows", 1)], None)

time: 155 us -> 154 us (level)
  transfers between devices with their start and end apart: 33 -> 33, of which waited for: 20 -> 19; matrix products, arithmetic and copies ran while one was open for 1% -> 1% of each run, Pallas kernels for 16% -> 17%
where the time goes in v6:
time: 154 us
  waiting for transfers between devices  49.5 us (32%)
  Pallas kernels  42.6 us (28%)
  starting transfers between devices  39.6 us (26%)
  local copies, waits for them, and re-layouts  10.6 us (7%)
  blocking collectives  8.96 us (6%)
    ppermute x33, waiting for transfers between devices, swap(): return lax.ppermute(x, axis, [(i, i ^ mask) for i in range(size)])  49.5 us
    ppermute x33, starting transfers between devices, swap(): return lax.ppermute(x, axis, [(i, i ^ mask) for i in range(size)])  39.6 us
    pallas_call x2, Pallas kernels, forward(): pl.pallas_call(functools.partial(forward_kernel, chips, begin, end, slots...  16.7 us
    unnamed x10, local copies, waits for them, and re-layouts  10.6 us
    all_gather x1, blocking collectives, body(): norm_next = jnp.sum(lax.all_gather(norm_next, 'rows'), axis=0)  8.96 us
    pallas_call x1, Pallas kernels, gaussian(): pl.pallas_call(functools.partial(kernel_kernel, segments), grid_spec=pltp...  7.48 us
    pallas_call x5, Pallas kernels, transposed(): pl.pallas_call(functools.partial(transposed_kernel, m, shift, begin, side...  6.5 us
    pallas_call x2, Pallas kernels, last_transposed(): pl.pallas_call(functools.partial(last_kernel, m, [piece[:2] for piece in...  4 us
  transfers between devices with their start and end apart: 33, of which 19 were waited for; matrix products, arithmetic and copies ran while one was open for 1% of the time, Pallas kernels for 17%

profile of v6, /device:TPU:0, one launch (start us, length us, event | category | flops | bytes accessed | tf_op | source)
XLA Modules:
  0.0 153.8 jit_solution(13867274457073988662)
XLA Ops:
  0.6 12.3 %shard_map.85 = (f32[3,520,128]{2,1,0:T(8,128)S(1)}, f32[4,520,128]{2,1,0:T(8,128)S(1)}) custom-call(f32[4096,2048]{1,0:T(8,128)} %l_ref.17, f32[2048,128]{1,0:T(8,128)} %refs_4_.2, f32[2048,128]{1,0:T(8,128)} %r_ref.7), custom_call_target="tpu_custom_call" | custom-call | flops 1 | bytes 1 | tf_op jit(solution)/shard_map/pallas_call | solution.py:146
  13.5 2.2 %collective-permute-done.refs_1_ = f32[4,520,128]{2,1,0:T(8,128)S(1)} collective-permute-done((f32[4,520,128]{2,1,0:T(8,128)S(1)}, f32[4,520,128]{2,1,0:T(8,128)S(1)}, u32[]{:S(2)}, u32[]{:S(2)}) %collective-permute-start) | collective-permute-done | bytes 1064992 | tf_op jit(solution)/shard_map/ppermute | solution.py:488
  15.9 2.9 %collective-permute-start.1 = (f32[520,128]{1,0:T(8,128)S(1)}, f32[520,128]{1,0:T(8,128)S(1)}, u32[]{:S(2)}, u32[]{:S(2)}) collective-permute-start(f32[520,128]{1,0:T(8,128)S(1)} %get-tuple-element.56), channel_id=1, source_target_pairs={{0,8},{4,12},{8,0},{12,4},{16,24},{20,28},{24,16},{28,20},{1,9},{5... | collective-permute-start | bytes 798728 | tf_op jit(solution)/shard_map/ppermute | solution.py:488
  20.4 7.5 %shard_map.89 = (bf16[4,512,1024]{2,1,0:T(8,128)(2,1)S(1)}, bf16[4,512,1024]{2,1,0:T(8,128)(2,1)S(1)}) custom-call(s32[3]{0:T(128)S(1)} %pad_add_fusion.place, f32[512,256]{1,0:T(8,128)S(1)} %copy-done.3, f32[512,256]{1,0:T(8,128)S(1)} %collective-permute-done.4.other_ref, f32[4096,256]{1,0:T(8,128)} %c_ref.1), custom_call_target="tpu_custom_call" | custom-call | flops 1 | bytes 1 | tf_op jit(solution)/shard_map/pallas_call | solution.py:235
  27.9 4.5 %shard_map.87 = f32[1,520,128]{2,1,0:T(8,128)S(1)} custom-call(f32[4096,2048]{1,0:T(8,128)} %l_ref.17, f32[2048,128]{1,0:T(8,128)} %refs_4_.2, f32[2048,128]{1,0:T(8,128)} %r_ref.7), custom_call_target="tpu_custom_call" | custom-call | flops 1 | bytes 1 | tf_op jit(solution)/shard_map/pallas_call | solution.py:146
  32.8 1.7 %collective-permute-start.7 = (f32[512,128]{1,0:T(8,128)S(1)}, f32[512,128]{1,0:T(8,128)S(1)}, u32[]{:S(2)}, u32[]{:S(2)}) collective-permute-start(f32[512,128]{1,0:T(8,128)S(1)} %get-tuple-element.65.piece_ref), channel_id=1, source_target_pairs={{0,8},{4,12},{8,0},{12,4},{16,24},{20,28},{24,16},{28,20},{1,9},{5... | collective-permute-start | bytes 786440 | tf_op jit(solution)/shard_map/ppermute | solution.py:488
  36.1 4.3 %collective-permute-done.7.x_ref.piece_ref = f32[512,128]{1,0:T(8,128)S(1)} collective-permute-done((f32[512,128]{1,0:T(8,128)S(1)}, f32[512,128]{1,0:T(8,128)S(1)}, u32[]{:S(2)}, u32[]{:S(2)}) %collective-permute-start.7) | collective-permute-done | bytes 262176 | tf_op jit(solution)/shard_map/ppermute | solution.py:488
  40.4 1.8 %collective-permute-start.8 = (f32[256,128]{1,0:T(8,128)S(1)}, f32[256,128]{1,0:T(8,128)S(1)}, u32[]{:S(2)}, u32[]{:S(2)}) collective-permute-start(f32[256,128]{1,0:T(8,128)S(1)} %shard_map.91), channel_id=1, source_target_pairs={{0,16},{4,20},{8,24},{12,28},{16,0},{20,4},{24,8},{28,12},{1,17},{... | collective-permute-start | bytes 393224 | tf_op jit(solution)/shard_map/ppermute | solution.py:488
  51.1 4.0 %collective-permute-done.10 = f32[256,128]{1,0:T(8,128)S(1)} collective-permute-done((f32[256,128]{1,0:T(8,128)S(1)}, f32[256,128]{1,0:T(8,128)S(1)}, u32[]{:S(2)}, u32[]{:S(2)}) %collective-permute-start.10) | collective-permute-done | bytes 131104 | tf_op jit(solution)/shard_map/ppermute | solution.py:488
  55.0 3.7 %collective-permute-start.11 = (f32[256,128]{1,0:T(8,128)S(1)}, f32[256,128]{1,0:T(8,128)S(1)}, u32[]{:S(2)}, u32[]{:S(2)}) collective-permute-start(f32[256,128]{1,0:T(8,128)S(1)} %slice_add_fusion), channel_id=1, source_target_pairs={{0,3},{1,2},{2,1},{3,0},{4,7},{5,6},{6,5},{7,4},{8,11},{9,10},{10,... | collective-permute-start | bytes 393224 | tf_op jit(solution)/shard_map/ppermute | solution.py:488
  58.7 3.2 %collective-permute-done.11 = f32[256,128]{1,0:T(8,128)S(1)} collective-permute-done((f32[256,128]{1,0:T(8,128)S(1)}, f32[256,128]{1,0:T(8,128)S(1)}, u32[]{:S(2)}, u32[]{:S(2)}) %collective-permute-start.11) | collective-permute-done | bytes 131104 | tf_op jit(solution)/shard_map/ppermute | solution.py:488
  62.0 2.3 %collective-permute-start.12 = (f32[256,128]{1,0:T(8,128)S(1)}, f32[256,128]{1,0:T(8,128)S(1)}, u32[]{:S(2)}, u32[]{:S(2)}) collective-permute-start(f32[256,128]{1,0:T(8,128)S(1)} %add.32), channel_id=1, source_target_pairs={{0,1},{1,0},{2,3},{3,2},{4,5},{5,4},{6,7},{7,6},{8,9},{9,8},{10,11... | collective-permute-start | bytes 393224 | tf_op jit(solution)/shard_map/ppermute | solution.py:488
  64.3 2.9 %collective-permute-done.12 = f32[256,128]{1,0:T(8,128)S(1)} collective-permute-done((f32[256,128]{1,0:T(8,128)S(1)}, f32[256,128]{1,0:T(8,128)S(1)}, u32[]{:S(2)}, u32[]{:S(2)}) %collective-permute-start.12) | collective-permute-done | bytes 131104 | tf_op jit(solution)/shard_map/ppermute | solution.py:488
  73.4 10.5 %copy-done = f32[4096,2048]{1,0:T(8,128)S(1)} copy-done((f32[4096,2048]{1,0:T(8,128)S(1)}, f32[4096,2048]{1,0:T(8,128)}, u32[]{:S(2)}) %copy-start) | copy-done | bytes 33554456
  87.4 2.4 %shard_map.102.refs_1_ = f32[128,2048]{1,0:T(8,128)S(1)} custom-call(f32[4096,2048]{1,0:T(8,128)S(1)} %copy-done, f32[512,128]{1,0:T(8,128)S(1)} %get-tuple-element.76.refs_0_, f32[512,128]{1,0:T(8,128)S(1)} %collective-permute-done.20.refs_1_), custom_call_target="tpu_custom_call" | custom-call | flops 1 | bytes 1 | tf_op jit(solution)/shard_map/pallas_call | solution.py:346
  89.8 4.5 %collective-permute-done.19.x_ref.refs_0_ = f32[512,128]{1,0:T(8,128)S(1)} collective-permute-done((f32[512,128]{1,0:T(8,128)S(1)}, f32[512,128]{1,0:T(8,128)S(1)}, u32[]{:S(2)}, u32[]{:S(2)}) %collective-permute-start.19) | collective-permute-done | bytes 262176 | tf_op jit(solution)/shard_map/ppermute | solution.py:488
  103.1 2.1 %collective-permute-start.26 = (f32[256,128]{1,0:T(8,128)S(1)}, f32[256,128]{1,0:T(8,128)S(1)}, u32[]{:S(2)}, u32[]{:S(2)}) collective-permute-start(f32[256,128]{1,0:T(8,128)S(1)} %get-tuple-element.87), channel_id=1, source_target_pairs={{0,1},{1,0},{2,3},{3,2},{4,5},{5,4},{6,7},{7,6},{8,9},{9,8},{10,11... | collective-permute-start | bytes 393224 | tf_op jit(solution)/shard_map/ppermute | solution.py:488
  105.2 2.8 %shard_map.110 = (f32[768,128]{1,0:T(8,128)S(1)}, f32[768,128]{1,0:T(8,128)S(1)}) custom-call(f32[4096,2048]{1,0:T(8,128)S(1)} %copy-done, f32[128,2048]{1,0:T(8,128)S(1)} %shard_map.107.acc_ref, f32[512,128]{1,0:T(8,128)S(1)} %collective-permute-done.22.refs_0_, f32[512,128]{1,0:T(8,128)S(1)} %collective-permute-done.23.refs_1_, ...), custom_call_target="tpu_custom_call" | custom-call | flops 1 | bytes 1 | tf_op jit(solution)/shard_map/pallas_call | solution.py:389
  110.9 2.8 %collective-permute-start.27 = (f32[256,128]{1,0:T(8,128)S(1)}, f32[256,128]{1,0:T(8,128)S(1)}, u32[]{:S(2)}, u32[]{:S(2)}) collective-permute-start(f32[256,128]{1,0:T(8,128)S(1)} %add.35), channel_id=1, source_target_pairs={{0,3},{1,2},{2,1},{3,0},{4,7},{5,6},{6,5},{7,4},{8,11},{9,10},{10,... | collective-permute-start | bytes 393224 | tf_op jit(solution)/shard_map/ppermute | solution.py:488
  113.6 6.5 %collective-permute-done.29 = f32[768,128]{1,0:T(8,128)S(1)} collective-permute-done((f32[768,128]{1,0:T(8,128)S(1)}, f32[768,128]{1,0:T(8,128)S(1)}, u32[]{:S(2)}, u32[]{:S(2)}) %collective-permute-start.29) | collective-permute-done | bytes 393248 | tf_op jit(solution)/shard_map/ppermute | solution.py:488
  120.2 4.6 %collective-permute-done.27 = f32[256,128]{1,0:T(8,128)S(1)} collective-permute-done((f32[256,128]{1,0:T(8,128)S(1)}, f32[256,128]{1,0:T(8,128)S(1)}, u32[]{:S(2)}, u32[]{:S(2)}) %collective-permute-start.27) | collective-permute-done | bytes 131104 | tf_op jit(solution)/shard_map/ppermute | solution.py:488
  126.2 11.1 %collective-permute-done.30 = f32[768,128]{1,0:T(8,128)S(1)} collective-permute-done((f32[768,128]{1,0:T(8,128)S(1)}, f32[768,128]{1,0:T(8,128)S(1)}, u32[]{:S(2)}, u32[]{:S(2)}) %collective-permute-start.30) | collective-permute-done | bytes 393248 | tf_op jit(solution)/shard_map/ppermute | solution.py:488
  137.9 3.7 %collective-permute-start.32 = (f32[8,128]{1,0:T(8,128)S(1)}, f32[8,128]{1,0:T(8,128)S(1)}, u32[]{:S(2)}, u32[]{:S(2)}) collective-permute-start(f32[8,128]{1,0:T(8,128)S(1)} %get-tuple-element.96), channel_id=1, source_target_pairs={{0,1},{1,0},{2,3},{3,2},{4,5},{5,4},{6,7},{7,6},{8,9},{9,8},{10,11... | collective-permute-start | bytes 12296 | tf_op jit(solution)/shard_map/ppermute | solution.py:488
  143.2 9.0 %all-gather = f32[64,128]{1,0:T(8,128)S(1)} all-gather(f32[8,128]{1,0:T(8,128)S(1)} %add.39), channel_id=2, replica_groups=mesh['rows'=8,'cols'=4] {'rows'}, dimensions={0}, use_global_device_ids=true | all-gather | bytes 36864 | tf_op jit(solution)/shard_map/all_gather | solution.py:563
  (95 shorter events, 39.2 us)
Async XLA Ops:
  13.5 7.0 %collective-permute-start.4 = (f32[512,256]{1,0:T(8,128)S(1)}, f32[512,256]{1,0:T(8,128)S(1)}, u32[]{:S(2)}, u32[]{:S(2)}) collective-permute-start(f32[512,256]{1,0:T(8,128)S(1)} %copy-done.3), channel_id=1, source_target_pairs={{0,4},{4,0},{8,12},{12,8},{16,20},{20,16},{24,28},{28,24},{1,5},{5... | collective-permute-start | bytes 1572872 | tf_op jit(solution)/shard_map/ppermute | solution.py:488
  15.9 16.5 %collective-permute-start.1 = (f32[520,128]{1,0:T(8,128)S(1)}, f32[520,128]{1,0:T(8,128)S(1)}, u32[]{:S(2)}, u32[]{:S(2)}) collective-permute-start(f32[520,128]{1,0:T(8,128)S(1)} %get-tuple-element.56), channel_id=1, source_target_pairs={{0,8},{4,12},{8,0},{12,4},{16,24},{20,28},{24,16},{28,20},{1,9},{5... | collective-permute-start | bytes 798728 | tf_op jit(solution)/shard_map/ppermute | solution.py:488
  18.8 13.9 %collective-permute-start.2 = (f32[520,128]{1,0:T(8,128)S(1)}, f32[520,128]{1,0:T(8,128)S(1)}, u32[]{:S(2)}, u32[]{:S(2)}) collective-permute-start(f32[520,128]{1,0:T(8,128)S(1)} %get-tuple-element.57), channel_id=1, source_target_pairs={{0,16},{4,20},{8,24},{12,28},{16,0},{20,4},{24,8},{28,12},{1,17},{... | collective-permute-start | bytes 798728 | tf_op jit(solution)/shard_map/ppermute | solution.py:488
  20.3 12.3 %collective-permute-start.3 = (f32[520,128]{1,0:T(8,128)S(1)}, f32[520,128]{1,0:T(8,128)S(1)}, u32[]{:S(2)}, u32[]{:S(2)}) collective-permute-start(f32[520,128]{1,0:T(8,128)S(1)} %get-tuple-element.58), channel_id=1, source_target_pairs={{0,24},{4,28},{8,16},{12,20},{16,8},{20,12},{24,0},{28,4},{1,25},{... | collective-permute-start | bytes 798728 | tf_op jit(solution)/shard_map/ppermute | solution.py:488
  32.8 7.6 %collective-permute-start.7 = (f32[512,128]{1,0:T(8,128)S(1)}, f32[512,128]{1,0:T(8,128)S(1)}, u32[]{:S(2)}, u32[]{:S(2)}) collective-permute-start(f32[512,128]{1,0:T(8,128)S(1)} %get-tuple-element.65.piece_ref), channel_id=1, source_target_pairs={{0,8},{4,12},{8,0},{12,4},{16,24},{20,28},{24,16},{28,20},{1,9},{5... | collective-permute-start | bytes 786440 | tf_op jit(solution)/shard_map/ppermute | solution.py:488
  34.5 7.6 %collective-permute-start.5 = (f32[512,128]{1,0:T(8,128)S(1)}, f32[512,128]{1,0:T(8,128)S(1)}, u32[]{:S(2)}, u32[]{:S(2)}) collective-permute-start(f32[512,128]{1,0:T(8,128)S(1)} %get-tuple-element.65.piece_ref), channel_id=1, source_target_pairs={{0,16},{4,20},{8,24},{12,28},{16,0},{20,4},{24,8},{28,12},{1,17},{... | collective-permute-start | bytes 786440 | tf_op jit(solution)/shard_map/ppermute | solution.py:488
  40.4 5.6 %collective-permute-start.8 = (f32[256,128]{1,0:T(8,128)S(1)}, f32[256,128]{1,0:T(8,128)S(1)}, u32[]{:S(2)}, u32[]{:S(2)}) collective-permute-start(f32[256,128]{1,0:T(8,128)S(1)} %shard_map.91), channel_id=1, source_target_pairs={{0,16},{4,20},{8,24},{12,28},{16,0},{20,4},{24,8},{28,12},{1,17},{... | collective-permute-start | bytes 393224 | tf_op jit(solution)/shard_map/ppermute | solution.py:488
  49.4 5.6 %collective-permute-start.10 = (f32[256,128]{1,0:T(8,128)S(1)}, f32[256,128]{1,0:T(8,128)S(1)}, u32[]{:S(2)}, u32[]{:S(2)}) collective-permute-start(f32[256,128]{1,0:T(8,128)S(1)} %slice.21), channel_id=1, source_target_pairs={{0,1},{1,0},{2,3},{3,2},{4,5},{5,4},{6,7},{7,6},{8,9},{9,8},{10,11... | collective-permute-start | bytes 393224 | tf_op jit(solution)/shard_map/ppermute | solution.py:488
  55.0 6.9 %collective-permute-start.11 = (f32[256,128]{1,0:T(8,128)S(1)}, f32[256,128]{1,0:T(8,128)S(1)}, u32[]{:S(2)}, u32[]{:S(2)}) collective-permute-start(f32[256,128]{1,0:T(8,128)S(1)} %slice_add_fusion), channel_id=1, source_target_pairs={{0,3},{1,2},{2,1},{3,0},{4,7},{5,6},{6,5},{7,4},{8,11},{9,10},{10,... | collective-permute-start | bytes 393224 | tf_op jit(solution)/shard_map/ppermute | solution.py:488
  62.0 5.3 %collective-permute-start.12 = (f32[256,128]{1,0:T(8,128)S(1)}, f32[256,128]{1,0:T(8,128)S(1)}, u32[]{:S(2)}, u32[]{:S(2)}) collective-permute-start(f32[256,128]{1,0:T(8,128)S(1)} %add.32), channel_id=1, source_target_pairs={{0,1},{1,0},{2,3},{3,2},{4,5},{5,4},{6,7},{7,6},{8,9},{9,8},{10,11... | collective-permute-start | bytes 393224 | tf_op jit(solution)/shard_map/ppermute | solution.py:488
  69.9 14.6 %collective-permute-start.14 = (f32[520,128]{1,0:T(8,128)S(1)}, f32[520,128]{1,0:T(8,128)S(1)}, u32[]{:S(2)}, u32[]{:S(2)}) collective-permute-start(f32[520,128]{1,0:T(8,128)S(1)} %get-tuple-element.72), channel_id=1, source_target_pairs={{0,8},{4,12},{8,0},{12,4},{16,24},{20,28},{24,16},{28,20},{1,9},{5... | collective-permute-start | bytes 798728 | tf_op jit(solution)/shard_map/ppermute | solution.py:488
  71.4 14.0 %collective-permute-start.15 = (f32[520,128]{1,0:T(8,128)S(1)}, f32[520,128]{1,0:T(8,128)S(1)}, u32[]{:S(2)}, u32[]{:S(2)}) collective-permute-start(f32[520,128]{1,0:T(8,128)S(1)} %get-tuple-element.73), channel_id=1, source_target_pairs={{0,16},{4,20},{8,24},{12,28},{16,0},{20,4},{24,8},{28,12},{1,17},{... | collective-permute-start | bytes 798728 | tf_op jit(solution)/shard_map/ppermute | solution.py:488
  71.9 13.5 %collective-permute-start.16 = (f32[520,128]{1,0:T(8,128)S(1)}, f32[520,128]{1,0:T(8,128)S(1)}, u32[]{:S(2)}, u32[]{:S(2)}) collective-permute-start(f32[520,128]{1,0:T(8,128)S(1)} %get-tuple-element.74), channel_id=1, source_target_pairs={{0,24},{4,28},{8,16},{12,20},{16,8},{20,12},{24,0},{28,4},{1,25},{... | collective-permute-start | bytes 798728 | tf_op jit(solution)/shard_map/ppermute | solution.py:488
  85.6 8.7 %collective-permute-start.19 = (f32[512,128]{1,0:T(8,128)S(1)}, f32[512,128]{1,0:T(8,128)S(1)}, u32[]{:S(2)}, u32[]{:S(2)}) collective-permute-start(f32[512,128]{1,0:T(8,128)S(1)} %get-tuple-element.76.refs_0_), channel_id=1, source_target_pairs={{0,8},{4,12},{8,0},{12,4},{16,24},{20,28},{24,16},{28,20},{1,9},{5... | collective-permute-start | bytes 786440 | tf_op jit(solution)/shard_map/ppermute | solution.py:488
  86.2 8.7 %collective-permute-start.17 = (f32[512,128]{1,0:T(8,128)S(1)}, f32[512,128]{1,0:T(8,128)S(1)}, u32[]{:S(2)}, u32[]{:S(2)}) collective-permute-start(f32[512,128]{1,0:T(8,128)S(1)} %get-tuple-element.76.refs_0_), channel_id=1, source_target_pairs={{0,16},{4,20},{8,24},{12,28},{16,0},{20,4},{24,8},{28,12},{1,17},{... | collective-permute-start | bytes 786440 | tf_op jit(solution)/shard_map/ppermute | solution.py:488
  94.3 5.1 %collective-permute-start.21 = (f32[256,128]{1,0:T(8,128)S(1)}, f32[256,128]{1,0:T(8,128)S(1)}, u32[]{:S(2)}, u32[]{:S(2)}) collective-permute-start(f32[256,128]{1,0:T(8,128)S(1)} %shard_map.103), channel_id=1, source_target_pairs={{0,16},{4,20},{8,24},{12,28},{16,0},{20,4},{24,8},{28,12},{1,17},{... | collective-permute-start | bytes 393224 | tf_op jit(solution)/shard_map/ppermute | solution.py:488
  94.9 5.3 %collective-permute-start.18 = (f32[256,128]{1,0:T(8,128)S(1)}, f32[256,128]{1,0:T(8,128)S(1)}, u32[]{:S(2)}, u32[]{:S(2)}) collective-permute-start(f32[256,128]{1,0:T(8,128)S(1)} %shard_map.101), channel_id=1, source_target_pairs={{0,8},{4,12},{8,0},{12,4},{16,24},{20,28},{24,16},{28,20},{1,9},{5... | collective-permute-start | bytes 393224 | tf_op jit(solution)/shard_map/ppermute | solution.py:488
  103.1 6.0 %collective-permute-start.26 = (f32[256,128]{1,0:T(8,128)S(1)}, f32[256,128]{1,0:T(8,128)S(1)}, u32[]{:S(2)}, u32[]{:S(2)}) collective-permute-start(f32[256,128]{1,0:T(8,128)S(1)} %get-tuple-element.87), channel_id=1, source_target_pairs={{0,1},{1,0},{2,3},{3,2},{4,5},{5,4},{6,7},{7,6},{8,9},{9,8},{10,11... | collective-permute-start | bytes 393224 | tf_op jit(solution)/shard_map/ppermute | solution.py:488
  109.1 11.1 %collective-permute-start.29 = (f32[768,128]{1,0:T(8,128)S(1)}, f32[768,128]{1,0:T(8,128)S(1)}, u32[]{:S(2)}, u32[]{:S(2)}) collective-permute-start(f32[768,128]{1,0:T(8,128)S(1)} %get-tuple-element.91), channel_id=1, source_target_pairs={{0,1},{1,0},{2,3},{3,2},{4,5},{5,4},{6,7},{7,6},{8,9},{9,8},{10,11... | collective-permute-start | bytes 1179656 | tf_op jit(solution)/shard_map/ppermute | solution.py:488
  110.9 14.0 %collective-permute-start.27 = (f32[256,128]{1,0:T(8,128)S(1)}, f32[256,128]{1,0:T(8,128)S(1)}, u32[]{:S(2)}, u32[]{:S(2)}) collective-permute-start(f32[256,128]{1,0:T(8,128)S(1)} %add.35), channel_id=1, source_target_pairs={{0,3},{1,2},{2,1},{3,0},{4,7},{5,6},{6,5},{7,4},{8,11},{9,10},{10,... | collective-permute-start | bytes 393224 | tf_op jit(solution)/shard_map/ppermute | solution.py:488
  124.9 12.4 %collective-permute-start.30 = (f32[768,128]{1,0:T(8,128)S(1)}, f32[768,128]{1,0:T(8,128)S(1)}, u32[]{:S(2)}, u32[]{:S(2)}) collective-permute-start(f32[768,128]{1,0:T(8,128)S(1)} %add.37), channel_id=1, source_target_pairs={{0,3},{1,2},{2,1},{3,0},{4,7},{5,6},{6,5},{7,4},{8,11},{9,10},{10,... | collective-permute-start | bytes 1179656 | tf_op jit(solution)/shard_map/ppermute | solution.py:488
  126.1 11.7 %collective-permute-start.28 = (f32[256,128]{1,0:T(8,128)S(1)}, f32[256,128]{1,0:T(8,128)S(1)}, u32[]{:S(2)}, u32[]{:S(2)}) collective-permute-start(f32[256,128]{1,0:T(8,128)S(1)} %get-tuple-element.88.refs_0_), channel_id=1, source_target_pairs={{0,1},{1,0},{2,3},{3,2},{4,5},{5,4},{6,7},{7,6},{8,9},{9,8},{10,11... | collective-permute-start | bytes 393224 | tf_op jit(solution)/shard_map/ppermute | solution.py:488
  137.9 5.4 %collective-permute-start.32 = (f32[8,128]{1,0:T(8,128)S(1)}, f32[8,128]{1,0:T(8,128)S(1)}, u32[]{:S(2)}, u32[]{:S(2)}) collective-permute-start(f32[8,128]{1,0:T(8,128)S(1)} %get-tuple-element.96), channel_id=1, source_target_pairs={{0,1},{1,0},{2,3},{3,2},{4,5},{5,4},{6,7},{7,6},{8,9},{9,8},{10,11... | collective-permute-start | bytes 12296 | tf_op jit(solution)/shard_map/ppermute | solution.py:488
  141.6 10.6 %collective-permute-start.31 = (f32[768,128]{1,0:T(8,128)S(1)}, f32[768,128]{1,0:T(8,128)S(1)}, u32[]{:S(2)}, u32[]{:S(2)}) collective-permute-start(f32[768,128]{1,0:T(8,128)S(1)} %get-tuple-element.95.refs_2_), channel_id=1, source_target_pairs={{0,1},{1,0},{2,3},{3,2},{4,5},{5,4},{6,7},{7,6},{8,9},{9,8},{10,11... | collective-permute-start | bytes 1179656 | tf_op jit(solution)/shard_map/ppermute | solution.py:488
  (14 other events, 127.5 us)

commit v7 on v6

--- a/solution.py
+++ b/solution.py
@@ -141,7 +141,7 @@
         jax.ShapeDtypeStruct((count, m + PAD, t), f32)
         for count in ((1,) if own else (chips - 1, chips))
     )
-    slots = 3
+    slots = 4
     far = pl.BlockSpec(memory_space=pl.ANY)
     return pl.pallas_call(
         functools.partial(forward_kernel, chips, begin, end, slots),
@@ -324,11 +324,11 @@
     )(*args)
 
 
-def transposed_kernel(m, shift, begin, sides, first, l_ref, *refs):
+def transposed_kernel(m, places, first, l_ref, *refs):
     chip, core, _ = here(2)
-    pieces, refs = refs[: len(sides)], refs[len(sides) :]
+    pieces, refs = refs[: len(places)], refs[len(places) :]
     value = None if first else refs[0][...]
-    for side, ref in zip(sides, pieces):
+    for (shift, begin, side), ref in zip(places, pieces):
         n = ref.shape[0]
         step = min(n, 256)
         for i in range(0, n, step):
@@ -339,12 +339,12 @@
     refs[-1][...] = value
 
 
-def transposed(m, shift, begin, sides, inv_factor, pieces, acc):
+def transposed(m, places, inv_factor, pieces, acc):
     depth = inv_factor.shape[1]
     t = pieces[0].shape[1]
     args = [resident(inv_factor), *pieces] + ([] if acc is None else [acc])
     return pl.pallas_call(
-        functools.partial(transposed_kernel, m, shift, begin, sides, acc is None),
+        functools.partial(transposed_kernel, m, places, acc is None),
         in_specs=[local] * len(args),
         out_specs=local,
         out_shape=jax.ShapeDtypeStruct((t, depth), f32),
@@ -530,13 +530,15 @@
     got += back_product((0,), high, low, part, other, before[-1:], (inv_factor,))
     own, pred_norm = add([got[-1], *got[:-1]], [(m, t), (PAD, t)], (inv_factor,))
 
-    acc = transposed(m, 0, 0, (0, 1), inv_factor, [own, swap(own, "rows", 1)], None)
+    acc = transposed(m, [(0, 0, 0), (0, 0, 1)], inv_factor, [own, swap(own, "rows", 1)], None)
     acc, arrived = gather(own, (inv_factor,), acc)
     late = []
-    for shift, begin, piece in arrived:
-        piece, acc = lax.optimization_barrier((piece, acc))
-        late.append((shift, begin, swap(piece, "rows", 1)))
-        acc = transposed(m, shift, begin, (0,), inv_factor, [piece], acc)
+    turns = [arrived[:2], *([one] for one in arrived[2:])]
+    for turn in turns:
+        pieces, acc = lax.optimization_barrier(([one[2] for one in turn], acc))
+        places = [(shift, begin, 0) for shift, begin, _ in turn]
+        late += [(*one[:2], swap(piece, "rows", 1)) for one, piece in zip(turn, pieces)]
+        acc = transposed(m, places, inv_factor, pieces, acc)
     pieces, norm_next, step_one, step_two, done = [], None, (), (), ()
     for c, (begin, _) in enumerate(cuts(residual.shape[0] // segments)):
         image, send = last_transposed(m, c, segments, inv_factor, late, acc)

time: 154 us -> 154 us (level)
    pallas_call x5 -> x4, Pallas kernels: 6.5 us -> 6.53 us  [transposed(): pl.pallas_call(functools.partial(transposed_kernel, m, places, acc is Non...]
  transfers between devices with their start and end apart: 33 -> 33, of which waited for: 19 -> 18; matrix products, arithmetic and copies ran while one was open for 1% -> 1% of each run, Pallas kernels for 17% -> 17%
where the time goes in v7:
time: 154 us
  waiting for transfers between devices  49.9 us (32%)
  Pallas kernels  42.6 us (28%)
  starting transfers between devices  39.5 us (26%)
  local copies, waits for them, and re-layouts  10.6 us (7%)
  blocking collectives  8.68 us (6%)
    ppermute x33, waiting for transfers between devices, swap(): return lax.ppermute(x, axis, [(i, i ^ mask) for i in range(size)])  49.9 us
    ppermute x33, starting transfers between devices, swap(): return lax.ppermute(x, axis, [(i, i ^ mask) for i in range(size)])  39.5 us
    pallas_call x2, Pallas kernels, forward(): pl.pallas_call(functools.partial(forward_kernel, chips, begin, end, slots...  16.7 us
    unnamed x10, local copies, waits for them, and re-layouts  10.6 us
    all_gather x1, blocking collectives, body(): norm_next = jnp.sum(lax.all_gather(norm_next, 'rows'), axis=0)  8.68 us
    pallas_call x1, Pallas kernels, gaussian(): pl.pallas_call(functools.partial(kernel_kernel, segments), grid_spec=pltp...  7.48 us
    pallas_call x4, Pallas kernels, transposed(): pl.pallas_call(functools.partial(transposed_kernel, m, places, acc is Non...  6.53 us
    pallas_call x2, Pallas kernels, last_transposed(): pl.pallas_call(functools.partial(last_kernel, m, [piece[:2] for piece in...  4.01 us
  transfers between devices with their start and end apart: 33, of which 18 were waited for; matrix products, arithmetic and copies ran while one was open for 1% of the time, Pallas kernels for 17%

profile of v7, /device:TPU:0, one launch (start us, length us, event | category | flops | bytes accessed | tf_op | source)
XLA Modules:
  0.0 153.7 jit_solution(4133057406791677485)
XLA Ops:
  0.6 12.2 %shard_map.85 = (f32[3,520,128]{2,1,0:T(8,128)S(1)}, f32[4,520,128]{2,1,0:T(8,128)S(1)}) custom-call(f32[4096,2048]{1,0:T(8,128)} %l_ref.15, f32[2048,128]{1,0:T(8,128)} %refs_4_.2, f32[2048,128]{1,0:T(8,128)} %r_ref.7), custom_call_target="tpu_custom_call" | custom-call | flops 1 | bytes 1 | tf_op jit(solution)/shard_map/pallas_call | solution.py:146
  13.5 2.2 %collective-permute-done.refs_1_ = f32[4,520,128]{2,1,0:T(8,128)S(1)} collective-permute-done((f32[4,520,128]{2,1,0:T(8,128)S(1)}, f32[4,520,128]{2,1,0:T(8,128)S(1)}, u32[]{:S(2)}, u32[]{:S(2)}) %collective-permute-start) | collective-permute-done | bytes 1064992 | tf_op jit(solution)/shard_map/ppermute | solution.py:488
  15.8 2.9 %collective-permute-start.1 = (f32[520,128]{1,0:T(8,128)S(1)}, f32[520,128]{1,0:T(8,128)S(1)}, u32[]{:S(2)}, u32[]{:S(2)}) collective-permute-start(f32[520,128]{1,0:T(8,128)S(1)} %get-tuple-element.56), channel_id=1, source_target_pairs={{0,8},{4,12},{8,0},{12,4},{16,24},{20,28},{24,16},{28,20},{1,9},{5... | collective-permute-start | bytes 798728 | tf_op jit(solution)/shard_map/ppermute | solution.py:488
  20.4 7.5 %shard_map.89 = (bf16[4,512,1024]{2,1,0:T(8,128)(2,1)S(1)}, bf16[4,512,1024]{2,1,0:T(8,128)(2,1)S(1)}) custom-call(s32[3]{0:T(128)S(1)} %pad_add_fusion.place, f32[512,256]{1,0:T(8,128)S(1)} %copy-done.3, f32[512,256]{1,0:T(8,128)S(1)} %collective-permute-done.4.other_ref, f32[4096,256]{1,0:T(8,128)} %c_ref.1), custom_call_target="tpu_custom_call" | custom-call | flops 1 | bytes 1 | tf_op jit(solution)/shard_map/pallas_call | solution.py:235
  27.9 4.5 %shard_map.87 = f32[1,520,128]{2,1,0:T(8,128)S(1)} custom-call(f32[4096,2048]{1,0:T(8,128)} %l_ref.15, f32[2048,128]{1,0:T(8,128)} %refs_4_.2, f32[2048,128]{1,0:T(8,128)} %r_ref.7), custom_call_target="tpu_custom_call" | custom-call | flops 1 | bytes 1 | tf_op jit(solution)/shard_map/pallas_call | solution.py:146
  36.0 4.3 %collective-permute-done.7.x_ref.piece_ref = f32[512,128]{1,0:T(8,128)S(1)} collective-permute-done((f32[512,128]{1,0:T(8,128)S(1)}, f32[512,128]{1,0:T(8,128)S(1)}, u32[]{:S(2)}, u32[]{:S(2)}) %collective-permute-start.7) | collective-permute-done | bytes 262176 | tf_op jit(solution)/shard_map/ppermute | solution.py:488
  40.4 1.8 %collective-permute-start.8 = (f32[256,128]{1,0:T(8,128)S(1)}, f32[256,128]{1,0:T(8,128)S(1)}, u32[]{:S(2)}, u32[]{:S(2)}) collective-permute-start(f32[256,128]{1,0:T(8,128)S(1)} %shard_map.91), channel_id=1, source_target_pairs={{0,16},{4,20},{8,24},{12,28},{16,0},{20,4},{24,8},{28,12},{1,17},{... | collective-permute-start | bytes 393224 | tf_op jit(solution)/shard_map/ppermute | solution.py:488
  51.0 3.9 %collective-permute-done.10 = f32[256,128]{1,0:T(8,128)S(1)} collective-permute-done((f32[256,128]{1,0:T(8,128)S(1)}, f32[256,128]{1,0:T(8,128)S(1)}, u32[]{:S(2)}, u32[]{:S(2)}) %collective-permute-start.10) | collective-permute-done | bytes 131104 | tf_op jit(solution)/shard_map/ppermute | solution.py:488
  55.0 3.7 %collective-permute-start.11 = (f32[256,128]{1,0:T(8,128)S(1)}, f32[256,128]{1,0:T(8,128)S(1)}, u32[]{:S(2)}, u32[]{:S(2)}) collective-permute-start(f32[256,128]{1,0:T(8,128)S(1)} %slice_add_fusion), channel_id=1, source_target_pairs={{0,3},{1,2},{2,1},{3,0},{4,7},{5,6},{6,5},{7,4},{8,11},{9,10},{10,... | collective-permute-start | bytes 393224 | tf_op jit(solution)/shard_map/ppermute | solution.py:488
  58.7 3.2 %collective-permute-done.11 = f32[256,128]{1,0:T(8,128)S(1)} collective-permute-done((f32[256,128]{1,0:T(8,128)S(1)}, f32[256,128]{1,0:T(8,128)S(1)}, u32[]{:S(2)}, u32[]{:S(2)}) %collective-permute-start.11) | collective-permute-done | bytes 131104 | tf_op jit(solution)/shard_map/ppermute | solution.py:488
  61.9 2.4 %collective-permute-start.12 = (f32[256,128]{1,0:T(8,128)S(1)}, f32[256,128]{1,0:T(8,128)S(1)}, u32[]{:S(2)}, u32[]{:S(2)}) collective-permute-start(f32[256,128]{1,0:T(8,128)S(1)} %add.32), channel_id=1, source_target_pairs={{0,1},{1,0},{2,3},{3,2},{4,5},{5,4},{6,7},{7,6},{8,9},{9,8},{10,11... | collective-permute-start | bytes 393224 | tf_op jit(solution)/shard_map/ppermute | solution.py:488
  64.3 2.9 %collective-permute-done.12 = f32[256,128]{1,0:T(8,128)S(1)} collective-permute-done((f32[256,128]{1,0:T(8,128)S(1)}, f32[256,128]{1,0:T(8,128)S(1)}, u32[]{:S(2)}, u32[]{:S(2)}) %collective-permute-start.12) | collective-permute-done | bytes 131104 | tf_op jit(solution)/shard_map/ppermute | solution.py:488
  73.4 10.5 %copy-done = f32[4096,2048]{1,0:T(8,128)S(1)} copy-done((f32[4096,2048]{1,0:T(8,128)S(1)}, f32[4096,2048]{1,0:T(8,128)}, u32[]{:S(2)}) %copy-start) | copy-done | bytes 33554456
  87.3 2.4 %shard_map.102.refs_2_ = f32[128,2048]{1,0:T(8,128)S(1)} custom-call(f32[4096,2048]{1,0:T(8,128)S(1)} %copy-done, f32[512,128]{1,0:T(8,128)S(1)} %get-tuple-element.76.refs_0_, f32[512,128]{1,0:T(8,128)S(1)} %collective-permute-done.20.refs_1_), custom_call_target="tpu_custom_call" | custom-call | flops 1 | bytes 1 | tf_op jit(solution)/shard_map/pallas_call | solution.py:346
  89.7 4.5 %collective-permute-done.19.x_ref.refs_0_ = f32[512,128]{1,0:T(8,128)S(1)} collective-permute-done((f32[512,128]{1,0:T(8,128)S(1)}, f32[512,128]{1,0:T(8,128)S(1)}, u32[]{:S(2)}, u32[]{:S(2)}) %collective-permute-start.19) | collective-permute-done | bytes 262176 | tf_op jit(solution)/shard_map/ppermute | solution.py:488
  96.7 2.4 %shard_map.104.refs_1_ = f32[128,2048]{1,0:T(8,128)S(1)} custom-call(f32[4096,2048]{1,0:T(8,128)S(1)} %copy-done, f32[512,128]{1,0:T(8,128)S(1)} %collective-permute-done.19.x_ref.refs_0_, f32[512,128]{1,0:T(8,128)S(1)} %collective-permute-done.17.x_ref.refs_1_, f32[128,2048]{1,0:T(8,128)S(1)} %shard_map.102.refs_2_), custom_call_target="tpu_custom_call" | custom-call | flops 1 | bytes 1 | tf_op jit(solution)/shard_map/pallas_call | solution.py:346
  103.0 2.1 %collective-permute-start.26 = (f32[256,128]{1,0:T(8,128)S(1)}, f32[256,128]{1,0:T(8,128)S(1)}, u32[]{:S(2)}, u32[]{:S(2)}) collective-permute-start(f32[256,128]{1,0:T(8,128)S(1)} %get-tuple-element.87), channel_id=1, source_target_pairs={{0,1},{1,0},{2,3},{3,2},{4,5},{5,4},{6,7},{7,6},{8,9},{9,8},{10,11... | collective-permute-start | bytes 393224 | tf_op jit(solution)/shard_map/ppermute | solution.py:488
  105.1 2.8 %shard_map.109 = (f32[768,128]{1,0:T(8,128)S(1)}, f32[768,128]{1,0:T(8,128)S(1)}) custom-call(f32[4096,2048]{1,0:T(8,128)S(1)} %copy-done, f32[128,2048]{1,0:T(8,128)S(1)} %shard_map.106.acc_ref, f32[512,128]{1,0:T(8,128)S(1)} %collective-permute-done.22.refs_0_, f32[512,128]{1,0:T(8,128)S(1)} %collective-permute-done.23.refs_1_, ...), custom_call_target="tpu_custom_call" | custom-call | flops 1 | bytes 1 | tf_op jit(solution)/shard_map/pallas_call | solution.py:389
  110.8 2.8 %collective-permute-start.27 = (f32[256,128]{1,0:T(8,128)S(1)}, f32[256,128]{1,0:T(8,128)S(1)}, u32[]{:S(2)}, u32[]{:S(2)}) collective-permute-start(f32[256,128]{1,0:T(8,128)S(1)} %add.35), channel_id=1, source_target_pairs={{0,3},{1,2},{2,1},{3,0},{4,7},{5,6},{6,5},{7,4},{8,11},{9,10},{10,... | collective-permute-start | bytes 393224 | tf_op jit(solution)/shard_map/ppermute | solution.py:488
  113.6 6.7 %collective-permute-done.29 = f32[768,128]{1,0:T(8,128)S(1)} collective-permute-done((f32[768,128]{1,0:T(8,128)S(1)}, f32[768,128]{1,0:T(8,128)S(1)}, u32[]{:S(2)}, u32[]{:S(2)}) %collective-permute-start.29) | collective-permute-done | bytes 393248 | tf_op jit(solution)/shard_map/ppermute | solution.py:488
  120.3 4.6 %collective-permute-done.27 = f32[256,128]{1,0:T(8,128)S(1)} collective-permute-done((f32[256,128]{1,0:T(8,128)S(1)}, f32[256,128]{1,0:T(8,128)S(1)}, u32[]{:S(2)}, u32[]{:S(2)}) %collective-permute-start.27) | collective-permute-done | bytes 131104 | tf_op jit(solution)/shard_map/ppermute | solution.py:488
  126.2 11.3 %collective-permute-done.30 = f32[768,128]{1,0:T(8,128)S(1)} collective-permute-done((f32[768,128]{1,0:T(8,128)S(1)}, f32[768,128]{1,0:T(8,128)S(1)}, u32[]{:S(2)}, u32[]{:S(2)}) %collective-permute-start.30) | collective-permute-done | bytes 393248 | tf_op jit(solution)/shard_map/ppermute | solution.py:488
  138.1 3.8 %collective-permute-start.32 = (f32[8,128]{1,0:T(8,128)S(1)}, f32[8,128]{1,0:T(8,128)S(1)}, u32[]{:S(2)}, u32[]{:S(2)}) collective-permute-start(f32[8,128]{1,0:T(8,128)S(1)} %get-tuple-element.96), channel_id=1, source_target_pairs={{0,1},{1,0},{2,3},{3,2},{4,5},{5,4},{6,7},{7,6},{8,9},{9,8},{10,11... | collective-permute-start | bytes 12296 | tf_op jit(solution)/shard_map/ppermute | solution.py:488
  143.5 8.7 %all-gather = f32[64,128]{1,0:T(8,128)S(1)} all-gather(f32[8,128]{1,0:T(8,128)S(1)} %add.39), channel_id=2, replica_groups=mesh['rows'=8,'cols'=4] {'rows'}, dimensions={0}, use_global_device_ids=true | all-gather | bytes 36864 | tf_op jit(solution)/shard_map/all_gather | solution.py:565
  (94 shorter events, 38.4 us)
Async XLA Ops:
  13.4 7.0 %collective-permute-start.4 = (f32[512,256]{1,0:T(8,128)S(1)}, f32[512,256]{1,0:T(8,128)S(1)}, u32[]{:S(2)}, u32[]{:S(2)}) collective-permute-start(f32[512,256]{1,0:T(8,128)S(1)} %copy-done.3), channel_id=1, source_target_pairs={{0,4},{4,0},{8,12},{12,8},{16,20},{20,16},{24,28},{28,24},{1,5},{5... | collective-permute-start | bytes 1572872 | tf_op jit(solution)/shard_map/ppermute | solution.py:488
  15.8 16.5 %collective-permute-start.1 = (f32[520,128]{1,0:T(8,128)S(1)}, f32[520,128]{1,0:T(8,128)S(1)}, u32[]{:S(2)}, u32[]{:S(2)}) collective-permute-start(f32[520,128]{1,0:T(8,128)S(1)} %get-tuple-element.56), channel_id=1, source_target_pairs={{0,8},{4,12},{8,0},{12,4},{16,24},{20,28},{24,16},{28,20},{1,9},{5... | collective-permute-start | bytes 798728 | tf_op jit(solution)/shard_map/ppermute | solution.py:488
  18.8 13.9 %collective-permute-start.2 = (f32[520,128]{1,0:T(8,128)S(1)}, f32[520,128]{1,0:T(8,128)S(1)}, u32[]{:S(2)}, u32[]{:S(2)}) collective-permute-start(f32[520,128]{1,0:T(8,128)S(1)} %get-tuple-element.57), channel_id=1, source_target_pairs={{0,16},{4,20},{8,24},{12,28},{16,0},{20,4},{24,8},{28,12},{1,17},{... | collective-permute-start | bytes 798728 | tf_op jit(solution)/shard_map/ppermute | solution.py:488
  20.3 12.3 %collective-permute-start.3 = (f32[520,128]{1,0:T(8,128)S(1)}, f32[520,128]{1,0:T(8,128)S(1)}, u32[]{:S(2)}, u32[]{:S(2)}) collective-permute-start(f32[520,128]{1,0:T(8,128)S(1)} %get-tuple-element.58), channel_id=1, source_target_pairs={{0,24},{4,28},{8,16},{12,20},{16,8},{20,12},{24,0},{28,4},{1,25},{... | collective-permute-start | bytes 798728 | tf_op jit(solution)/shard_map/ppermute | solution.py:488
  32.7 7.6 %collective-permute-start.7 = (f32[512,128]{1,0:T(8,128)S(1)}, f32[512,128]{1,0:T(8,128)S(1)}, u32[]{:S(2)}, u32[]{:S(2)}) collective-permute-start(f32[512,128]{1,0:T(8,128)S(1)} %get-tuple-element.65.piece_ref), channel_id=1, source_target_pairs={{0,8},{4,12},{8,0},{12,4},{16,24},{20,28},{24,16},{28,20},{1,9},{5... | collective-permute-start | bytes 786440 | tf_op jit(solution)/shard_map/ppermute | solution.py:488
  34.5 7.6 %collective-permute-start.5 = (f32[512,128]{1,0:T(8,128)S(1)}, f32[512,128]{1,0:T(8,128)S(1)}, u32[]{:S(2)}, u32[]{:S(2)}) collective-permute-start(f32[512,128]{1,0:T(8,128)S(1)} %get-tuple-element.65.piece_ref), channel_id=1, source_target_pairs={{0,16},{4,20},{8,24},{12,28},{16,0},{20,4},{24,8},{28,12},{1,17},{... | collective-permute-start | bytes 786440 | tf_op jit(solution)/shard_map/ppermute | solution.py:488
  40.4 5.6 %collective-permute-start.8 = (f32[256,128]{1,0:T(8,128)S(1)}, f32[256,128]{1,0:T(8,128)S(1)}, u32[]{:S(2)}, u32[]{:S(2)}) collective-permute-start(f32[256,128]{1,0:T(8,128)S(1)} %shard_map.91), channel_id=1, source_target_pairs={{0,16},{4,20},{8,24},{12,28},{16,0},{20,4},{24,8},{28,12},{1,17},{... | collective-permute-start | bytes 393224 | tf_op jit(solution)/shard_map/ppermute | solution.py:488
  49.4 5.6 %collective-permute-start.10 = (f32[256,128]{1,0:T(8,128)S(1)}, f32[256,128]{1,0:T(8,128)S(1)}, u32[]{:S(2)}, u32[]{:S(2)}) collective-permute-start(f32[256,128]{1,0:T(8,128)S(1)} %slice.21), channel_id=1, source_target_pairs={{0,1},{1,0},{2,3},{3,2},{4,5},{5,4},{6,7},{7,6},{8,9},{9,8},{10,11... | collective-permute-start | bytes 393224 | tf_op jit(solution)/shard_map/ppermute | solution.py:488
  55.0 6.9 %collective-permute-start.11 = (f32[256,128]{1,0:T(8,128)S(1)}, f32[256,128]{1,0:T(8,128)S(1)}, u32[]{:S(2)}, u32[]{:S(2)}) collective-permute-start(f32[256,128]{1,0:T(8,128)S(1)} %slice_add_fusion), channel_id=1, source_target_pairs={{0,3},{1,2},{2,1},{3,0},{4,7},{5,6},{6,5},{7,4},{8,11},{9,10},{10,... | collective-permute-start | bytes 393224 | tf_op jit(solution)/shard_map/ppermute | solution.py:488
  69.8 14.6 %collective-permute-start.14 = (f32[520,128]{1,0:T(8,128)S(1)}, f32[520,128]{1,0:T(8,128)S(1)}, u32[]{:S(2)}, u32[]{:S(2)}) collective-permute-start(f32[520,128]{1,0:T(8,128)S(1)} %get-tuple-element.72), channel_id=1, source_target_pairs={{0,8},{4,12},{8,0},{12,4},{16,24},{20,28},{24,16},{28,20},{1,9},{5... | collective-permute-start | bytes 798728 | tf_op jit(solution)/shard_map/ppermute | solution.py:488
  71.4 13.9 %collective-permute-start.15 = (f32[520,128]{1,0:T(8,128)S(1)}, f32[520,128]{1,0:T(8,128)S(1)}, u32[]{:S(2)}, u32[]{:S(2)}) collective-permute-start(f32[520,128]{1,0:T(8,128)S(1)} %get-tuple-element.73), channel_id=1, source_target_pairs={{0,16},{4,20},{8,24},{12,28},{16,0},{20,4},{24,8},{28,12},{1,17},{... | collective-permute-start | bytes 798728 | tf_op jit(solution)/shard_map/ppermute | solution.py:488
  71.9 13.5 %collective-permute-start.16 = (f32[520,128]{1,0:T(8,128)S(1)}, f32[520,128]{1,0:T(8,128)S(1)}, u32[]{:S(2)}, u32[]{:S(2)}) collective-permute-start(f32[520,128]{1,0:T(8,128)S(1)} %get-tuple-element.74), channel_id=1, source_target_pairs={{0,24},{4,28},{8,16},{12,20},{16,8},{20,12},{24,0},{28,4},{1,25},{... | collective-permute-start | bytes 798728 | tf_op jit(solution)/shard_map/ppermute | solution.py:488
  85.5 8.7 %collective-permute-start.19 = (f32[512,128]{1,0:T(8,128)S(1)}, f32[512,128]{1,0:T(8,128)S(1)}, u32[]{:S(2)}, u32[]{:S(2)}) collective-permute-start(f32[512,128]{1,0:T(8,128)S(1)} %get-tuple-element.76.refs_0_), channel_id=1, source_target_pairs={{0,8},{4,12},{8,0},{12,4},{16,24},{20,28},{24,16},{28,20},{1,9},{5... | collective-permute-start | bytes 786440 | tf_op jit(solution)/shard_map/ppermute | solution.py:488
  86.2 8.6 %collective-permute-start.17 = (f32[512,128]{1,0:T(8,128)S(1)}, f32[512,128]{1,0:T(8,128)S(1)}, u32[]{:S(2)}, u32[]{:S(2)}) collective-permute-start(f32[512,128]{1,0:T(8,128)S(1)} %get-tuple-element.76.refs_0_), channel_id=1, source_target_pairs={{0,16},{4,20},{8,24},{12,28},{16,0},{20,4},{24,8},{28,12},{1,17},{... | collective-permute-start | bytes 786440 | tf_op jit(solution)/shard_map/ppermute | solution.py:488
  94.8 5.3 %collective-permute-start.18 = (f32[256,128]{1,0:T(8,128)S(1)}, f32[256,128]{1,0:T(8,128)S(1)}, u32[]{:S(2)}, u32[]{:S(2)}) collective-permute-start(f32[256,128]{1,0:T(8,128)S(1)} %shard_map.101), channel_id=1, source_target_pairs={{0,8},{4,12},{8,0},{12,4},{16,24},{20,28},{24,16},{28,20},{1,9},{5... | collective-permute-start | bytes 393224 | tf_op jit(solution)/shard_map/ppermute | solution.py:488
  96.1 5.6 %collective-permute-start.22 = (f32[512,128]{1,0:T(8,128)S(1)}, f32[512,128]{1,0:T(8,128)S(1)}, u32[]{:S(2)}, u32[]{:S(2)}) collective-permute-start(f32[512,128]{1,0:T(8,128)S(1)} %collective-permute-done.19.x_ref.refs_0_), channel_id=1, source_target_pairs={{0,4},{4,0},{8,12},{12,8},{16,20},{20,16},{24,28},{28,24},{1,5},{5... | collective-permute-start | bytes 786440 | tf_op jit(solution)/shard_map/ppermute | solution.py:488
  96.1 5.6 %collective-permute-start.23 = (f32[512,128]{1,0:T(8,128)S(1)}, f32[512,128]{1,0:T(8,128)S(1)}, u32[]{:S(2)}, u32[]{:S(2)}) collective-permute-start(f32[512,128]{1,0:T(8,128)S(1)} %collective-permute-done.17.x_ref.refs_1_), channel_id=1, source_target_pairs={{0,4},{4,0},{8,12},{12,8},{16,20},{20,16},{24,28},{28,24},{1,5},{5... | collective-permute-start | bytes 786440 | tf_op jit(solution)/shard_map/ppermute | solution.py:488
  103.0 6.1 %collective-permute-start.26 = (f32[256,128]{1,0:T(8,128)S(1)}, f32[256,128]{1,0:T(8,128)S(1)}, u32[]{:S(2)}, u32[]{:S(2)}) collective-permute-start(f32[256,128]{1,0:T(8,128)S(1)} %get-tuple-element.87), channel_id=1, source_target_pairs={{0,1},{1,0},{2,3},{3,2},{4,5},{5,4},{6,7},{7,6},{8,9},{9,8},{10,11... | collective-permute-start | bytes 393224 | tf_op jit(solution)/shard_map/ppermute | solution.py:488
  109.1 11.2 %collective-permute-start.29 = (f32[768,128]{1,0:T(8,128)S(1)}, f32[768,128]{1,0:T(8,128)S(1)}, u32[]{:S(2)}, u32[]{:S(2)}) collective-permute-start(f32[768,128]{1,0:T(8,128)S(1)} %get-tuple-element.91), channel_id=1, source_target_pairs={{0,1},{1,0},{2,3},{3,2},{4,5},{5,4},{6,7},{7,6},{8,9},{9,8},{10,11... | collective-permute-start | bytes 1179656 | tf_op jit(solution)/shard_map/ppermute | solution.py:488
  110.8 14.1 %collective-permute-start.27 = (f32[256,128]{1,0:T(8,128)S(1)}, f32[256,128]{1,0:T(8,128)S(1)}, u32[]{:S(2)}, u32[]{:S(2)}) collective-permute-start(f32[256,128]{1,0:T(8,128)S(1)} %add.35), channel_id=1, source_target_pairs={{0,3},{1,2},{2,1},{3,0},{4,7},{5,6},{6,5},{7,4},{8,11},{9,10},{10,... | collective-permute-start | bytes 393224 | tf_op jit(solution)/shard_map/ppermute | solution.py:488
  125.0 12.6 %collective-permute-start.30 = (f32[768,128]{1,0:T(8,128)S(1)}, f32[768,128]{1,0:T(8,128)S(1)}, u32[]{:S(2)}, u32[]{:S(2)}) collective-permute-start(f32[768,128]{1,0:T(8,128)S(1)} %add.37), channel_id=1, source_target_pairs={{0,3},{1,2},{2,1},{3,0},{4,7},{5,6},{6,5},{7,4},{8,11},{9,10},{10,... | collective-permute-start | bytes 1179656 | tf_op jit(solution)/shard_map/ppermute | solution.py:488
  126.2 11.8 %collective-permute-start.28 = (f32[256,128]{1,0:T(8,128)S(1)}, f32[256,128]{1,0:T(8,128)S(1)}, u32[]{:S(2)}, u32[]{:S(2)}) collective-permute-start(f32[256,128]{1,0:T(8,128)S(1)} %get-tuple-element.88.refs_0_), channel_id=1, source_target_pairs={{0,1},{1,0},{2,3},{3,2},{4,5},{5,4},{6,7},{7,6},{8,9},{9,8},{10,11... | collective-permute-start | bytes 393224 | tf_op jit(solution)/shard_map/ppermute | solution.py:488
  138.1 5.4 %collective-permute-start.32 = (f32[8,128]{1,0:T(8,128)S(1)}, f32[8,128]{1,0:T(8,128)S(1)}, u32[]{:S(2)}, u32[]{:S(2)}) collective-permute-start(f32[8,128]{1,0:T(8,128)S(1)} %get-tuple-element.96), channel_id=1, source_target_pairs={{0,1},{1,0},{2,3},{3,2},{4,5},{5,4},{6,7},{7,6},{8,9},{9,8},{10,11... | collective-permute-start | bytes 12296 | tf_op jit(solution)/shard_map/ppermute | solution.py:488
  141.8 10.3 %collective-permute-start.31 = (f32[768,128]{1,0:T(8,128)S(1)}, f32[768,128]{1,0:T(8,128)S(1)}, u32[]{:S(2)}, u32[]{:S(2)}) collective-permute-start(f32[768,128]{1,0:T(8,128)S(1)} %get-tuple-element.95.refs_2_), channel_id=1, source_target_pairs={{0,1},{1,0},{2,3},{3,2},{4,5},{5,4},{6,7},{7,6},{8,9},{9,8},{10,11... | collective-permute-start | bytes 1179656 | tf_op jit(solution)/shard_map/ppermute | solution.py:488
  (14 other events, 130.1 us)

commit v8 on v7

--- a/solution.py
+++ b/solution.py
@@ -330,7 +330,7 @@
     value = None if first else refs[0][...]
     for (shift, begin, side), ref in zip(places, pieces):
         n = ref.shape[0]
-        step = min(n, 256)
+        step = min(n, 512)
         for i in range(0, n, step):
             start = pl.multiple_of(((chip ^ shift) * 2 + (core ^ side)) * m + begin + i, step)
             high, low = split(l_ref[pl.ds(start, step), :])

time: 154 us -> 154 us (level)
  transfers between devices with their start and end apart: 33 -> 33, of which waited for: 18 -> 20; matrix products, arithmetic and copies ran while one was open for 1% -> 1% of each run, Pallas kernels for 17% -> 17%
where the time goes in v8:
time: 154 us
  waiting for transfers between devices  49.8 us (32%)
  Pallas kernels  42.4 us (28%)
  starting transfers between devices  39.5 us (26%)
  local copies, waits for them, and re-layouts  10.6 us (7%)
  blocking collectives  8.95 us (6%)
    ppermute x33, waiting for transfers between devices, swap(): return lax.ppermute(x, axis, [(i, i ^ mask) for i in range(size)])  49.8 us
    ppermute x33, starting transfers between devices, swap(): return lax.ppermute(x, axis, [(i, i ^ mask) for i in range(size)])  39.5 us
    pallas_call x2, Pallas kernels, forward(): pl.pallas_call(functools.partial(forward_kernel, chips, begin, end, slots...  16.7 us
    unnamed x10, local copies, waits for them, and re-layouts  10.6 us
    all_gather x1, blocking collectives, body(): norm_next = jnp.sum(lax.all_gather(norm_next, 'rows'), axis=0)  8.95 us
    pallas_call x1, Pallas kernels, gaussian(): pl.pallas_call(functools.partial(kernel_kernel, segments), grid_spec=pltp...  7.48 us
    pallas_call x4, Pallas kernels, transposed(): pl.pallas_call(functools.partial(transposed_kernel, m, places, acc is Non...  6.32 us
    pallas_call x2, Pallas kernels, last_transposed(): pl.pallas_call(functools.partial(last_kernel, m, [piece[:2] for piece in...  4 us
  transfers between devices with their start and end apart: 33, of which 20 were waited for; matrix products, arithmetic and copies ran while one was open for 1% of the time, Pallas kernels for 17%

profile of v8, /device:TPU:0, one launch (start us, length us, event | category | flops | bytes accessed | tf_op | source)
XLA Modules:
  0.0 153.7 jit_solution(10728192228797884725)
XLA Ops:
  0.6 12.2 %shard_map.85 = (f32[3,520,128]{2,1,0:T(8,128)S(1)}, f32[4,520,128]{2,1,0:T(8,128)S(1)}) custom-call(f32[4096,2048]{1,0:T(8,128)} %l_ref.15, f32[2048,128]{1,0:T(8,128)} %refs_4_.2, f32[2048,128]{1,0:T(8,128)} %r_ref.7), custom_call_target="tpu_custom_call" | custom-call | flops 1 | bytes 1 | tf_op jit(solution)/shard_map/pallas_call | solution.py:146
  13.5 2.2 %collective-permute-done.refs_1_ = f32[4,520,128]{2,1,0:T(8,128)S(1)} collective-permute-done((f32[4,520,128]{2,1,0:T(8,128)S(1)}, f32[4,520,128]{2,1,0:T(8,128)S(1)}, u32[]{:S(2)}, u32[]{:S(2)}) %collective-permute-start) | collective-permute-done | bytes 1064992 | tf_op jit(solution)/shard_map/ppermute | solution.py:488
  15.8 2.9 %collective-permute-start.1 = (f32[520,128]{1,0:T(8,128)S(1)}, f32[520,128]{1,0:T(8,128)S(1)}, u32[]{:S(2)}, u32[]{:S(2)}) collective-permute-start(f32[520,128]{1,0:T(8,128)S(1)} %get-tuple-element.56), channel_id=1, source_target_pairs={{0,8},{4,12},{8,0},{12,4},{16,24},{20,28},{24,16},{28,20},{1,9},{5... | collective-permute-start | bytes 798728 | tf_op jit(solution)/shard_map/ppermute | solution.py:488
  20.4 7.5 %shard_map.89 = (bf16[4,512,1024]{2,1,0:T(8,128)(2,1)S(1)}, bf16[4,512,1024]{2,1,0:T(8,128)(2,1)S(1)}) custom-call(s32[3]{0:T(128)S(1)} %pad_add_fusion.place, f32[512,256]{1,0:T(8,128)S(1)} %copy-done.3, f32[512,256]{1,0:T(8,128)S(1)} %collective-permute-done.4.other_ref, f32[4096,256]{1,0:T(8,128)} %c_ref.1), custom_call_target="tpu_custom_call" | custom-call | flops 1 | bytes 1 | tf_op jit(solution)/shard_map/pallas_call | solution.py:235
  27.9 4.5 %shard_map.87 = f32[1,520,128]{2,1,0:T(8,128)S(1)} custom-call(f32[4096,2048]{1,0:T(8,128)} %l_ref.15, f32[2048,128]{1,0:T(8,128)} %refs_4_.2, f32[2048,128]{1,0:T(8,128)} %r_ref.7), custom_call_target="tpu_custom_call" | custom-call | flops 1 | bytes 1 | tf_op jit(solution)/shard_map/pallas_call | solution.py:146
  36.0 4.3 %collective-permute-done.7.x_ref.piece_ref = f32[512,128]{1,0:T(8,128)S(1)} collective-permute-done((f32[512,128]{1,0:T(8,128)S(1)}, f32[512,128]{1,0:T(8,128)S(1)}, u32[]{:S(2)}, u32[]{:S(2)}) %collective-permute-start.7) | collective-permute-done | bytes 262176 | tf_op jit(solution)/shard_map/ppermute | solution.py:488
  40.4 1.8 %collective-permute-start.8 = (f32[256,128]{1,0:T(8,128)S(1)}, f32[256,128]{1,0:T(8,128)S(1)}, u32[]{:S(2)}, u32[]{:S(2)}) collective-permute-start(f32[256,128]{1,0:T(8,128)S(1)} %shard_map.91), channel_id=1, source_target_pairs={{0,16},{4,20},{8,24},{12,28},{16,0},{20,4},{24,8},{28,12},{1,17},{... | collective-permute-start | bytes 393224 | tf_op jit(solution)/shard_map/ppermute | solution.py:488
  51.0 3.9 %collective-permute-done.10 = f32[256,128]{1,0:T(8,128)S(1)} collective-permute-done((f32[256,128]{1,0:T(8,128)S(1)}, f32[256,128]{1,0:T(8,128)S(1)}, u32[]{:S(2)}, u32[]{:S(2)}) %collective-permute-start.10) | collective-permute-done | bytes 131104 | tf_op jit(solution)/shard_map/ppermute | solution.py:488
  55.0 3.7 %collective-permute-start.11 = (f32[256,128]{1,0:T(8,128)S(1)}, f32[256,128]{1,0:T(8,128)S(1)}, u32[]{:S(2)}, u32[]{:S(2)}) collective-permute-start(f32[256,128]{1,0:T(8,128)S(1)} %slice_add_fusion), channel_id=1, source_target_pairs={{0,3},{1,2},{2,1},{3,0},{4,7},{5,6},{6,5},{7,4},{8,11},{9,10},{10,... | collective-permute-start | bytes 393224 | tf_op jit(solution)/shard_map/ppermute | solution.py:488
  58.7 3.2 %collective-permute-done.11 = f32[256,128]{1,0:T(8,128)S(1)} collective-permute-done((f32[256,128]{1,0:T(8,128)S(1)}, f32[256,128]{1,0:T(8,128)S(1)}, u32[]{:S(2)}, u32[]{:S(2)}) %collective-permute-start.11) | collective-permute-done | bytes 131104 | tf_op jit(solution)/shard_map/ppermute | solution.py:488
  61.9 2.4 %collective-permute-start.12 = (f32[256,128]{1,0:T(8,128)S(1)}, f32[256,128]{1,0:T(8,128)S(1)}, u32[]{:S(2)}, u32[]{:S(2)}) collective-permute-start(f32[256,128]{1,0:T(8,128)S(1)} %add.32), channel_id=1, source_target_pairs={{0,1},{1,0},{2,3},{3,2},{4,5},{5,4},{6,7},{7,6},{8,9},{9,8},{10,11... | collective-permute-start | bytes 393224 | tf_op jit(solution)/shard_map/ppermute | solution.py:488
  64.3 2.9 %collective-permute-done.12 = f32[256,128]{1,0:T(8,128)S(1)} collective-permute-done((f32[256,128]{1,0:T(8,128)S(1)}, f32[256,128]{1,0:T(8,128)S(1)}, u32[]{:S(2)}, u32[]{:S(2)}) %collective-permute-start.12) | collective-permute-done | bytes 131104 | tf_op jit(solution)/shard_map/ppermute | solution.py:488
  73.4 10.5 %copy-done = f32[4096,2048]{1,0:T(8,128)S(1)} copy-done((f32[4096,2048]{1,0:T(8,128)S(1)}, f32[4096,2048]{1,0:T(8,128)}, u32[]{:S(2)}) %copy-start) | copy-done | bytes 33554456
  87.3 2.4 %shard_map.102.refs_2_ = f32[128,2048]{1,0:T(8,128)S(1)} custom-call(f32[4096,2048]{1,0:T(8,128)S(1)} %copy-done, f32[512,128]{1,0:T(8,128)S(1)} %get-tuple-element.76.refs_0_, f32[512,128]{1,0:T(8,128)S(1)} %collective-permute-done.20.refs_1_), custom_call_target="tpu_custom_call" | custom-call | flops 1 | bytes 1 | tf_op jit(solution)/shard_map/pallas_call | solution.py:346
  89.7 4.5 %collective-permute-done.19.x_ref.refs_0_ = f32[512,128]{1,0:T(8,128)S(1)} collective-permute-done((f32[512,128]{1,0:T(8,128)S(1)}, f32[512,128]{1,0:T(8,128)S(1)}, u32[]{:S(2)}, u32[]{:S(2)}) %collective-permute-start.19) | collective-permute-done | bytes 262176 | tf_op jit(solution)/shard_map/ppermute | solution.py:488
  96.7 2.4 %shard_map.104.refs_1_ = f32[128,2048]{1,0:T(8,128)S(1)} custom-call(f32[4096,2048]{1,0:T(8,128)S(1)} %copy-done, f32[512,128]{1,0:T(8,128)S(1)} %collective-permute-done.19.x_ref.refs_0_, f32[512,128]{1,0:T(8,128)S(1)} %collective-permute-done.17.x_ref.refs_1_, f32[128,2048]{1,0:T(8,128)S(1)} %shard_map.102.refs_2_), custom_call_target="tpu_custom_call" | custom-call | flops 1 | bytes 1 | tf_op jit(solution)/shard_map/pallas_call | solution.py:346
  103.1 2.1 %collective-permute-start.26 = (f32[256,128]{1,0:T(8,128)S(1)}, f32[256,128]{1,0:T(8,128)S(1)}, u32[]{:S(2)}, u32[]{:S(2)}) collective-permute-start(f32[256,128]{1,0:T(8,128)S(1)} %get-tuple-element.87), channel_id=1, source_target_pairs={{0,1},{1,0},{2,3},{3,2},{4,5},{5,4},{6,7},{7,6},{8,9},{9,8},{10,11... | collective-permute-start | bytes 393224 | tf_op jit(solution)/shard_map/ppermute | solution.py:488
  105.2 2.8 %shard_map.109 = (f32[768,128]{1,0:T(8,128)S(1)}, f32[768,128]{1,0:T(8,128)S(1)}) custom-call(f32[4096,2048]{1,0:T(8,128)S(1)} %copy-done, f32[128,2048]{1,0:T(8,128)S(1)} %shard_map.106.acc_ref, f32[512,128]{1,0:T(8,128)S(1)} %collective-permute-done.22.refs_0_, f32[512,128]{1,0:T(8,128)S(1)} %collective-permute-done.23.refs_1_, ...), custom_call_target="tpu_custom_call" | custom-call | flops 1 | bytes 1 | tf_op jit(solution)/shard_map/pallas_call | solution.py:389
  110.8 2.8 %collective-permute-start.27 = (f32[256,128]{1,0:T(8,128)S(1)}, f32[256,128]{1,0:T(8,128)S(1)}, u32[]{:S(2)}, u32[]{:S(2)}) collective-permute-start(f32[256,128]{1,0:T(8,128)S(1)} %add.35), channel_id=1, source_target_pairs={{0,3},{1,2},{2,1},{3,0},{4,7},{5,6},{6,5},{7,4},{8,11},{9,10},{10,... | collective-permute-start | bytes 393224 | tf_op jit(solution)/shard_map/ppermute | solution.py:488
  113.6 6.5 %collective-permute-done.29 = f32[768,128]{1,0:T(8,128)S(1)} collective-permute-done((f32[768,128]{1,0:T(8,128)S(1)}, f32[768,128]{1,0:T(8,128)S(1)}, u32[]{:S(2)}, u32[]{:S(2)}) %collective-permute-start.29) | collective-permute-done | bytes 393248 | tf_op jit(solution)/shard_map/ppermute | solution.py:488
  120.2 4.6 %collective-permute-done.27 = f32[256,128]{1,0:T(8,128)S(1)} collective-permute-done((f32[256,128]{1,0:T(8,128)S(1)}, f32[256,128]{1,0:T(8,128)S(1)}, u32[]{:S(2)}, u32[]{:S(2)}) %collective-permute-start.27) | collective-permute-done | bytes 131104 | tf_op jit(solution)/shard_map/ppermute | solution.py:488
  126.1 11.1 %collective-permute-done.30 = f32[768,128]{1,0:T(8,128)S(1)} collective-permute-done((f32[768,128]{1,0:T(8,128)S(1)}, f32[768,128]{1,0:T(8,128)S(1)}, u32[]{:S(2)}, u32[]{:S(2)}) %collective-permute-start.30) | collective-permute-done | bytes 393248 | tf_op jit(solution)/shard_map/ppermute | solution.py:488
  137.8 3.7 %collective-permute-start.32 = (f32[8,128]{1,0:T(8,128)S(1)}, f32[8,128]{1,0:T(8,128)S(1)}, u32[]{:S(2)}, u32[]{:S(2)}) collective-permute-start(f32[8,128]{1,0:T(8,128)S(1)} %get-tuple-element.96), channel_id=1, source_target_pairs={{0,1},{1,0},{2,3},{3,2},{4,5},{5,4},{6,7},{7,6},{8,9},{9,8},{10,11... | collective-permute-start | bytes 12296 | tf_op jit(solution)/shard_map/ppermute | solution.py:488
  143.2 9.0 %all-gather = f32[64,128]{1,0:T(8,128)S(1)} all-gather(f32[8,128]{1,0:T(8,128)S(1)} %add.39), channel_id=2, replica_groups=mesh['rows'=8,'cols'=4] {'rows'}, dimensions={0}, use_global_device_ids=true | all-gather | bytes 36864 | tf_op jit(solution)/shard_map/all_gather | solution.py:565
  (94 shorter events, 38.5 us)
Async XLA Ops:
  13.4 7.0 %collective-permute-start.4 = (f32[512,256]{1,0:T(8,128)S(1)}, f32[512,256]{1,0:T(8,128)S(1)}, u32[]{:S(2)}, u32[]{:S(2)}) collective-permute-start(f32[512,256]{1,0:T(8,128)S(1)} %copy-done.3), channel_id=1, source_target_pairs={{0,4},{4,0},{8,12},{12,8},{16,20},{20,16},{24,28},{28,24},{1,5},{5... | collective-permute-start | bytes 1572872 | tf_op jit(solution)/shard_map/ppermute | solution.py:488
  15.8 16.5 %collective-permute-start.1 = (f32[520,128]{1,0:T(8,128)S(1)}, f32[520,128]{1,0:T(8,128)S(1)}, u32[]{:S(2)}, u32[]{:S(2)}) collective-permute-start(f32[520,128]{1,0:T(8,128)S(1)} %get-tuple-element.56), channel_id=1, source_target_pairs={{0,8},{4,12},{8,0},{12,4},{16,24},{20,28},{24,16},{28,20},{1,9},{5... | collective-permute-start | bytes 798728 | tf_op jit(solution)/shard_map/ppermute | solution.py:488
  18.8 13.9 %collective-permute-start.2 = (f32[520,128]{1,0:T(8,128)S(1)}, f32[520,128]{1,0:T(8,128)S(1)}, u32[]{:S(2)}, u32[]{:S(2)}) collective-permute-start(f32[520,128]{1,0:T(8,128)S(1)} %get-tuple-element.57), channel_id=1, source_target_pairs={{0,16},{4,20},{8,24},{12,28},{16,0},{20,4},{24,8},{28,12},{1,17},{... | collective-permute-start | bytes 798728 | tf_op jit(solution)/shard_map/ppermute | solution.py:488
  20.3 12.3 %collective-permute-start.3 = (f32[520,128]{1,0:T(8,128)S(1)}, f32[520,128]{1,0:T(8,128)S(1)}, u32[]{:S(2)}, u32[]{:S(2)}) collective-permute-start(f32[520,128]{1,0:T(8,128)S(1)} %get-tuple-element.58), channel_id=1, source_target_pairs={{0,24},{4,28},{8,16},{12,20},{16,8},{20,12},{24,0},{28,4},{1,25},{... | collective-permute-start | bytes 798728 | tf_op jit(solution)/shard_map/ppermute | solution.py:488
  32.7 7.6 %collective-permute-start.7 = (f32[512,128]{1,0:T(8,128)S(1)}, f32[512,128]{1,0:T(8,128)S(1)}, u32[]{:S(2)}, u32[]{:S(2)}) collective-permute-start(f32[512,128]{1,0:T(8,128)S(1)} %get-tuple-element.65.piece_ref), channel_id=1, source_target_pairs={{0,8},{4,12},{8,0},{12,4},{16,24},{20,28},{24,16},{28,20},{1,9},{5... | collective-permute-start | bytes 786440 | tf_op jit(solution)/shard_map/ppermute | solution.py:488
  34.5 7.6 %collective-permute-start.5 = (f32[512,128]{1,0:T(8,128)S(1)}, f32[512,128]{1,0:T(8,128)S(1)}, u32[]{:S(2)}, u32[]{:S(2)}) collective-permute-start(f32[512,128]{1,0:T(8,128)S(1)} %get-tuple-element.65.piece_ref), channel_id=1, source_target_pairs={{0,16},{4,20},{8,24},{12,28},{16,0},{20,4},{24,8},{28,12},{1,17},{... | collective-permute-start | bytes 786440 | tf_op jit(solution)/shard_map/ppermute | solution.py:488
  40.4 5.6 %collective-permute-start.8 = (f32[256,128]{1,0:T(8,128)S(1)}, f32[256,128]{1,0:T(8,128)S(1)}, u32[]{:S(2)}, u32[]{:S(2)}) collective-permute-start(f32[256,128]{1,0:T(8,128)S(1)} %shard_map.91), channel_id=1, source_target_pairs={{0,16},{4,20},{8,24},{12,28},{16,0},{20,4},{24,8},{28,12},{1,17},{... | collective-permute-start | bytes 393224 | tf_op jit(solution)/shard_map/ppermute | solution.py:488
  49.4 5.6 %collective-permute-start.10 = (f32[256,128]{1,0:T(8,128)S(1)}, f32[256,128]{1,0:T(8,128)S(1)}, u32[]{:S(2)}, u32[]{:S(2)}) collective-permute-start(f32[256,128]{1,0:T(8,128)S(1)} %slice.21), channel_id=1, source_target_pairs={{0,1},{1,0},{2,3},{3,2},{4,5},{5,4},{6,7},{7,6},{8,9},{9,8},{10,11... | collective-permute-start | bytes 393224 | tf_op jit(solution)/shard_map/ppermute | solution.py:488
  55.0 6.9 %collective-permute-start.11 = (f32[256,128]{1,0:T(8,128)S(1)}, f32[256,128]{1,0:T(8,128)S(1)}, u32[]{:S(2)}, u32[]{:S(2)}) collective-permute-start(f32[256,128]{1,0:T(8,128)S(1)} %slice_add_fusion), channel_id=1, source_target_pairs={{0,3},{1,2},{2,1},{3,0},{4,7},{5,6},{6,5},{7,4},{8,11},{9,10},{10,... | collective-permute-start | bytes 393224 | tf_op jit(solution)/shard_map/ppermute | solution.py:488
  69.8 14.6 %collective-permute-start.14 = (f32[520,128]{1,0:T(8,128)S(1)}, f32[520,128]{1,0:T(8,128)S(1)}, u32[]{:S(2)}, u32[]{:S(2)}) collective-permute-start(f32[520,128]{1,0:T(8,128)S(1)} %get-tuple-element.72), channel_id=1, source_target_pairs={{0,8},{4,12},{8,0},{12,4},{16,24},{20,28},{24,16},{28,20},{1,9},{5... | collective-permute-start | bytes 798728 | tf_op jit(solution)/shard_map/ppermute | solution.py:488
  71.4 13.9 %collective-permute-start.15 = (f32[520,128]{1,0:T(8,128)S(1)}, f32[520,128]{1,0:T(8,128)S(1)}, u32[]{:S(2)}, u32[]{:S(2)}) collective-permute-start(f32[520,128]{1,0:T(8,128)S(1)} %get-tuple-element.73), channel_id=1, source_target_pairs={{0,16},{4,20},{8,24},{12,28},{16,0},{20,4},{24,8},{28,12},{1,17},{... | collective-permute-start | bytes 798728 | tf_op jit(solution)/shard_map/ppermute | solution.py:488
  71.9 13.5 %collective-permute-start.16 = (f32[520,128]{1,0:T(8,128)S(1)}, f32[520,128]{1,0:T(8,128)S(1)}, u32[]{:S(2)}, u32[]{:S(2)}) collective-permute-start(f32[520,128]{1,0:T(8,128)S(1)} %get-tuple-element.74), channel_id=1, source_target_pairs={{0,24},{4,28},{8,16},{12,20},{16,8},{20,12},{24,0},{28,4},{1,25},{... | collective-permute-start | bytes 798728 | tf_op jit(solution)/shard_map/ppermute | solution.py:488
  85.5 8.7 %collective-permute-start.19 = (f32[512,128]{1,0:T(8,128)S(1)}, f32[512,128]{1,0:T(8,128)S(1)}, u32[]{:S(2)}, u32[]{:S(2)}) collective-permute-start(f32[512,128]{1,0:T(8,128)S(1)} %get-tuple-element.76.refs_0_), channel_id=1, source_target_pairs={{0,8},{4,12},{8,0},{12,4},{16,24},{20,28},{24,16},{28,20},{1,9},{5... | collective-permute-start | bytes 786440 | tf_op jit(solution)/shard_map/ppermute | solution.py:488
  86.2 8.6 %collective-permute-start.17 = (f32[512,128]{1,0:T(8,128)S(1)}, f32[512,128]{1,0:T(8,128)S(1)}, u32[]{:S(2)}, u32[]{:S(2)}) collective-permute-start(f32[512,128]{1,0:T(8,128)S(1)} %get-tuple-element.76.refs_0_), channel_id=1, source_target_pairs={{0,16},{4,20},{8,24},{12,28},{16,0},{20,4},{24,8},{28,12},{1,17},{... | collective-permute-start | bytes 786440 | tf_op jit(solution)/shard_map/ppermute | solution.py:488
  94.8 5.3 %collective-permute-start.18 = (f32[256,128]{1,0:T(8,128)S(1)}, f32[256,128]{1,0:T(8,128)S(1)}, u32[]{:S(2)}, u32[]{:S(2)}) collective-permute-start(f32[256,128]{1,0:T(8,128)S(1)} %shard_map.101), channel_id=1, source_target_pairs={{0,8},{4,12},{8,0},{12,4},{16,24},{20,28},{24,16},{28,20},{1,9},{5... | collective-permute-start | bytes 393224 | tf_op jit(solution)/shard_map/ppermute | solution.py:488
  96.1 5.7 %collective-permute-start.22 = (f32[512,128]{1,0:T(8,128)S(1)}, f32[512,128]{1,0:T(8,128)S(1)}, u32[]{:S(2)}, u32[]{:S(2)}) collective-permute-start(f32[512,128]{1,0:T(8,128)S(1)} %collective-permute-done.19.x_ref.refs_0_), channel_id=1, source_target_pairs={{0,4},{4,0},{8,12},{12,8},{16,20},{20,16},{24,28},{28,24},{1,5},{5... | collective-permute-start | bytes 786440 | tf_op jit(solution)/shard_map/ppermute | solution.py:488
  96.1 5.7 %collective-permute-start.23 = (f32[512,128]{1,0:T(8,128)S(1)}, f32[512,128]{1,0:T(8,128)S(1)}, u32[]{:S(2)}, u32[]{:S(2)}) collective-permute-start(f32[512,128]{1,0:T(8,128)S(1)} %collective-permute-done.17.x_ref.refs_1_), channel_id=1, source_target_pairs={{0,4},{4,0},{8,12},{12,8},{16,20},{20,16},{24,28},{28,24},{1,5},{5... | collective-permute-start | bytes 786440 | tf_op jit(solution)/shard_map/ppermute | solution.py:488
  103.1 6.0 %collective-permute-start.26 = (f32[256,128]{1,0:T(8,128)S(1)}, f32[256,128]{1,0:T(8,128)S(1)}, u32[]{:S(2)}, u32[]{:S(2)}) collective-permute-start(f32[256,128]{1,0:T(8,128)S(1)} %get-tuple-element.87), channel_id=1, source_target_pairs={{0,1},{1,0},{2,3},{3,2},{4,5},{5,4},{6,7},{7,6},{8,9},{9,8},{10,11... | collective-permute-start | bytes 393224 | tf_op jit(solution)/shard_map/ppermute | solution.py:488
  109.1 11.1 %collective-permute-start.29 = (f32[768,128]{1,0:T(8,128)S(1)}, f32[768,128]{1,0:T(8,128)S(1)}, u32[]{:S(2)}, u32[]{:S(2)}) collective-permute-start(f32[768,128]{1,0:T(8,128)S(1)} %get-tuple-element.91), channel_id=1, source_target_pairs={{0,1},{1,0},{2,3},{3,2},{4,5},{5,4},{6,7},{7,6},{8,9},{9,8},{10,11... | collective-permute-start | bytes 1179656 | tf_op jit(solution)/shard_map/ppermute | solution.py:488
  110.8 14.0 %collective-permute-start.27 = (f32[256,128]{1,0:T(8,128)S(1)}, f32[256,128]{1,0:T(8,128)S(1)}, u32[]{:S(2)}, u32[]{:S(2)}) collective-permute-start(f32[256,128]{1,0:T(8,128)S(1)} %add.35), channel_id=1, source_target_pairs={{0,3},{1,2},{2,1},{3,0},{4,7},{5,6},{6,5},{7,4},{8,11},{9,10},{10,... | collective-permute-start | bytes 393224 | tf_op jit(solution)/shard_map/ppermute | solution.py:488
  124.8 12.4 %collective-permute-start.30 = (f32[768,128]{1,0:T(8,128)S(1)}, f32[768,128]{1,0:T(8,128)S(1)}, u32[]{:S(2)}, u32[]{:S(2)}) collective-permute-start(f32[768,128]{1,0:T(8,128)S(1)} %add.37), channel_id=1, source_target_pairs={{0,3},{1,2},{2,1},{3,0},{4,7},{5,6},{6,5},{7,4},{8,11},{9,10},{10,... | collective-permute-start | bytes 1179656 | tf_op jit(solution)/shard_map/ppermute | solution.py:488
  126.0 11.7 %collective-permute-start.28 = (f32[256,128]{1,0:T(8,128)S(1)}, f32[256,128]{1,0:T(8,128)S(1)}, u32[]{:S(2)}, u32[]{:S(2)}) collective-permute-start(f32[256,128]{1,0:T(8,128)S(1)} %get-tuple-element.88.refs_0_), channel_id=1, source_target_pairs={{0,1},{1,0},{2,3},{3,2},{4,5},{5,4},{6,7},{7,6},{8,9},{9,8},{10,11... | collective-permute-start | bytes 393224 | tf_op jit(solution)/shard_map/ppermute | solution.py:488
  137.8 5.3 %collective-permute-start.32 = (f32[8,128]{1,0:T(8,128)S(1)}, f32[8,128]{1,0:T(8,128)S(1)}, u32[]{:S(2)}, u32[]{:S(2)}) collective-permute-start(f32[8,128]{1,0:T(8,128)S(1)} %get-tuple-element.96), channel_id=1, source_target_pairs={{0,1},{1,0},{2,3},{3,2},{4,5},{5,4},{6,7},{7,6},{8,9},{9,8},{10,11... | collective-permute-start | bytes 12296 | tf_op jit(solution)/shard_map/ppermute | solution.py:488
  141.6 10.6 %collective-permute-start.31 = (f32[768,128]{1,0:T(8,128)S(1)}, f32[768,128]{1,0:T(8,128)S(1)}, u32[]{:S(2)}, u32[]{:S(2)}) collective-permute-start(f32[768,128]{1,0:T(8,128)S(1)} %get-tuple-element.95.refs_2_), channel_id=1, source_target_pairs={{0,1},{1,0},{2,3},{3,2},{4,5},{5,4},{6,7},{7,6},{8,9},{9,8},{10,11... | collective-permute-start | bytes 1179656 | tf_op jit(solution)/shard_map/ppermute | solution.py:488
  (14 other events, 129.2 us)
